TPU v7x, 32 devices: a whole 2x2x4 slice. The times are simulated.
32 devices in a mesh: seq: 8 (over z, x), wt: 4 (over y, core).
Axes of the slice: x: 2, y: 2, z: 4, core: 2. Of those that a mesh axis runs over, the one named last changes fastest.
Arguments:
- block_in: bfloat16 [2, 4, 1024, 1536], P(None, 'wt', 'seq'), may hold values from -6 to 6
- start_flags: int32 [2, 4, 1024], P(None, 'wt', 'seq'), may hold values from 0 to 1, as said below
- out_grad: bfloat16 [2, 4, 1024, 1536], P(None, 'wt', 'seq'), may hold values from -6 to 6
- mix_gain: bfloat16 [2, 1536], P(None, ('seq', 'wt')), may hold values from 0.5 to 1.5
- proj_gelu: bfloat16 [2, 1536, 2048], P(None, ('seq', 'wt')), may hold values from -0.15625 to 0.15625
- proj_stream: bfloat16 [2, 1536, 2048], P(None, ('seq', 'wt')), may hold values from -0.15625 to 0.15625
- conv_taps: bfloat16 [2, 4, 2048], P(None, None, ('seq', 'wt')), may hold values from -3 to 3
- lru_gates: bfloat16 [2, 4096, 128], P(None, ('seq', 'wt')), may hold values from -0.5 to 0.5
- decay_param: bfloat16 [2, 2048], P(None, ('seq', 'wt')), may hold values from -11 to -5
- proj_out: bfloat16 [2, 2048, 1536], P(None, ('seq', 'wt')), may hold values from -0.25 to 0.25
- mlp_gain: bfloat16 [2, 1536], P(None, ('seq', 'wt')), may hold values from 0.5 to 1.5
- proj_gate: bfloat16 [2, 1536, 4608], P(None, ('seq', 'wt')), may hold values from -0.15625 to 0.15625
- proj_up: bfloat16 [2, 1536, 4608], P(None, ('seq', 'wt')), may hold values from -0.15625 to 0.15625
- proj_down: bfloat16 [2, 4608, 1536], P(None, ('seq', 'wt')), may hold values from -0.1875 to 0.1875
Outputs:
- block_out: bfloat16 [2, 4, 1024, 1536], P(None, 'wt', 'seq')
- grad_input: bfloat16 [2, 4, 1024, 1536], P(None, 'wt', 'seq')
- grad_mix_gain: float32 [2, 1536], P(None, ('seq', 'wt'))
- grad_proj_gelu: float32 [2, 1536, 2048], P(None, ('seq', 'wt'))
- grad_proj_stream: float32 [2, 1536, 2048], P(None, ('seq', 'wt'))
- grad_conv_taps: float32 [2, 4, 2048], P(None, None, ('seq', 'wt'))
- grad_lru_gates: float32 [2, 4096, 128], P(None, ('seq', 'wt'))
- grad_decay_param: float32 [2, 2048], P(None, ('seq', 'wt'))
- grad_proj_out: float32 [2, 2048, 1536], P(None, ('seq', 'wt'))
- grad_mlp_gain: float32 [2, 1536], P(None, ('seq', 'wt'))
- grad_proj_gate: float32 [2, 1536, 4608], P(None, ('seq', 'wt'))
- grad_proj_up: float32 [2, 1536, 4608], P(None, ('seq', 'wt'))
- grad_proj_down: float32 [2, 4608, 1536], P(None, ('seq', 'wt'))
Inputs may be any that keep to these rules, and one draw needn't show every extreme that they name: `start_flags`: 1 where a sequence begins, 0 elsewhere; position 0 of every stream begins one.
All inputs are finite; a program needn't handle non-finite values.
Results may differ from a plain program's by a relative error of at most 0.033.
Values may be sent and summed in bfloat16 or wider, within the bound.
No kernel may reach another device: no remote copies, remote signals or barrier semaphores. Data moves between devices by JAX's collectives and lax.ppermute only.
A program may use at most 576 MiB of HBM per device.

v0:
```python
import jax
import jax.numpy as jnp
from jax import lax
from jax.sharding import PartitionSpec as P

HEAD_W = 128
CONV = 4


norm_eps = 1e-06
decay_scale = 8.0


def from_behind(block, axis, distance):
    devices = range(lax.axis_size(axis))
    route = [(i - distance, i) for i in devices if i - distance in devices]
    return lax.ppermute(block, axis, route)


def carried_in(value, axis, combine, identity, reverse):
    devices, position = (lax.axis_size(axis), lax.axis_index(axis))
    everything = jax.tree.map(
        lambda part, kind: lax.all_gather(part.astype(kind), axis),
        value,
        (jnp.bfloat16, jnp.bfloat16),
    )
    start = jax.tree.map(
        lambda part, zero: jnp.broadcast_to(jnp.asarray(zero, part.dtype), part.shape),
        value,
        identity,
    )

    def turn(k, before):
        at = devices - 1 - k if reverse else k
        reached = at > position if reverse else at < position
        new = combine(
            before, jax.tree.map(lambda part, own: part[at].astype(own.dtype), everything, value)
        )
        return jax.tree.map(lambda a, b: jnp.where(reached, a, b), new, before)

    return lax.fori_loop(0, devices, turn, start)


def rms_norm(values, gain_vec):
    return (
        values * lax.rsqrt(jnp.mean(values * values, axis=-1, keepdims=True) + norm_eps) * gain_vec
    )


def conv_mix(padded_rows, keep_rows, conv_weight):
    tap_count = conv_weight.shape[0]
    reach = tap_count - 1
    token_count = padded_rows.shape[1] - reach
    summed = conv_weight[0] * padded_rows[:, reach : reach + token_count]
    valid_mask = jnp.ones_like(keep_rows[:, reach : reach + token_count])
    for lag_index in range(1, tap_count):
        begin = reach - lag_index + 1
        valid_mask = valid_mask * keep_rows[:, begin : begin + token_count]
        lagged = padded_rows[:, reach - lag_index : reach - lag_index + token_count]
        summed = summed + conv_weight[lag_index] * lagged * valid_mask[..., None]
    return summed


def coefficients(conv_out, rate_pre, input_pre, decay_values, start_mask):
    keep_mask = (1.0 - start_mask)[..., None]
    log_decay = -decay_scale * jax.nn.softplus(decay_values) * jax.nn.sigmoid(rate_pre)
    decay_eff = jnp.exp(log_decay) * keep_mask
    scale_sq = keep_mask * -jnp.expm1(2.0 * log_decay) + start_mask[..., None]
    return (decay_eff, jnp.sqrt(scale_sq) * jax.nn.sigmoid(input_pre) * conv_out)


def chain_step(earlier, later):
    return (earlier[0] * later[0], later[0] * earlier[1] + later[1])


def chain_back(earlier, later):
    return (earlier[0] * later[0], later[1] + later[0] * earlier[1])


def gelu_mix(gate_vals, up_vals):
    return jax.nn.gelu(gate_vals) * up_vals


def product_dot(left, right, form):
    return jnp.einsum(form, left, right, preferred_element_type=jnp.float32)


def forward_layer(values, start_mask, weights):
    (
        mix_gain,
        proj_gelu,
        proj_stream,
        conv_taps,
        lru_gates,
        decay_param,
        proj_out,
        mlp_gain,
        proj_gate,
        proj_up,
        proj_down,
    ) = weights
    batch_rows, token_count, _ = values.shape
    reach = CONV - 1
    normed = rms_norm(values, mix_gain.astype(jnp.float32)).astype(jnp.bfloat16)
    branch_pre = product_dot(normed, proj_gelu, "mtk,kn->mtn")
    stream_in = product_dot(normed, proj_stream, "mtk,kn->mtn").astype(jnp.bfloat16)
    edge_rows, edge_flags = from_behind(
        (
            stream_in[:, token_count - reach :],
            start_mask[:, token_count - reach :].astype(jnp.bfloat16),
        ),
        "seq",
        1,
    )
    extended = jnp.concatenate([edge_rows, stream_in], axis=1)
    extended_keep = 1.0 - jnp.concatenate([edge_flags.astype(jnp.float32), start_mask], axis=1)
    conv_out = conv_mix(
        extended.astype(jnp.float32), extended_keep, conv_taps.astype(jnp.float32)
    ).astype(jnp.bfloat16)
    lru_width = conv_out.shape[2]
    head_count = lru_width // HEAD_W
    gate_blocks = lru_gates.reshape(2, head_count, HEAD_W, HEAD_W)
    pre_gates = product_dot(
        conv_out.reshape(batch_rows, token_count, head_count, HEAD_W),
        gate_blocks,
        "mtni,gnio->gmtno",
    )
    rate_pre = pre_gates[0].reshape(batch_rows, token_count, lru_width)
    input_pre = pre_gates[1].reshape(batch_rows, token_count, lru_width)
    decay_eff, driven = coefficients(
        conv_out.astype(jnp.float32),
        rate_pre,
        input_pre,
        decay_param.astype(jnp.float32),
        start_mask,
    )
    decay_cum, local_states = lax.associative_scan(chain_step, (decay_eff, driven), axis=1)
    identity = (
        jnp.ones((batch_rows, lru_width), jnp.float32),
        jnp.zeros((batch_rows, lru_width), jnp.float32),
    )
    incoming = carried_in(
        (decay_cum[:, token_count - 1], local_states[:, token_count - 1]),
        "seq",
        chain_step,
        identity,
        False,
    )[1]
    states = local_states + decay_cum * incoming[:, None, :]
    merged = (states * jax.nn.gelu(branch_pre)).astype(jnp.bfloat16)
    hidden_res = values + product_dot(merged, proj_out, "mtr,rd->mtd")
    mlp_in = rms_norm(hidden_res, mlp_gain.astype(jnp.float32)).astype(jnp.bfloat16)
    gate_pre = product_dot(mlp_in, proj_gate, "mtd,df->mtf")
    up_pre = product_dot(mlp_in, proj_up, "mtd,df->mtf")
    product = gelu_mix(gate_pre, up_pre).astype(jnp.bfloat16)
    output = hidden_res + product_dot(product, proj_down, "mtf,fd->mtd")
    kept_state = (
        values,
        normed,
        branch_pre,
        extended,
        extended_keep,
        conv_out,
        rate_pre,
        input_pre,
        decay_eff,
        decay_cum,
        states,
        incoming,
        merged,
        hidden_res,
        mlp_in,
        gate_pre,
        up_pre,
        product,
    )
    return (output, kept_state)


def mlp_backward(grad_out, weights, kept_state):
    (
        mix_gain,
        proj_gelu,
        proj_stream,
        conv_taps,
        lru_gates,
        decay_param,
        proj_out,
        mlp_gain,
        proj_gate,
        proj_up,
        proj_down,
    ) = weights
    hidden_res, mlp_in, gate_pre, up_pre, product = kept_state[13:]
    down_grad = grad_out.astype(jnp.bfloat16)
    grad_down = product_dot(product, down_grad, "mtf,mtd->fd")
    grad_product = product_dot(down_grad, proj_down, "mtd,fd->mtf")
    _, mix_back = jax.vjp(gelu_mix, gate_pre, up_pre)
    grad_gate_f, grad_up_f = mix_back(grad_product)
    grad_gate = grad_gate_f.astype(jnp.bfloat16)
    grad_up = grad_up_f.astype(jnp.bfloat16)
    grad_wgate = product_dot(mlp_in, grad_gate, "mtd,mtf->df")
    grad_wup = product_dot(mlp_in, grad_up, "mtd,mtf->df")
    grad_mlp_in = product_dot(grad_gate, proj_gate, "mtf,df->mtd") + product_dot(
        grad_up, proj_up, "mtf,df->mtd"
    )
    _, second_back = jax.vjp(rms_norm, hidden_res, mlp_gain.astype(jnp.float32))
    grad_res_part, grad_mlp_gain = second_back(grad_mlp_in)
    return (grad_out + grad_res_part, (grad_mlp_gain, grad_wgate, grad_wup, grad_down))


def mixer_backward(grad_hidden, start_mask, weights, kept_state):
    (
        mix_gain,
        proj_gelu,
        proj_stream,
        conv_taps,
        lru_gates,
        decay_param,
        proj_out,
        mlp_gain,
        proj_gate,
        proj_up,
        proj_down,
    ) = weights
    (
        values,
        normed,
        branch_pre,
        extended,
        extended_keep,
        conv_out,
        rate_pre,
        input_pre,
        decay_eff,
        decay_cum,
        states,
        incoming,
        merged,
    ) = kept_state[:13]
    batch_rows, token_count, _ = values.shape
    reach = CONV - 1
    lru_width = conv_out.shape[2]
    head_count = lru_width // HEAD_W
    branch_grad = grad_hidden.astype(jnp.bfloat16)
    grad_wout = product_dot(merged, branch_grad, "mtr,mtd->rd")
    grad_merged = product_dot(branch_grad, proj_out, "mtd,rd->mtr")
    activated, gelu_back = jax.vjp(jax.nn.gelu, branch_pre)
    grad_states = grad_merged * activated
    grad_branch = gelu_back(grad_merged * states)[0].astype(jnp.bfloat16)
    link_decay = jnp.concatenate([decay_eff[:, 1:], jnp.ones_like(decay_eff[:, :1])], axis=1)
    link_cum, flipped = lax.associative_scan(
        chain_step, (link_decay[:, ::-1], grad_states[:, ::-1]), axis=1
    )
    local_back = flipped[:, ::-1]
    suffix = link_cum[:, ::-1]
    identity = (
        jnp.ones((batch_rows, lru_width), jnp.float32),
        jnp.zeros((batch_rows, lru_width), jnp.float32),
    )
    returning = carried_in(
        (decay_cum[:, token_count - 1], decay_eff[:, 0] * local_back[:, 0]),
        "seq",
        chain_back,
        identity,
        True,
    )[1]
    total_back = local_back + suffix * returning[:, None, :]
    previous = jnp.concatenate([incoming[:, None, :], states[:, : token_count - 1]], axis=1)

    def coeff_local(conv_vals, rate_vals, input_vals, decay_vals):
        return coefficients(conv_vals, rate_vals, input_vals, decay_vals, start_mask)

    _, coeff_back = jax.vjp(
        coeff_local,
        conv_out.astype(jnp.float32),
        rate_pre,
        input_pre,
        decay_param.astype(jnp.float32),
    )
    grad_conv_out, grad_rate, grad_input, grad_decay = coeff_back(
        (total_back * previous, total_back)
    )
    pre_grad = jnp.stack([grad_rate.astype(jnp.bfloat16), grad_input.astype(jnp.bfloat16)])
    pre_grad = pre_grad.reshape(2, batch_rows, token_count, head_count, HEAD_W)
    gate_blocks = lru_gates.reshape(2, head_count, HEAD_W, HEAD_W)
    conv_heads = conv_out.reshape(batch_rows, token_count, head_count, HEAD_W)
    grad_gates = product_dot(conv_heads, pre_grad, "mtni,gmtno->gnio").reshape(
        2 * lru_width, HEAD_W
    )
    grad_conv_out = grad_conv_out + product_dot(pre_grad, gate_blocks, "gmtno,gnio->mtni").reshape(
        batch_rows, token_count, lru_width
    )

    def conv_local(padded_rows, conv_weight):
        return conv_mix(padded_rows, extended_keep, conv_weight)

    _, conv_back = jax.vjp(conv_local, extended.astype(jnp.float32), conv_taps.astype(jnp.float32))
    grad_extended, grad_conv = conv_back(grad_conv_out)
    arriving = from_behind(grad_extended[:, :reach].astype(jnp.bfloat16), "seq", -1).astype(
        jnp.float32
    )
    grad_stream = (
        grad_extended[:, reach:] + jnp.pad(arriving, ((0, 0), (token_count - reach, 0), (0, 0)))
    ).astype(jnp.bfloat16)
    grad_wgelu = product_dot(normed, grad_branch, "mtk,mtn->kn")
    grad_wstream = product_dot(normed, grad_stream, "mtk,mtn->kn")
    grad_normed = product_dot(grad_branch, proj_gelu, "mtn,kn->mtk") + product_dot(
        grad_stream, proj_stream, "mtn,kn->mtk"
    )
    _, first_back = jax.vjp(rms_norm, values, mix_gain.astype(jnp.float32))
    grad_values_part, grad_mix_gain = first_back(grad_normed)
    rec_grads = (
        grad_mix_gain,
        grad_wgelu,
        grad_wstream,
        grad_conv,
        grad_gates,
        grad_decay,
        grad_wout,
    )
    return (grad_hidden + grad_values_part, rec_grads)


def fetch_weights(shard_weights, layer_index):
    (
        mix_gain,
        proj_gelu,
        proj_stream,
        conv_taps,
        lru_gates,
        decay_param,
        proj_out,
        mlp_gain,
        proj_gate,
        proj_up,
        proj_down,
    ) = shard_weights
    return (
        lax.all_gather(mix_gain[layer_index], ("seq", "wt"), axis=0, tiled=True),
        lax.all_gather(proj_gelu[layer_index], ("seq", "wt"), axis=0, tiled=True),
        lax.all_gather(proj_stream[layer_index], ("seq", "wt"), axis=0, tiled=True),
        lax.all_gather(conv_taps[layer_index], ("seq", "wt"), axis=1, tiled=True),
        lax.all_gather(lru_gates[layer_index], ("seq", "wt"), axis=0, tiled=True),
        lax.all_gather(decay_param[layer_index], ("seq", "wt"), axis=0, tiled=True),
        lax.all_gather(proj_out[layer_index], ("seq", "wt"), axis=0, tiled=True),
        lax.all_gather(mlp_gain[layer_index], ("seq", "wt"), axis=0, tiled=True),
        lax.all_gather(proj_gate[layer_index], ("seq", "wt"), axis=0, tiled=True),
        lax.all_gather(proj_up[layer_index], ("seq", "wt"), axis=0, tiled=True),
        lax.all_gather(proj_down[layer_index], ("seq", "wt"), axis=0, tiled=True),
    )


def refetch_weights(shard_weights, layer_index):
    (
        mix_gain,
        proj_gelu,
        proj_stream,
        conv_taps,
        lru_gates,
        decay_param,
        proj_out,
        mlp_gain,
        proj_gate,
        proj_up,
        proj_down,
    ) = shard_weights
    return (
        lax.all_gather(mix_gain[layer_index], ("seq", "wt"), axis=0, tiled=True),
        lax.all_gather(proj_gelu[layer_index], ("seq", "wt"), axis=0, tiled=True),
        lax.all_gather(proj_stream[layer_index], ("seq", "wt"), axis=0, tiled=True),
        lax.all_gather(conv_taps[layer_index], ("seq", "wt"), axis=1, tiled=True),
        lax.all_gather(lru_gates[layer_index], ("seq", "wt"), axis=0, tiled=True),
        lax.all_gather(decay_param[layer_index], ("seq", "wt"), axis=0, tiled=True),
        lax.all_gather(proj_out[layer_index], ("seq", "wt"), axis=0, tiled=True),
        lax.all_gather(mlp_gain[layer_index], ("seq", "wt"), axis=0, tiled=True),
        lax.all_gather(proj_gate[layer_index], ("seq", "wt"), axis=0, tiled=True),
        lax.all_gather(proj_up[layer_index], ("seq", "wt"), axis=0, tiled=True),
        lax.all_gather(proj_down[layer_index], ("seq", "wt"), axis=0, tiled=True),
    )


def spread_mlp(mlp_grads):
    grad_mlp_gain, grad_wgate, grad_wup, grad_down = mlp_grads
    return tuple(
        (
            lax.psum_scatter(grad_mlp_gain, ("seq", "wt"), scatter_dimension=0, tiled=True),
            lax.psum_scatter(grad_wgate, ("seq", "wt"), scatter_dimension=0, tiled=True),
            lax.psum_scatter(grad_wup, ("seq", "wt"), scatter_dimension=0, tiled=True),
            lax.psum_scatter(grad_down, ("seq", "wt"), scatter_dimension=0, tiled=True),
        )
    )


def spread_rec(rec_grads):
    grad_mix_gain, grad_wgelu, grad_wstream, grad_conv, grad_gates, grad_decay, grad_wout = (
        rec_grads
    )
    return tuple(
        (
            lax.psum_scatter(grad_mix_gain, ("seq", "wt"), scatter_dimension=0, tiled=True),
            lax.psum_scatter(grad_wgelu, ("seq", "wt"), scatter_dimension=0, tiled=True),
            lax.psum_scatter(grad_wstream, ("seq", "wt"), scatter_dimension=0, tiled=True),
            lax.psum_scatter(grad_conv, ("seq", "wt"), scatter_dimension=1, tiled=True),
            lax.psum_scatter(grad_gates, ("seq", "wt"), scatter_dimension=0, tiled=True),
            lax.psum_scatter(grad_decay, ("seq", "wt"), scatter_dimension=0, tiled=True),
            lax.psum_scatter(grad_wout, ("seq", "wt"), scatter_dimension=0, tiled=True),
        )
    )


def run_batch(values_in, start_ints, grad_in, shard_weights):
    start_mask = start_ints.astype(jnp.float32)
    layer_count = shard_weights[0].shape[0]
    values = values_in.astype(jnp.float32)
    kept_list = []
    weights = None
    for layer_index in range(layer_count):
        weights = fetch_weights(shard_weights, layer_index)
        values, kept_state = forward_layer(values, start_mask, weights)
        kept_list.append(kept_state)
    gradient = grad_in.astype(jnp.float32)
    reduced = [None] * layer_count
    for layer_index in reversed(range(layer_count)):
        if layer_index != layer_count - 1:
            weights = refetch_weights(shard_weights, layer_index)
        kept_state = kept_list[layer_index]
        gradient, mlp_grads = mlp_backward(gradient, weights, kept_state)
        mlp_shards = spread_mlp(mlp_grads)
        gradient, rec_grads = mixer_backward(gradient, start_mask, weights, kept_state)
        rec_shards = spread_rec(rec_grads)
        reduced[layer_index] = rec_shards + mlp_shards
        kept_list[layer_index] = None
    return (values, gradient, reduced)


def per_device(
    block_in,
    start_flags,
    out_grad,
    mix_gain,
    proj_gelu,
    proj_stream,
    conv_taps,
    lru_gates,
    decay_param,
    proj_out,
    mlp_gain,
    proj_gate,
    proj_up,
    proj_down,
):
    shard_weights = (
        mix_gain,
        proj_gelu,
        proj_stream,
        conv_taps,
        lru_gates,
        decay_param,
        proj_out,
        mlp_gain,
        proj_gate,
        proj_up,
        proj_down,
    )
    output, grad_values, totals = run_batch(
        block_in[:, 0], start_flags[:, 0], out_grad[:, 0], shard_weights
    )
    layer_count = len(totals)
    stacked = [
        jnp.stack([totals[layer_index][member] for layer_index in range(layer_count)])
        for member in range(11)
    ]
    return (
        output.astype(jnp.bfloat16)[:, None],
        grad_values.astype(jnp.bfloat16)[:, None],
        stacked[0],
        stacked[1],
        stacked[2],
        stacked[3],
        stacked[4],
        stacked[5],
        stacked[6],
        stacked[7],
        stacked[8],
        stacked[9],
        stacked[10],
    )


def solution(mesh):
    placed = (
        P(None, "wt", "seq", None),
        P(None, "wt", "seq"),
        P(None, "wt", "seq", None),
        P(None, ("seq", "wt")),
        P(None, ("seq", "wt"), None),
        P(None, ("seq", "wt"), None),
        P(None, None, ("seq", "wt")),
        P(None, ("seq", "wt"), None),
        P(None, ("seq", "wt")),
        P(None, ("seq", "wt"), None),
        P(None, ("seq", "wt")),
        P(None, ("seq", "wt"), None),
        P(None, ("seq", "wt"), None),
        P(None, ("seq", "wt"), None),
    )
    return jax.shard_map(
        per_device,
        mesh=mesh,
        in_specs=placed,
        out_specs=(
            P(None, "wt", "seq", None),
            P(None, "wt", "seq", None),
            P(None, ("seq", "wt")),
            P(None, ("seq", "wt"), None),
            P(None, ("seq", "wt"), None),
            P(None, None, ("seq", "wt")),
            P(None, ("seq", "wt"), None),
            P(None, ("seq", "wt")),
            P(None, ("seq", "wt"), None),
            P(None, ("seq", "wt")),
            P(None, ("seq", "wt"), None),
            P(None, ("seq", "wt"), None),
            P(None, ("seq", "wt"), None),
        ),
        check_vma=False,
    )
```

profile of v0, /device:TPU:3, one launch (start us, length us, event | category | flops | bytes accessed | tf_op | source)
XLA Modules:
  0.0 4947.7 jit_solution(15456652269636788413)
XLA Ops:
  27.0 40.9 all-reduce.147
  68.4 41.9 all-gather.1
  111.4 42.6 slice_reduce_fusion.7
  155.4 42.4 all-gather.14
  198.9 43.0 slice_reduce_fusion.3
  454.1 22.8 all-gather.6
  491.5 24.9 all-gather.5
  610.3 61.1 %all-gather.57.cloned.1.call-done = bf16[1,1536,2048]{2,1,0:T(8,128)(2,1)} async-done(((bf16[1,48,2048]{2,1,0:T(8,128)(2,1)}), bf16[1,1536,2048]{2,1,0:T(8,128)(2,1)}) %all-gather.57.cloned.1.call-update) | async-done | bytes 6291472 | tf_op jit(solution)/shard_map/all_gather | solution.py:342
  679.4 96.7 %all-gather.69.cloned.1.call-done = bf16[1,4608,1536]{2,1,0:T(8,128)(2,1)} async-done(((bf16[1,144,1536]{2,1,0:T(8,128)(2,1)}), bf16[1,4608,1536]{2,1,0:T(8,128)(2,1)}) %all-gather.69.cloned.1.call-update) | async-done | bytes 14155792 | tf_op jit(solution)/shard_map/all_gather | solution.py:350
  798.5 32.0 all-gather.59.cloned.1.call-done
  1031.9 25.0 all-gather.19
  1071.4 24.5 all-gather.18
  1124.4 60.4 %all-gather.65.cloned.1.call-done = bf16[1,1536,4608]{2,1,0:T(8,128)(2,1)} async-done(((bf16[1,48,4608]{2,1,0:T(8,128)(2,1)}), bf16[1,1536,4608]{2,1,0:T(8,128)(2,1)}) %all-gather.65.cloned.1.call-update) | async-done | bytes 14155792 | tf_op jit(solution)/shard_map/all_gather | solution.py:348
  1436.3 22.6 all-gather.26
  1700.6 22.3 all-gather.27
  1754.8 16.8 rev.18
  1975.8 53.0 %all-reduce.146 = (f32[1536]{0:T(1024)S(1)}, f32[1536]{0:T(1024)S(1)}, f32[2048]{0:T(1024)S(1)}, f32[2048]{0:T(1024)S(1)}, f32[1536]{0:T(1024)S(1)}, /*index=5*/f32[1536]{0:T(1024)S(1)}) all-reduce(f32[1536]{0:T(1024)S(1)} %copy-done.236, f32[1536]{0:T(1024)S(1)} %get-tuple-element.615, ...), channel_id=31, replica_groups=mesh['seq'=8,'wt'=4] {'seq','wt'}, use_global_device_ids=true, to_apply=%region_19.21.clone | all-reduce | flops 10240 | bytes 81920
  2034.6 35.9 reduce-scatter.51.cloned.1.call-done
  2072.0 133.5 %reduce-scatter.31.cloned.1.call-done = f32[128,128]{1,0:T(8,128)} async-done(((f32[4096,128]{1,0:T(8,128)}), f32[128,128]{1,0:T(8,128)}) %reduce-scatter.31.cloned.1.call-update) | async-done | bytes 65552 | tf_op jit(solution)/shard_map/reduce_scatter | solution.py:405
  2205.4 135.0 %reduce-scatter.29.cloned.1.call-done = f32[128,128]{1,0:T(8,128)} async-done(((f32[4096,128]{1,0:T(8,128)}), f32[128,128]{1,0:T(8,128)}) %reduce-scatter.29.cloned.1.call-update) | async-done | bytes 65552 | tf_op jit(solution)/shard_map/reduce_scatter | solution.py:405
  2342.0 169.5 %reduce-scatter.23.cloned.1.call-done = f32[48,2048]{1,0:T(8,128)} async-done(((f32[1536,2048]{1,0:T(8,128)}), f32[48,2048]{1,0:T(8,128)}) %reduce-scatter.23.cloned.1.call-update) | async-done | bytes 393232 | tf_op jit(solution)/shard_map/reduce_scatter | solution.py:402
  2511.5 161.7 %reduce-scatter.21.cloned.1.call-done = f32[48,2048]{1,0:T(8,128)} async-done(((f32[1536,2048]{1,0:T(8,128)}), f32[48,2048]{1,0:T(8,128)}) %reduce-scatter.21.cloned.1.call-update) | async-done | bytes 393232 | tf_op jit(solution)/shard_map/reduce_scatter | solution.py:402
  2675.2 158.6 %reduce-scatter.35.cloned.1.call-done = f32[64,1536]{1,0:T(8,128)} async-done(((f32[2048,1536]{1,0:T(8,128)}), f32[64,1536]{1,0:T(8,128)}) %reduce-scatter.35.cloned.1.call-update) | async-done | bytes 393232 | tf_op jit(solution)/shard_map/reduce_scatter | solution.py:407
  2833.9 161.9 %reduce-scatter.33.cloned.1.call-done = f32[64,1536]{1,0:T(8,128)} async-done(((f32[2048,1536]{1,0:T(8,128)}), f32[64,1536]{1,0:T(8,128)}) %reduce-scatter.33.cloned.1.call-update) | async-done | bytes 393232 | tf_op jit(solution)/shard_map/reduce_scatter | solution.py:407
  2997.8 158.4 %reduce-scatter.27.cloned.1.call-done = f32[48,2048]{1,0:T(8,128)} async-done(((f32[1536,2048]{1,0:T(8,128)}), f32[48,2048]{1,0:T(8,128)}) %reduce-scatter.27.cloned.1.call-update) | async-done | bytes 393232 | tf_op jit(solution)/shard_map/reduce_scatter | solution.py:403
  3156.2 161.7 %reduce-scatter.25.cloned.1.call-done = f32[48,2048]{1,0:T(8,128)} async-done(((f32[1536,2048]{1,0:T(8,128)}), f32[48,2048]{1,0:T(8,128)}) %reduce-scatter.25.cloned.1.call-update) | async-done | bytes 393232 | tf_op jit(solution)/shard_map/reduce_scatter | solution.py:403
  3320.0 268.5 %reduce-scatter.47.cloned.1.call-done = f32[144,1536]{1,0:T(8,128)} async-done(((f32[4608,1536]{1,0:T(8,128)}), f32[144,1536]{1,0:T(8,128)}) %reduce-scatter.47.cloned.1.call-update) | async-done | bytes 884752 | tf_op jit(solution)/shard_map/reduce_scatter | solution.py:390
  3588.5 269.8 %reduce-scatter.45.cloned.1.call-done = f32[144,1536]{1,0:T(8,128)} async-done(((f32[4608,1536]{1,0:T(8,128)}), f32[144,1536]{1,0:T(8,128)}) %reduce-scatter.45.cloned.1.call-update) | async-done | bytes 884752 | tf_op jit(solution)/shard_map/reduce_scatter | solution.py:390
  3861.0 266.9 %reduce-scatter.43.cloned.1.call-done = f32[48,4608]{1,0:T(8,128)} async-done(((f32[1536,4608]{1,0:T(8,128)}), f32[48,4608]{1,0:T(8,128)}) %reduce-scatter.43.cloned.1.call-update) | async-done | bytes 884752 | tf_op jit(solution)/shard_map/reduce_scatter | solution.py:389
  4127.9 270.0 %reduce-scatter.41.cloned.1.call-done = f32[48,4608]{1,0:T(8,128)} async-done(((f32[1536,4608]{1,0:T(8,128)}), f32[48,4608]{1,0:T(8,128)}) %reduce-scatter.41.cloned.1.call-update) | async-done | bytes 884752 | tf_op jit(solution)/shard_map/reduce_scatter | solution.py:389
  4400.7 267.3 %reduce-scatter.39.cloned.1.call-done = f32[48,4608]{1,0:T(8,128)} async-done(((f32[1536,4608]{1,0:T(8,128)}), f32[48,4608]{1,0:T(8,128)}) %reduce-scatter.39.cloned.1.call-update) | async-done | bytes 884752 | tf_op jit(solution)/shard_map/reduce_scatter | solution.py:388
  4668.0 269.7 %reduce-scatter.37.cloned.1.call-done = f32[48,4608]{1,0:T(8,128)} async-done(((f32[1536,4608]{1,0:T(8,128)}), f32[48,4608]{1,0:T(8,128)}) %reduce-scatter.37.cloned.1.call-update) | async-done | bytes 884752 | tf_op jit(solution)/shard_map/reduce_scatter | solution.py:388
  (1257 shorter events, 1379.6 us)
Async XLA Ops:
  7.2 236.0 %all-gather.43.cloned.1.call-start = ((), (), s32[]{:S(2)}) async-start(), calls=%async_computation.30 | async-start | bytes 6488064 | tf_op jit(solution)/shard_map/all_gather | solution.py:342
  9.1 251.1 %all-gather.45.cloned.1.call-start = ((), (), s32[]{:S(2)}) async-start(), calls=%async_computation.31 | async-start | bytes 1081344 | tf_op jit(solution)/shard_map/all_gather | solution.py:344
  10.6 507.0 %all-gather.47.cloned.1.call-start = ((), (), s32[]{:S(2)}) async-start(), calls=%async_computation.32 | async-start | bytes 6488064 | tf_op jit(solution)/shard_map/all_gather | solution.py:341
  12.6 515.1 %all-gather.49.cloned.1.call-start = ((), (), s32[]{:S(2)}) async-start(), calls=%async_computation.33 | async-start | bytes 6488064 | tf_op jit(solution)/shard_map/all_gather | solution.py:346
  13.5 549.4 %all-gather.51.cloned.1.call-start = ((), (), s32[]{:S(2)}) async-start(), calls=%async_computation.34 | async-start | bytes 14598144 | tf_op jit(solution)/shard_map/all_gather | solution.py:348
  14.6 558.9 %all-gather.53.cloned.1.call-start = ((), (), s32[]{:S(2)}) async-start(), calls=%async_computation.35 | async-start | bytes 14598144 | tf_op jit(solution)/shard_map/all_gather | solution.py:349
  15.7 585.1 %all-gather.55.cloned.1.call-start = ((), (), s32[]{:S(2)}) async-start(), calls=%async_computation.36 | async-start | bytes 14598144 | tf_op jit(solution)/shard_map/all_gather | solution.py:350
  18.0 653.5 %all-gather.57.cloned.1.call-start = ((), (), s32[]{:S(2)}) async-start(), calls=%async_computation.37 | async-start | bytes 6488064 | tf_op jit(solution)/shard_map/all_gather | solution.py:342
  18.7 757.4 %all-gather.69.cloned.1.call-start = ((), (), s32[]{:S(2)}) async-start(), calls=%async_computation.43 | async-start | bytes 14598144 | tf_op jit(solution)/shard_map/all_gather | solution.py:350
  19.5 811.1 %all-gather.59.cloned.1.call-start = ((), (), s32[]{:S(2)}) async-start(), calls=%async_computation.38 | async-start | bytes 1081344 | tf_op jit(solution)/shard_map/all_gather | solution.py:344
  20.0 1076.7 %all-gather.61.cloned.1.call-start = ((), (), s32[]{:S(2)}) async-start(), calls=%async_computation.39 | async-start | bytes 6488064 | tf_op jit(solution)/shard_map/all_gather | solution.py:341
  20.8 1086.0 %all-gather.63.cloned.1.call-start = ((), (), s32[]{:S(2)}) async-start(), calls=%async_computation.40 | async-start | bytes 6488064 | tf_op jit(solution)/shard_map/all_gather | solution.py:346
  21.4 1092.2 %all-gather.67.cloned.1.call-start = ((), (), s32[]{:S(2)}) async-start(), calls=%async_computation.42 | async-start | bytes 14598144 | tf_op jit(solution)/shard_map/all_gather | solution.py:349
  22.1 1162.7 %all-gather.65.cloned.1.call-start = ((), (), s32[]{:S(2)}) async-start(), calls=%async_computation.41 | async-start | bytes 14598144 | tf_op jit(solution)/shard_map/all_gather | solution.py:348
  22.3 220.8 %collective-permute-start.1 = (bf16[2,3]{1,0:T(2,128)(2,1)S(1)}, bf16[2,3]{1,0:T(2,128)(2,1)S(1)}, u32[]{:S(2)}, u32[]{:S(2)}) collective-permute-start(bf16[2,3]{1,0:T(2,128)(2,1)S(1)} %slice.1081), channel_id=1, source_target_pairs={{0,4},{4,8},{8,12},{12,16},{16,20},{20,24},{24,28},{1,5},{5,9},{9,... | collective-permute-start | bytes 44 | tf_op jit(solution)/shard_map/ppermute | solution.py:17
  25.5 2008.3 %reduce-scatter.49.cloned.1.call-start = ((), (), s32[]{:S(2)}) async-start(), calls=%async_computation.44 | async-start | bytes 1081344
  676.1 115.7 %collective-permute-start.2 = (bf16[2,3,2048]{2,1,0:T(4,128)(2,1)S(1)}, bf16[2,3,2048]{2,1,0:T(4,128)(2,1)S(1)}, u32[]{:S(2)}, u32[]{:S(2)}) collective-permute-start(bf16[2,3,2048]{2,1,0:T(4,128)(2,1)S(1)} %slice.1469), channel_id=1, source_target_pairs={{0,4},{4,8},{8,12},{12,16},{16,20},{20,24},{24,28},{1,5},{5,9},{9,... | collective-permute-start | bytes 73736 | tf_op jit(solution)/shard_map/ppermute | solution.py:17
  1804.5 266.0 %reduce-scatter.51.cloned.1.call-start = ((), (), s32[]{:S(2)}) async-start(), calls=%async_computation.45 | async-start | bytes 1081344
  1806.0 399.4 %reduce-scatter.31.cloned.1.call-start = ((), (), s32[]{:S(2)}) async-start(), calls=%async_computation.21 | async-start | bytes 2162688 | tf_op jit(solution)/shard_map/reduce_scatter | solution.py:405
  1808.1 532.4 %reduce-scatter.29.cloned.1.call-start = ((), (), s32[]{:S(2)}) async-start(), calls=%async_computation.20 | async-start | bytes 2162688 | tf_op jit(solution)/shard_map/reduce_scatter | solution.py:405
  1811.7 699.7 %reduce-scatter.23.cloned.1.call-start = ((), (), s32[]{:S(2)}) async-start(), calls=%async_computation.17 | async-start | bytes 12976128 | tf_op jit(solution)/shard_map/reduce_scatter | solution.py:402
  1819.5 853.7 %reduce-scatter.21.cloned.1.call-start = ((), (), s32[]{:S(2)}) async-start(), calls=%async_computation.16 | async-start | bytes 12976128 | tf_op jit(solution)/shard_map/reduce_scatter | solution.py:402
  1827.4 1006.5 %reduce-scatter.35.cloned.1.call-start = ((), (), s32[]{:S(2)}) async-start(), calls=%async_computation.23 | async-start | bytes 12976128 | tf_op jit(solution)/shard_map/reduce_scatter | solution.py:407
  1836.3 1159.5 %reduce-scatter.33.cloned.1.call-start = ((), (), s32[]{:S(2)}) async-start(), calls=%async_computation.22 | async-start | bytes 12976128 | tf_op jit(solution)/shard_map/reduce_scatter | solution.py:407
  1845.3 1311.0 %reduce-scatter.27.cloned.1.call-start = ((), (), s32[]{:S(2)}) async-start(), calls=%async_computation.19 | async-start | bytes 12976128 | tf_op jit(solution)/shard_map/reduce_scatter | solution.py:403
  1853.9 1464.0 %reduce-scatter.25.cloned.1.call-start = ((), (), s32[]{:S(2)}) async-start(), calls=%async_computation.18 | async-start | bytes 12976128 | tf_op jit(solution)/shard_map/reduce_scatter | solution.py:403
  1869.5 1719.0 %reduce-scatter.47.cloned.1.call-start = ((), (), s32[]{:S(2)}) async-start(), calls=%async_computation.29 | async-start | bytes 29196288 | tf_op jit(solution)/shard_map/reduce_scatter | solution.py:390
  1883.6 1974.7 %reduce-scatter.45.cloned.1.call-start = ((), (), s32[]{:S(2)}) async-start(), calls=%async_computation.28 | async-start | bytes 29196288 | tf_op jit(solution)/shard_map/reduce_scatter | solution.py:390
  1898.1 2229.9 %reduce-scatter.43.cloned.1.call-start = ((), (), s32[]{:S(2)}) async-start(), calls=%async_computation.27 | async-start | bytes 29196288 | tf_op jit(solution)/shard_map/reduce_scatter | solution.py:389
  1912.2 2485.8 %reduce-scatter.41.cloned.1.call-start = ((), (), s32[]{:S(2)}) async-start(), calls=%async_computation.26 | async-start | bytes 29196288 | tf_op jit(solution)/shard_map/reduce_scatter | solution.py:389
  1926.3 2741.6 %reduce-scatter.39.cloned.1.call-start = ((), (), s32[]{:S(2)}) async-start(), calls=%async_computation.25 | async-start | bytes 29196288 | tf_op jit(solution)/shard_map/reduce_scatter | solution.py:388
  1939.4 2998.3 %reduce-scatter.37.cloned.1.call-start = ((), (), s32[]{:S(2)}) async-start(), calls=%async_computation.24 | async-start | bytes 29196288 | tf_op jit(solution)/shard_map/reduce_scatter | solution.py:388
  (254 other events, 5446.7 us)
Sparse Core Ops, SparseCore 0:
  11.5 71.9 all-gather.42
  86.9 53.1 all-gather.44
  143.0 69.1 all-gather.46
  214.9 70.0 all-gather.48
  287.8 101.7 all-gather.50
  392.3 102.7 all-gather.52
  498.1 102.7 all-gather.54
  603.7 67.7 all-gather.56
  674.4 101.7 all-gather.68
  778.8 51.6 all-gather.58
  833.5 68.6 all-gather.60
  904.9 68.0 all-gather.62
  976.0 103.2 all-gather.66
  1082.1 102.6 all-gather.64
  1804.6 132.4 reduce-scatter.48
  1939.3 131.1 reduce-scatter.50
  2072.6 132.7 reduce-scatter.30
  2207.6 132.7 reduce-scatter.28
  2346.5 164.9 reduce-scatter.22
  2518.4 154.7 reduce-scatter.20
  2679.2 154.6 reduce-scatter.34
  2840.9 154.7 reduce-scatter.32
  3001.8 154.4 reduce-scatter.26
  3163.1 154.7 reduce-scatter.24
  3324.4 264.0 reduce-scatter.46
  3594.8 263.4 reduce-scatter.44
  3864.5 263.3 reduce-scatter.42
  4134.4 263.5 reduce-scatter.40
  4404.4 263.5 reduce-scatter.38
  4674.2 263.3 reduce-scatter.36
where the time goes:
time: 4970 us; the launch traced here: 4950 us
  waiting for transfers between devices  3160 us (64%)
  local copies, waits for them, and re-layouts  816 us (16%)
  matrix products  336 us (7%)
  blocking collectives  320 us (6%)
  other arithmetic  274 us (6%)
    reduce_scatter x2, waiting for transfers between devices, spread_mlp(): lax.psum_scatter(grad_down, ('seq', 'wt'), scatter_dimension=0, tiled=True)  538 us
    reduce_scatter x2, waiting for transfers between devices, spread_mlp(): lax.psum_scatter(grad_wgate, ('seq', 'wt'), scatter_dimension=0, tiled=True)  537 us
    reduce_scatter x2, waiting for transfers between devices, spread_mlp(): lax.psum_scatter(grad_wup, ('seq', 'wt'), scatter_dimension=0, tiled=True)  537 us
    dot_general x42, matrix products, product_dot(): return jnp.einsum(form, left, right, preferred_element_type=jnp.float32)  336 us
    reduce_scatter x2, waiting for transfers between devices, spread_rec(): lax.psum_scatter(grad_wgelu, ('seq', 'wt'), scatter_dimension=0, tiled=True)  331 us
    reduce_scatter x2, waiting for transfers between devices, spread_rec(): lax.psum_scatter(grad_wout, ('seq', 'wt'), scatter_dimension=0, tiled=True)  321 us
    reduce_scatter x2, waiting for transfers between devices, spread_rec(): lax.psum_scatter(grad_wstream, ('seq', 'wt'), scatter_dimension=0, tiled=...  320 us
    reduce_scatter x2, waiting for transfers between devices, spread_rec(): lax.psum_scatter(grad_gates, ('seq', 'wt'), scatter_dimension=0, tiled=True)  269 us
  transfers between devices with their start and end apart: 35, of which 22 were waited for; matrix products, arithmetic and copies ran while one was open for 17% of the time, Pallas kernels for 0%

commit v1 on v0

v1 whole, which is shorter than its diff:
```python
import functools

import jax
import jax.numpy as jnp
from jax import lax
from jax.experimental import pallas as pl
from jax.experimental.pallas import tpu as pltpu
from jax.sharding import PartitionSpec as P

f32 = jnp.float32
bf16 = jnp.bfloat16
HEAD_W = 128
CONV = 4
REACH = CONV - 1
TP = 4
EPS = 1e-06
DECAY = 8.0
GELU_C = 0.7978845608
GELU_K = 0.044715


def dot(left, right, out=f32):
    return lax.dot_general(left, right, (((1,), (0,)), ((), ())), preferred_element_type=f32).astype(out)


def dot_t(left, right, out=f32):
    return lax.dot_general(left, right, (((1,), (1,)), ((), ())), preferred_element_type=f32).astype(out)


def dot_tokens(left, right, out=bf16):
    return lax.dot_general(left, right, (((0,), (0,)), ((), ())), preferred_element_type=f32).astype(out)


def sigmoid(v):
    return 1.0 / (1.0 + jnp.exp(-v))


def gelu(v):
    return 0.5 * v * (1.0 + jnp.tanh(GELU_C * (v + GELU_K * v * v * v)))


def gelu_and_slope(v):
    square = v * v
    t = jnp.tanh(GELU_C * v * (1.0 + GELU_K * square))
    value = 0.5 * v * (1.0 + t)
    slope = 0.5 * (1.0 + t) + 0.5 * v * (1.0 - t * t) * GELU_C * (1.0 + 3.0 * GELU_K * square)
    return value, slope


def minus_expm1(y, e):
    series = -y * (1.0 + y * (1 / 2) * (1.0 + y * (1 / 3) * (1.0 + y * (1 / 4) * (1.0 + y * (1 / 5) * (1.0 + y * (1 / 6))))))
    return jnp.where(y > -0.25, series, 1.0 - e)


def rms_norm(v, gain):
    return v * lax.rsqrt(jnp.mean(v * v, axis=-1, keepdims=True) + EPS) * gain


def rms_norm_back(v, gain, dy):
    r = lax.rsqrt(jnp.mean(v * v, axis=-1, keepdims=True) + EPS)
    dgain = jnp.sum(dy * v * r, axis=0)
    dyg = dy * gain
    dv = r * dyg - v * (r * r * r) * jnp.mean(dyg * v, axis=-1, keepdims=True)
    return dv, dgain


def swap(x, k):
    return lax.ppermute(x, "wt", [(i, i ^ k) for i in range(TP)])


def tp_gather(x):
    far = swap(x, 2)
    near = swap(x, 1)
    diagonal = swap(far, 1)
    return jnp.concatenate([x, near, far, diagonal], axis=0)


def tp_scatter(part):
    far = (part[2].astype(f32) + swap(part[3], 1).astype(f32)).astype(bf16)
    across = swap(far, 2)
    near = swap(part[1], 1)
    return part[0].astype(f32) + near.astype(f32) + across.astype(f32)


def wt_exchange(pieces):
    w = lax.axis_index("wt")
    pick = lambda stack, j: lax.dynamic_index_in_dim(stack, j, 0, keepdims=False)
    got = [pick(pieces, w)] + [swap(pick(pieces, w ^ k), k) for k in range(1, TP)]
    stack = jnp.stack(got)
    return [pick(stack, w ^ j) for j in range(TP)]


def ring_tables():
    n = lax.axis_size("seq")
    order = [0, 1, 3, 5, 7, 6, 4, 2] if n == 8 else list(range(n))
    place = [0] * n
    for i, dev in enumerate(order):
        place[dev] = i
    right = [(order[i], order[(i + 1) % n]) for i in range(n)]
    left = [(b, a) for a, b in right]
    position = jnp.asarray(place, jnp.int32)[lax.axis_index("seq")]
    table = jnp.asarray(order, jnp.int32)
    device = lambda offset: table[lax.rem(position + offset + n, n)]
    return n, right, left, device


def ring_gather(block, flip, after=None):
    n, right, left, device = ring_tables()
    if flip:
        right, left = left, right
    sign = -1 if flip else 1
    if after is not None:
        block, _ = lax.optimization_barrier((block, after))
    out = jnp.zeros((n,) + block.shape, block.dtype)
    put = lambda o, b, k: lax.dynamic_update_index_in_dim(o, b, device(k), 0)
    out = put(out, block, 0)
    a = b = block
    marks = []
    for hop in range(1, n // 2 + 1):
        a = lax.ppermute(a, "seq", right)
        if hop <= n - 1 - n // 2:
            b = lax.ppermute(b, "seq", left)
            out = put(out, b, sign * hop)
        out = put(out, a, -sign * hop)
        marks.append(a)
    return out, marks


def ring_scatter(stack, flip):
    n, right, left, device = ring_tables()
    if flip:
        right, left = left, right
    sign = -1 if flip else 1
    chunk = lambda k: lax.dynamic_index_in_dim(stack, device(sign * k), 0, keepdims=False)
    add = lambda x, y: (x.astype(f32) + y.astype(f32)).astype(bf16)
    far, near = n // 2, n - 1 - n // 2
    a, b = chunk(far), chunk(-near)
    for hop in range(1, far + 1):
        a = lax.ppermute(a, "seq", right)
        if hop < far:
            a = add(a, chunk(far - hop))
        if hop <= near:
            b = lax.ppermute(b, "seq", left)
            if hop < near:
                b = add(b, chunk(hop - near))
    return chunk(0).astype(f32) + a.astype(f32) + b.astype(f32)


def shift_seq(x, distance):
    n = lax.axis_size("seq")
    return lax.ppermute(x, "seq", [(i, i + distance) for i in range(n) if 0 <= i + distance < n])


def carry_in(decay, state, direction):
    n = lax.axis_size("seq")
    width = decay.shape[-1]
    inclusive = jnp.concatenate([decay, state], axis=-1)

    def then(near, far):
        return jnp.concatenate(
            [near[:, :width] * far[:, :width], near[:, width:] + near[:, :width] * far[:, width:]], axis=-1
        )

    reach, covered, total = 1, 0, None
    while covered < n - 1:
        first = shift_seq(inclusive, direction * reach)
        second = shift_seq(inclusive, direction * 2 * reach) if covered + reach < n - 1 else None
        both = first if second is None else then(first, second)
        total = both if total is None else then(total, both)
        covered += 2 * reach if second is not None else reach
        inclusive = then(inclusive, both)
        reach *= 3
    return total[:, width:]


def head_route(rows):
    n = lax.axis_size("seq")
    per = HEAD_W // rows
    route = []
    for s in range(n):
        base = s // per * per
        for w in range(TP):
            b = TP * (s - base) + w
            route.append((s * TP + w, (base + b % per) * TP + b // per))
    return route


def to_heads(x):
    route = head_route(x.shape[0])
    return x if all(a == b for a, b in route) else lax.ppermute(x, ("seq", "wt"), route)


def from_heads(x):
    route = head_route(x.shape[0])
    return x if all(a == b for a, b in route) else lax.ppermute(x, ("seq", "wt"), [(b, a) for a, b in route])


def vector_scatter(v):
    w, s = lax.axis_index("wt"), lax.axis_index("seq")
    pick = lambda x, j, ax: lax.dynamic_index_in_dim(x, j, ax, keepdims=False)
    n, _, k = v.shape
    v = v.reshape(n, 2, 2, k)
    hi, lo = w >> 1, w & 1
    v = pick(v, hi, 1) + swap(pick(v, 1 - hi, 1), 2)
    v = pick(v, lo, 1) + swap(pick(v, 1 - lo, 1), 1)
    half = n // 2
    while half:
        v = v.reshape(2, half, k)
        bit = (s // half) % 2
        other = lax.ppermute(pick(v, 1 - bit, 0), "seq", [(i, i ^ half) for i in range(n)])
        v = pick(v, bit, 0) + other
        half //= 2
    return v.reshape(k)


def lay_stream(buf, src, streams, tokens, lead):
    for b in range(streams):
        buf[pl.ds(lead + b, tokens, stride=streams), :] = src[pl.ds(b * tokens, tokens), :].astype(f32)


def gate_values(pre_rows, decay_row, keep):
    sr = sigmoid(pre_rows[:, :HEAD_W])
    si = sigmoid(pre_rows[:, HEAD_W:])
    log_a = decay_row * sr
    raw = jnp.exp(log_a)
    e2 = raw * raw
    msq = keep * minus_expm1(2.0 * log_a, e2) + (1.0 - keep)
    return sr, si, raw, e2, jnp.sqrt(msq)


def mix_kernel(
    streams, tokens, stream_ref, halo_ref, keep_ref, taps_ref, decay_ref, gates_ref,
    a_ref, d_ref, conv_ref, ends_ref, buf, pre,
):
    lead = REACH * streams
    rows = streams * tokens
    step = 128
    buf[pl.ds(0, lead), :] = halo_ref[...]
    lay_stream(buf, stream_ref, streams, tokens, lead)
    taps = [taps_ref[pl.ds(k, 1), :] for k in range(CONV)]

    def conv_step(i, _):
        r = pl.multiple_of(i * step, step)
        total = taps[0] * buf[pl.ds(r + lead, step), :]
        valid = None
        for k in range(1, CONV):
            keep = keep_ref[pl.ds(r + lead - (k - 1) * streams, step), :]
            valid = keep if valid is None else valid * keep
            total = total + taps[k] * buf[pl.ds(r + lead - k * streams, step), :] * valid
        conv_ref[pl.ds(r, step), :] = total.astype(bf16)
        return 0

    lax.fori_loop(0, rows // step, conv_step, 0)
    pre[...] = jnp.dot(conv_ref[...], gates_ref[0], preferred_element_type=f32)

    def gate_step(i, _):
        r = pl.multiple_of(i * step, step)
        keep = keep_ref[pl.ds(r + lead, step), :]
        _, si, raw, _, m = gate_values(pre[pl.ds(r, step), :], decay_ref[...], keep)
        a_ref[pl.ds(r, step), :] = raw * keep
        d_ref[pl.ds(r, step), :] = m * si * conv_ref[pl.ds(r, step), :].astype(f32)
        return 0

    lax.fori_loop(0, rows // step, gate_step, 0)

    def scan_step(t, carry):
        total, h = carry
        r = pl.multiple_of(t * streams, streams)
        a = a_ref[pl.ds(r, streams), :]
        return total * a, a * h + d_ref[pl.ds(r, streams), :]

    total, h = lax.fori_loop(
        0, tokens, scan_step, (jnp.ones((streams, HEAD_W), f32), jnp.zeros((streams, HEAD_W), f32)), unroll=8
    )
    ends_ref[0] = total
    ends_ref[1] = h


def state_kernel(streams, tokens, a_ref, d_ref, start_ref, branch_ref, h_ref, merged_ref):
    def scan_step(t, h):
        r = pl.multiple_of(t * streams, streams)
        h = a_ref[pl.ds(r, streams), :] * h + d_ref[pl.ds(r, streams), :]
        h_ref[pl.ds(r, streams), :] = h
        return h

    lax.fori_loop(0, tokens, scan_step, start_ref[...], unroll=8)
    for b in range(streams):
        at = pl.ds(b * tokens, tokens)
        h = h_ref[pl.ds(b, tokens, stride=streams), :]
        merged_ref[at, :] = (h * gelu(branch_ref[at, :])).astype(bf16)


def state_back_kernel(streams, tokens, dm_ref, branch_ref, a_ref, h_ref, dh_ref, db_ref, ends_ref):
    for b in range(streams):
        at = pl.ds(b * tokens, tokens)
        dm = dm_ref[at, :]
        value, slope = gelu_and_slope(branch_ref[at, :])
        h = h_ref[pl.ds(b, tokens, stride=streams), :]
        dh_ref[pl.ds(b, tokens, stride=streams), :] = dm * value
        db_ref[at, :] = (dm * h * slope).astype(bf16)

    def scan_step(i, g):
        r = pl.multiple_of((tokens - 1 - i) * streams, streams)
        return a_ref[pl.ds(r, streams), :] * (dh_ref[pl.ds(r, streams), :] + g)

    ends_ref[...] = lax.fori_loop(0, tokens, scan_step, jnp.zeros((streams, HEAD_W), f32), unroll=8)


def mix_back_kernel(
    streams, tokens, dh_ref, a_ref, h_ref, start_ref, back_ref, conv_ref, stream_ref, halo_ref, keep_ref, taps_ref,
    decay_ref, slope_ref, gates_ref,
    ds_ref, tail_ref, head_ref, dgates_ref, dtaps_ref, ddecay_ref,
    buf, pre, back, dpre, dconv,
):
    lead = REACH * streams
    rows = streams * tokens
    step = 128
    buf[pl.ds(0, lead), :] = halo_ref[...]
    lay_stream(buf, stream_ref, streams, tokens, lead)
    pre[...] = jnp.dot(conv_ref[...], gates_ref[0], preferred_element_type=f32)

    def scan_step(i, g):
        r = pl.multiple_of((tokens - 1 - i) * streams, streams)
        total = dh_ref[pl.ds(r, streams), :] + g
        back[pl.ds(r, streams), :] = total
        return a_ref[pl.ds(r, streams), :] * total

    lax.fori_loop(0, tokens, scan_step, back_ref[...], unroll=8)
    dconv[pl.ds(rows, lead), :] = jnp.zeros((lead, HEAD_W), f32)

    def gate_step(i, acc):
        r = pl.multiple_of(i * step, step)
        keep = keep_ref[pl.ds(r + lead, step), :]
        decay = decay_ref[...]
        sr, si, raw, e2, m = gate_values(pre[pl.ds(r, step), :], decay, keep)
        g = back[pl.ds(r, step), :]
        conv = conv_ref[pl.ds(r, step), :].astype(f32)
        before = h_ref[pl.ds(jnp.maximum(r - streams, 0), step), :]
        shifted = jnp.concatenate([start_ref[...], before[: step - streams]], axis=0)
        previous = jnp.where(i == 0, shifted, before)
        gsi = g * si
        gm = gsi * m
        dconv[pl.ds(r, step), :] = gm
        d_input = gm * conv * (1.0 - si)
        d_log = g * previous * raw * keep - gsi * conv * keep * e2 / m
        by_rate = d_log * sr
        d_rate = by_rate * decay * (1.0 - sr)
        dpre[pl.ds(r, step), :] = jnp.concatenate([d_rate.astype(bf16), d_input.astype(bf16)], axis=1)
        return acc + jnp.sum(by_rate.reshape(step // 8, 8, HEAD_W), axis=0)

    acc = lax.fori_loop(0, rows // step, gate_step, jnp.zeros((8, HEAD_W), f32))
    ddecay_ref[...] = jnp.sum(acc, axis=0, keepdims=True) * slope_ref[...]
    dgates_ref[0] = lax.dot_general(conv_ref[...], dpre[...], (((0,), (0,)), ((), ())), preferred_element_type=f32)
    pre[:, :HEAD_W] = lax.dot_general(dpre[...], gates_ref[0], (((1,), (1,)), ((), ())), preferred_element_type=f32)
    taps = [taps_ref[pl.ds(k, 1), :] for k in range(CONV)]

    def add_step(i, accs):
        r = pl.multiple_of(i * step, step)
        dc = dconv[pl.ds(r, step), :] + pre[pl.ds(r, step), :HEAD_W]
        dconv[pl.ds(r, step), :] = dc
        out, valid = [], None
        for k in range(CONV):
            term = dc * buf[pl.ds(r + lead - k * streams, step), :]
            if k:
                keep = keep_ref[pl.ds(r + lead - (k - 1) * streams, step), :]
                valid = keep if valid is None else valid * keep
                term = term * valid
            out.append(accs[k] + jnp.sum(term.reshape(step // 8, 8, HEAD_W), axis=0))
        return tuple(out)

    accs = lax.fori_loop(0, rows // step, add_step, tuple(jnp.zeros((8, HEAD_W), f32) for _ in range(CONV)))
    for k in range(CONV):
        dtaps_ref[pl.ds(k, 1), :] = jnp.sum(accs[k], axis=0, keepdims=True)

    def stream_rows(r, count):
        total = taps[0] * dconv[pl.ds(r, count), :]
        valid = None
        for k in range(1, CONV):
            keep = keep_ref[pl.ds(r + lead + k * streams, count), :]
            valid = keep if valid is None else valid * keep
            total = total + taps[k] * dconv[pl.ds(r + k * streams, count), :] * valid
        return total

    def stream_step(i, _):
        r = pl.multiple_of(i * step, step)
        buf[pl.ds(r, step), :] = stream_rows(r, step)
        return 0

    lax.fori_loop(0, rows // step, stream_step, 0)
    tail_ref[...] = buf[pl.ds(rows - lead, lead), :]
    for b in range(streams):
        ds_ref[pl.ds(b * tokens, tokens), :] = buf[pl.ds(b, tokens, stride=streams), :].astype(bf16)
    for j in range(REACH):
        total = None
        valid = None
        for k in range(1, CONV):
            at = j + k - REACH
            keep = keep_ref[pl.ds((j + k) * streams, streams), :]
            valid = keep if valid is None else valid * keep
            if at >= 0:
                term = taps[k] * dconv[pl.ds(at * streams, streams), :] * valid
                total = term if total is None else total + term
        head_ref[pl.ds(j * streams, streams), :] = total


def by_head(rows):
    return pl.BlockSpec((rows, HEAD_W), lambda h: (0, h))


def whole(rows):
    return pl.BlockSpec((rows, HEAD_W), lambda h: (0, 0))


def params():
    return pltpu.CompilerParams(vmem_limit_bytes=40 * 2**20, dimension_semantics=("arbitrary",))


def mix(streams, stream, halo, keep, taps, decay, gates):
    rows, width = stream.shape
    tokens, heads, lead = rows // streams, width // HEAD_W, REACH * streams
    two = pl.BlockSpec((2, streams, HEAD_W), lambda h: (0, 0, h))
    shape = jax.ShapeDtypeStruct
    return pl.pallas_call(
        functools.partial(mix_kernel, streams, tokens),
        grid=(heads,),
        in_specs=[
            by_head(rows), by_head(lead), whole(keep.shape[0]), by_head(CONV), by_head(1),
            pl.BlockSpec((1, HEAD_W, 2 * HEAD_W), lambda h: (h, 0, 0)),
        ],
        out_specs=[by_head(rows), by_head(rows), by_head(rows), two],
        out_shape=[
            shape((rows, width), f32), shape((rows, width), f32), shape((rows, width), bf16), shape((2, streams, width), f32),
        ],
        scratch_shapes=[pltpu.VMEM((rows + lead, HEAD_W), f32), pltpu.VMEM((rows, 2 * HEAD_W), f32)],
        compiler_params=params(),
        cost_estimate=pl.CostEstimate(flops=rows * width * 600, bytes_accessed=rows * width * 12, transcendentals=rows * width * 6),
    )(stream, halo, keep, taps, decay, gates)


def states(streams, a, driven, start, branch):
    rows, width = a.shape
    tokens, heads = rows // streams, width // HEAD_W
    shape = jax.ShapeDtypeStruct
    return pl.pallas_call(
        functools.partial(state_kernel, streams, tokens),
        grid=(heads,),
        in_specs=[by_head(rows), by_head(rows), by_head(streams), by_head(rows)],
        out_specs=[by_head(rows), by_head(rows)],
        out_shape=[shape((rows, width), f32), shape((rows, width), bf16)],
        compiler_params=params(),
        cost_estimate=pl.CostEstimate(flops=rows * width * 30, bytes_accessed=rows * width * 18, transcendentals=rows * width),
    )(a, driven, start, branch)


def states_back(streams, d_merged, branch, a, h):
    rows, width = a.shape
    tokens, heads = rows // streams, width // HEAD_W
    shape = jax.ShapeDtypeStruct
    return pl.pallas_call(
        functools.partial(state_back_kernel, streams, tokens),
        grid=(heads,),
        in_specs=[by_head(rows)] * 4,
        out_specs=[by_head(rows), by_head(rows), by_head(streams)],
        out_shape=[shape((rows, width), f32), shape((rows, width), bf16), shape((streams, width), f32)],
        compiler_params=params(),
        cost_estimate=pl.CostEstimate(flops=rows * width * 40, bytes_accessed=rows * width * 22, transcendentals=rows * width),
    )(d_merged, branch, a, h)


def mix_back(streams, dh, a, h, start, back, conv, stream, halo, keep, taps, decay, slope, gates):
    rows, width = a.shape
    tokens, heads, lead = rows // streams, width // HEAD_W, REACH * streams
    shape = jax.ShapeDtypeStruct
    gate_spec = pl.BlockSpec((1, HEAD_W, 2 * HEAD_W), lambda h: (h, 0, 0))
    return pl.pallas_call(
        functools.partial(mix_back_kernel, streams, tokens),
        grid=(heads,),
        in_specs=[
            by_head(rows), by_head(rows), by_head(rows), by_head(streams), by_head(streams), by_head(rows), by_head(rows),
            by_head(lead), whole(keep.shape[0]), by_head(CONV), by_head(1), by_head(1), gate_spec,
        ],
        out_specs=[by_head(rows), by_head(lead), by_head(lead), gate_spec, by_head(CONV), by_head(1)],
        out_shape=[
            shape((rows, width), bf16), shape((lead, width), f32), shape((lead, width), f32),
            shape((heads, HEAD_W, 2 * HEAD_W), f32), shape((CONV, width), f32), shape((1, width), f32),
        ],
        scratch_shapes=[
            pltpu.VMEM((rows + lead, HEAD_W), f32), pltpu.VMEM((rows, 2 * HEAD_W), f32), pltpu.VMEM((rows, HEAD_W), f32),
            pltpu.VMEM((rows, 2 * HEAD_W), bf16), pltpu.VMEM((rows + lead, HEAD_W), f32),
        ],
        compiler_params=params(),
        cost_estimate=pl.CostEstimate(flops=rows * width * 1200, bytes_accessed=rows * width * 22, transcendentals=rows * width * 6),
    )(dh, a, h, start, back, conv, stream, halo, keep, taps, decay, slope, gates)


def head_columns(block):
    rows, width = block.shape
    groups = width // (TP * HEAD_W)
    return block.reshape(rows, groups, TP, HEAD_W).transpose(2, 0, 1, 3).reshape(TP, rows, width // TP)


def ff_columns(block):
    rows, width = block.shape
    n = lax.axis_size("seq")
    return block.reshape(rows, n, TP, width // (n * TP)).transpose(2, 0, 1, 3).reshape(TP, rows, width // TP)


def head_columns_back(pieces):
    groups = pieces[0].shape[1] // HEAD_W
    rows = pieces[0].shape[0]
    stack = jnp.stack([p.reshape(rows, groups, HEAD_W) for p in pieces], axis=2)
    return stack.reshape(rows, -1)


def ff_columns_back(pieces):
    n = lax.axis_size("seq")
    rows, width = pieces[0].shape
    stack = jnp.stack([p.reshape(rows, n, width // n) for p in pieces], axis=2)
    return stack.reshape(rows, -1)


def send_weights(shards, after):
    (mix_gain, proj_gelu, proj_stream, conv_taps, lru_gates, decay_param, proj_out, mlp_gain, proj_gate, proj_up, proj_down) = shards
    rp = proj_gelu.shape[0]
    gr = lru_gates.shape[0] // TP
    small = jnp.concatenate([mix_gain, mlp_gain, conv_taps.reshape(-1), decay_param])
    top = jnp.pad(small, (0, (rp - gr) * HEAD_W - small.shape[0])).reshape(rp - gr, HEAD_W)
    extra = jnp.concatenate([top, jnp.zeros((gr, HEAD_W), bf16)])
    pieces = jnp.concatenate(
        [head_columns(proj_gelu), head_columns(proj_stream), jnp.broadcast_to(extra, (TP, rp, HEAD_W))], axis=2
    )
    got = jnp.stack(wt_exchange(pieces))
    gates = to_heads(lru_gates).reshape(TP, gr, HEAD_W)
    width = got.shape[2] - HEAD_W
    got = lax.dynamic_update_slice(got, gates, (0, rp - gr, width))
    first, marks1 = ring_gather(got.reshape(TP * rp, width + HEAD_W), False, after)
    rows = jnp.concatenate([proj_down, to_heads(proj_out)])
    second, marks2 = ring_gather(rows, True, marks1[1])
    wide = jnp.concatenate([ff_columns(proj_gate), ff_columns(proj_up)], axis=2)
    wide = jnp.stack(wt_exchange(wide)).reshape(TP * rp, -1)
    third, marks3 = ring_gather(wide, False, marks2[1])
    return (first, second, third), marks3[1]


def open_weights(gathered, sizes):
    first, second, third = gathered
    rp, gr, cp, fb = sizes
    w = lax.axis_index("wt")
    n = first.shape[0]
    depth = n * TP * rp
    width = first.shape[2] - HEAD_W
    flat = first.reshape(depth, width + HEAD_W)
    extra = flat[:, width:].reshape(n * TP, rp, HEAD_W)
    small = extra[:, : rp - gr].reshape(n * TP, -1)
    mix_gain = small[:, :rp].reshape(-1).astype(f32)
    mlp_gain = small[:, rp : 2 * rp].reshape(-1).astype(f32)
    at = 2 * rp

    def own_heads(v):
        v = v.reshape(v.shape[0], -1, TP, HEAD_W)
        return lax.dynamic_index_in_dim(v, w, 2, keepdims=False).reshape(v.shape[0], -1).astype(f32)

    taps = own_heads(small[:, at : at + CONV * cp].reshape(n * TP, CONV, cp).transpose(1, 0, 2).reshape(CONV, -1))
    decay = own_heads(small[:, at + CONV * cp : at + (CONV + 1) * cp].reshape(1, -1))
    gates = extra[:, rp - gr :].reshape(2, -1, HEAD_W, HEAD_W).transpose(1, 2, 0, 3)
    gates = gates.reshape(-1, HEAD_W, 2 * HEAD_W)
    return dict(
        gelu=flat[:, : width // 2], stream=flat[:, width // 2 : width],
        mix_gain=mix_gain, mlp_gain=mlp_gain, taps=taps, gates=gates,
        decay=-DECAY * jax.nn.softplus(decay), slope=-DECAY * jax.nn.sigmoid(decay),
        down=second[:, :fb].reshape(n * fb, -1), out=second[:, fb:].reshape(-1, second.shape[2]),
        wide=third.reshape(depth, -1),
    )


def forward_block(x, keep, streams, wts):
    width = x.shape[1]
    normed = tp_gather(rms_norm(x, wts["mix_gain"]).astype(bf16))
    tokens = normed.shape[0] // streams
    last = normed.reshape(streams, tokens, width)[:, tokens - REACH :].transpose(1, 0, 2)
    halo_in = shift_seq(last.reshape(REACH * streams, width), 1)
    stream = dot(normed, wts["stream"], bf16)
    branch = dot(normed, wts["gelu"])
    halo = dot(halo_in, wts["stream"], bf16).astype(f32)
    a, driven, conv, ends = mix(streams, stream, halo, keep, wts["taps"], wts["decay"], wts["gates"])
    start = carry_in(ends[0], ends[1], 1)
    h, merged = states(streams, a, driven, start, branch)
    x1 = x + tp_scatter(dot(merged, wts["out"], bf16).reshape(TP, -1, width))
    mlp_in = tp_gather(rms_norm(x1, wts["mlp_gain"]).astype(bf16))
    wide = dot(mlp_in, wts["wide"])
    half = wide.shape[1] // 2
    product = (gelu(wide[:, :half]) * wide[:, half:]).astype(bf16)
    x2 = x1 + tp_scatter(dot(product, wts["down"], bf16).reshape(TP, -1, width))
    kept = dict(
        x=x, normed=normed, stream=stream, branch=branch, halo=halo, a=a, conv=conv, whole=ends[0], start=start, h=h,
        merged=merged, x1=x1, mlp_in=mlp_in, wide=wide, product=product,
    )
    return x2, kept


def mlp_back(gx, g_down, wts, kept):
    width = gx.shape[1]
    n = lax.axis_size("seq")
    grad_down = dot_tokens(kept["product"], g_down)
    d_product = dot_t(g_down, wts["down"])
    wide = kept["wide"]
    half = wide.shape[1] // 2
    value, slope = gelu_and_slope(wide[:, :half])
    d_wide = jnp.concatenate([(d_product * wide[:, half:] * slope).astype(bf16), (d_product * value).astype(bf16)], axis=1)
    grad_wide = dot_tokens(kept["mlp_in"], d_wide)
    d_mlp_in = tp_scatter(dot_t(d_wide, wts["wide"], bf16).reshape(TP, -1, width))
    dv, d_gain = rms_norm_back(kept["x1"], wts["mlp_gain"], d_mlp_in)
    down = ring_scatter(grad_down.reshape(n, -1, width), False)
    wide = ring_scatter(grad_wide.reshape(n, -1, grad_wide.shape[1]), True)
    return gx + dv, d_gain, down, wide


def mixer_back(d_x1, keep, streams, wts, kept, d_mlp_gain, d_mix_gain, sizes):
    rp, gr, cp, fb = sizes
    width = d_x1.shape[1]
    n, w = lax.axis_size("seq"), lax.axis_index("wt")
    g_branch = tp_gather(d_x1.astype(bf16))
    d_merged = dot_t(g_branch, wts["out"])
    grad_out = dot_tokens(kept["merged"], g_branch)
    dh, d_branch, ends = states_back(streams, d_merged, kept["branch"], kept["a"], kept["h"])
    back = carry_in(kept["whole"], ends, -1)
    d_stream, tail, head, d_gates, d_taps, d_decay = mix_back(
        streams, dh, kept["a"], kept["h"], kept["start"], back, kept["conv"], kept["stream"], kept["halo"], keep,
        wts["taps"], wts["decay"], wts["slope"], wts["gates"],
    )
    tail = (tail + shift_seq(head, -1)).astype(bf16)
    tokens = d_stream.shape[0] // streams
    d_stream = lax.dynamic_update_slice(
        d_stream.reshape(streams, tokens, -1), tail.reshape(REACH, streams, -1).transpose(1, 0, 2), (0, tokens - REACH, 0)
    ).reshape(d_stream.shape)
    both = jnp.concatenate([d_branch, d_stream], axis=1)
    grad_both = dot_tokens(kept["normed"], both)

    def full(v):
        lines = v.reshape(v.shape[0], -1, 1, HEAD_W)
        return jnp.where(lax.iota(jnp.int32, TP)[None, None, :, None] == w, lines, 0.0).reshape(v.shape[0], n * TP, -1)

    small = jnp.concatenate(
        [
            d_mix_gain.reshape(n * TP, rp), d_mlp_gain.reshape(n * TP, rp),
            full(d_taps).transpose(1, 0, 2).reshape(n * TP, -1), full(d_decay)[0],
        ],
        axis=1,
    ).astype(bf16)
    used = small.shape[1]
    small = jnp.pad(small, ((0, 0), (0, (rp - gr) * HEAD_W - used))).reshape(n * TP, rp - gr, HEAD_W)
    gates = d_gates.reshape(-1, HEAD_W, 2, HEAD_W).transpose(2, 0, 1, 3).reshape(n * TP, gr, HEAD_W).astype(bf16)
    extra = jnp.concatenate([small, gates], axis=1).reshape(n, TP * rp, HEAD_W)
    both_sum = ring_scatter(
        jnp.concatenate([grad_both.reshape(n, TP * rp, -1), extra], axis=2), False
    )
    out = from_heads(ring_scatter(grad_out.reshape(n, -1, width), True))
    d_normed = tp_scatter(
        (dot_t(d_branch, wts["gelu"]) + dot_t(d_stream, wts["stream"])).astype(bf16).reshape(TP, -1, width)
    )
    dv, d_gain = rms_norm_back(kept["x"], wts["mix_gain"], d_normed)
    return d_x1 + dv, d_gain, both_sum, out, used


def finish_wide(wide, rp):
    pieces = wt_exchange(wide.astype(bf16).reshape(TP, rp, -1))
    half = wide.shape[1] // 2
    return (
        ff_columns_back([p[:, :half] for p in pieces]).astype(f32),
        ff_columns_back([p[:, half:] for p in pieces]).astype(f32),
    )


def finish_both(both, sizes, used):
    rp, gr, cp, fb = sizes
    width = both.shape[1] - HEAD_W
    stack = both.reshape(TP, rp, -1)
    gates = from_heads(stack[:, rp - gr :, width:].reshape(TP * gr, HEAD_W))
    pieces = wt_exchange(both.astype(bf16).reshape(TP, rp, -1))
    half = width // 2
    gelu_part = head_columns_back([p[:, :half] for p in pieces]).astype(f32)
    stream_part = head_columns_back([p[:, half:width] for p in pieces]).astype(f32)
    small = sum(p[: rp - gr, width:].astype(f32) for p in pieces).reshape(-1)[:used]
    d_mix, d_mlp = small[:rp], small[rp : 2 * rp]
    d_taps = small[2 * rp : 2 * rp + CONV * cp].reshape(CONV, cp)
    d_decay = small[2 * rp + CONV * cp :]
    return gelu_part, stream_part, gates, d_mix, d_mlp, d_taps, d_decay


def per_device(block_in, start_flags, out_grad, *shards):
    layers = shards[0].shape[0]
    n = lax.axis_size("seq")
    micro, _, tokens, width = block_in.shape
    streams = micro * TP
    lead = REACH * streams
    sizes = (shards[1].shape[1], shards[4].shape[1] // TP, shards[5].shape[1], shards[10].shape[1])
    rp = sizes[0]

    gathered, mark = [], None
    for layer in range(layers):
        sent, mark = send_weights([s[layer] for s in shards], mark)
        gathered.append(sent)

    flags = tp_gather(start_flags[:, 0].astype(f32))
    keep = 1.0 - flags.T
    behind = 1.0 - shift_seq(flags[:, tokens - REACH :].T, 1)
    keep = jnp.concatenate([behind, keep, jnp.ones((REACH, streams), f32)]).reshape(-1, 1)
    keep = jnp.broadcast_to(keep, (keep.shape[0], HEAD_W))

    x = block_in[:, 0].astype(f32).reshape(micro * tokens, width)
    grad = out_grad[:, 0].reshape(micro * tokens, width)
    wts, kept = [], []
    for layer in range(layers):
        wts.append(open_weights(gathered[layer], sizes))
        x, saved = forward_block(x, keep, streams, wts[layer])
        kept.append(saved)

    gx = grad.astype(f32)
    d_mix = jnp.zeros((width,), f32)
    results = [None] * layers
    for layer in reversed(range(layers)):
        g_down = tp_gather(gx.astype(bf16))
        d_x1, d_mlp, down, wide = mlp_back(gx, g_down, wts[layer], kept[layer])
        gate_part, up_part = finish_wide(wide, rp)
        gx, d_mix_next, both, out, used = mixer_back(d_x1, keep, streams, wts[layer], kept[layer], d_mlp, d_mix, sizes)
        gelu_part, stream_part, gates, mix_part, mlp_part, taps, decay = finish_both(both, sizes, used)
        if layer != layers - 1:
            results[layer + 1][0] = mix_part
        results[layer] = [None, gelu_part, stream_part, taps, gates, decay, out, mlp_part, gate_part, up_part, down]
        d_mix = d_mix_next
    results[0][0] = vector_scatter(d_mix.reshape(n, TP, rp))
    shape = (micro, 1, tokens, width)
    stacked = [jnp.stack([results[layer][k] for layer in range(layers)]) for k in range(11)]
    return (x.astype(bf16).reshape(shape), gx.astype(bf16).reshape(shape), *stacked)


def solution(mesh):
    both = ("seq", "wt")
    tokens = P(None, "wt", "seq", None)
    vector, matrix = P(None, both), P(None, both, None)
    weights = (vector, matrix, matrix, P(None, None, both), matrix, vector, matrix, vector, matrix, matrix, matrix)
    return jax.shard_map(
        per_device,
        mesh=mesh,
        in_specs=(tokens, P(None, "wt", "seq"), tokens, *weights),
        out_specs=(tokens, tokens, *weights),
        check_vma=False,
    )
```

time: 4970 us -> 1290 us (0.26)
  waiting for transfers between devices: 3160 us -> 473 us
  local copies, waits for them, and re-layouts: 816 us -> 170 us
  blocking collectives: 320 us -> 0 us
  starting transfers between devices: 18.2 us -> 266 us
  matrix products: 336 us -> 160 us
  other arithmetic: 274 us -> 114 us
  Pallas kernels: 0 us -> 62.8 us
    reduce_scatter x14 -> x0, waiting for transfers between devices: 2850 us -> none  [the longest x2 538 us: spread_mlp(): lax.psum_scatter(grad_down, ('seq', 'wt'), scatter_dimension=0, tiled=True)]
    slice x203 -> x50, local copies, waits for them, and re-layouts: 521 us -> 28.8 us  [the longest x8 8.42 us: finish_wide(): p[:, half:]]
    ppermute x5 -> x203, waiting for transfers between devices: 6.39 us -> 473 us  [the longest x24 135 us: ring_gather(): a = lax.ppermute(a, 'seq', right)]
    all_gather x14 -> x0, waiting for transfers between devices: 265 us -> none  [the longest x2 111 us: fetch_weights(): lax.all_gather(proj_down[layer_index], ('seq', 'wt'), axis=0, tiled=True)]
    ppermute x5 -> x203, starting transfers between devices: 16.6 us -> 266 us  [the longest x77 119 us: swap(): return lax.ppermute(x, 'wt', [(i, i ^ k) for i in range(TP)])]
    all_gather x8 -> x0, blocking collectives: 226 us -> none  [the longest x6 142 us: carried_in(): lax.all_gather(part.astype(kind), axis)]
    dot_general x42 -> x30, matrix products: 336 us -> 160 us  [the longest x10 66.1 us: dot_t(): lax.dot_general(left, right, (((1,), (1,)), ((), ())), preferred_element_...]
    pad x96 -> x0, local copies, waits for them, and re-layouts: 141 us -> none  [the longest x48 93.7 us: forward_layer(): lax.associative_scan(chain_step, (decay_eff, driven), axis=1)]
  transfers between devices with their start and end apart: 35 -> 203, of which waited for: 22 -> 70; matrix products, arithmetic and copies ran while one was open for 17% -> 31% of each run, Pallas kernels for 0% -> 5%
where the time goes in v1:
time: 1290 us; the launch traced here: 1270 us
  waiting for transfers between devices  473 us (37%)
  starting transfers between devices  266 us (21%)
  local copies, waits for them, and re-layouts  170 us (13%)
  matrix products  160 us (12%)
  other arithmetic  114 us (9%)
  Pallas kernels  62.8 us (5%)
  between operations  28.7 us (2%)
    ppermute x24, waiting for transfers between devices, ring_gather(): a = lax.ppermute(a, 'seq', right)  135 us
    ppermute x77, starting transfers between devices, swap(): return lax.ppermute(x, 'wt', [(i, i ^ k) for i in range(TP)])  119 us
    ppermute x77, waiting for transfers between devices, swap(): return lax.ppermute(x, 'wt', [(i, i ^ k) for i in range(TP)])  105 us
    ppermute x32, waiting for transfers between devices, ring_scatter(): a = lax.ppermute(a, 'seq', right)  68.3 us
    ppermute x18, waiting for transfers between devices, ring_gather(): b = lax.ppermute(b, 'seq', left)  66.5 us
    dot_general x10, matrix products, dot_t(): lax.dot_general(left, right, (((1,), (1,)), ((), ())), preferred_element_...  66.1 us
    ppermute x21, starting transfers between devices, shift_seq(): lax.ppermute(x, 'seq', [(i, i + distance) for i in range(n) if 0 <= i + d...  51.8 us
    dot_general x8, matrix products, dot_tokens(): lax.dot_general(left, right, (((0,), (0,)), ((), ())), preferred_element_...  48.8 us
  transfers between devices with their start and end apart: 203, of which 70 were waited for; matrix products, arithmetic and copies ran while one was open for 31% of the time, Pallas kernels for 5%

profile of v1, /device:TPU:3, one launch (start us, length us, event | category | flops | bytes accessed | tf_op | source)
XLA Modules:
  0.0 1274.2 jit_solution(3950616655993113426)
XLA Ops:
  99.5 8.9 collective-permute-done.6
  115.1 19.3 %collective-permute-done.8 = bf16[192,1152]{1,0:T(8,128)(2,1)S(1)} collective-permute-done((bf16[192,1152]{1,0:T(8,128)(2,1)S(1)}, bf16[192,1152]{1,0:T(8,128)(2,1)S(1)}, u32[]{:S(2)}, u32[]{:S(2)}) %collective-permute-start.8) | collective-permute-done | bytes 442400 | tf_op jit(solution)/shard_map/ppermute | solution.py:120
  162.1 28.5 %collective-permute-done.27 = bf16[208,1536]{1,0:T(8,128)(2,1)S(1)} collective-permute-done((bf16[208,1536]{1,0:T(8,128)(2,1)}, bf16[208,1536]{1,0:T(8,128)(2,1)S(1)}, u32[]{:S(2)}, u32[]{:S(2)}) %collective-permute-start.27) | collective-permute-done | bytes 639008 | tf_op jit(solution)/shard_map/ppermute | solution.py:122
  199.0 10.3 collective-permute-done.39
  226.3 8.8 shard_map.489
  285.2 26.1 %collective-permute-done.55 = bf16[192,1152]{1,0:T(8,128)(2,1)S(1)} collective-permute-done((bf16[192,1152]{1,0:T(8,128)(2,1)S(1)}, bf16[192,1152]{1,0:T(8,128)(2,1)S(1)}, u32[]{:S(2)}, u32[]{:S(2)}) %collective-permute-start.55) | collective-permute-done | bytes 442400 | tf_op jit(solution)/shard_map/ppermute | solution.py:120
  331.9 11.7 collective-permute-done.57
  351.6 11.0 collective-permute-done.45
  364.7 10.0 collective-permute-done.69
  378.1 8.8 fusion.99
  413.3 11.6 collective-permute-done.48
  434.6 11.0 collective-permute-done.60
  457.9 13.6 %collective-permute-done.62 = bf16[24,1536]{1,0:T(8,128)(2,1)S(1)} collective-permute-done((bf16[24,1536]{1,0:T(8,128)(2,1)S(1)}, bf16[24,1536]{1,0:T(8,128)(2,1)S(1)}, u32[]{:S(2)}, u32[]{:S(2)}) %collective-permute-start.62) | collective-permute-done | bytes 73760 | tf_op jit(solution)/shard_map/ppermute | solution.py:151
  512.8 12.5 collective-permute-done.86
  530.2 17.6 %collective-permute-done.89 = bf16[192,2304]{1,0:T(8,128)(2,1)S(1)} collective-permute-done((bf16[192,2304]{1,0:T(8,128)(2,1)S(1)}, bf16[192,2304]{1,0:T(8,128)(2,1)S(1)}, u32[]{:S(2)}, u32[]{:S(2)}) %collective-permute-start.89) | collective-permute-done | bytes 884768 | tf_op jit(solution)/shard_map/ppermute | solution.py:120
  550.6 16.8 %collective-permute-done.90 = bf16[192,2304]{1,0:T(8,128)(2,1)S(1)} collective-permute-done((bf16[192,2304]{1,0:T(8,128)(2,1)S(1)}, bf16[192,2304]{1,0:T(8,128)(2,1)S(1)}, u32[]{:S(2)}, u32[]{:S(2)}) %collective-permute-start.90) | collective-permute-done | bytes 884768 | tf_op jit(solution)/shard_map/ppermute | solution.py:120
  567.5 12.0 fusion.98
  579.6 14.2 %multiply_convert_fusion.3 = (bf16[1024,1152]{1,0:T(8,128)(2,1)}, bf16[1024,1152]{1,0:T(8,128)(2,1)}, bf16[1024,1152]{1,0:T(8,128)(2,1)}) fusion(f32[1024,2304]{1,0:T(8,128)} %fusion.98, bf16[1152,1536]{1,0:T(8,128)(2,1)S(1)} %bitcast.812, bf16[256,1536]{1,0:T(8,128)(2,1)} %collective-permute-done.96, bf16[256,1536]{1,0:T(8,128)(2,1)} %collective-permute-done.95, ...), kind=kOutput, calls=%fused_computation.42 | convolution fusion | flops 3673030656 | bytes 23199744 | tf_op jit(solution)/shard_map/dot_general | solution.py:27
  603.6 9.3 convolution_convert_fusion.5
  627.7 10.7 convolution_convert_fusion
  640.0 20.3 %collective-permute-done.99 = bf16[256,1536]{1,0:T(8,128)(2,1)S(1)} collective-permute-done((bf16[256,1536]{1,0:T(8,128)(2,1)}, bf16[256,1536]{1,0:T(8,128)(2,1)S(1)}, u32[]{:S(2)}, u32[]{:S(2)}) %collective-permute-start.99) | collective-permute-done | bytes 786464 | tf_op jit(solution)/shard_map/ppermute | solution.py:68
  732.9 14.7 %shard_map.494 = (bf16[1024,512]{1,0:T(8,128)(2,1)S(1)}, f32[24,512]{1,0:T(8,128)S(1)}, f32[24,512]{1,0:T(8,128)S(1)}, f32[4,128,256]{2,1,0:T(8,128)S(1)}, f32[4,512]{1,0:T(4,128)S(1)}, /*index=5*/f32[1,512]{1,0:T(1,128)S(1)}) custom-call(f32[1024,512]{1,0:T(8,128)S(1)} %copy-done.12, f32[1024,512]{1,0:T(8,128)S(1)} %get-tuple-element.55.a_ref, ...), custom_call_target="tpu_custom_call" | custom-call | flops 629145600 | bytes 11534336 | tf_op jit(solution)/shard_map/pallas_call | solution.py:475
  762.9 9.8 collective-permute-start.109
  787.7 11.0 collective-permute-done.110
  841.2 12.5 multiply_convert_fusion.1
  853.7 9.4 convolution_convert_fusion.4
  864.7 10.4 convolution_convert_fusion.1
  878.0 10.9 collective-permute-done.190
  940.4 12.1 collective-permute-done.118
  992.7 14.7 %shard_map.496 = (bf16[1024,512]{1,0:T(8,128)(2,1)S(1)}, f32[24,512]{1,0:T(8,128)S(1)}, f32[24,512]{1,0:T(8,128)S(1)}, f32[4,128,256]{2,1,0:T(8,128)S(1)}, f32[4,512]{1,0:T(4,128)S(1)}, /*index=5*/f32[1,512]{1,0:T(1,128)S(1)}) custom-call(f32[1024,512]{1,0:T(8,128)S(1)} %get-tuple-element.71.dh_ref, f32[1024,512]{1,0:T(8,128)S(1)} %copy-done.1, ...), custom_call_target="tpu_custom_call" | custom-call | flops 629145600 | bytes 11534336 | tf_op jit(solution)/shard_map/pallas_call | solution.py:475
  1220.4 9.5 collective-permute-done.131
  1242.4 9.5 collective-permute-done.139
  (1210 shorter events, 828.0 us)
Async XLA Ops:
  1.3 45.7 %collective-permute-start.15 = (f32[2,128]{1,0:T(2,128)S(1)}, f32[2,128]{1,0:T(2,128)}, u32[]{:S(2)}, u32[]{:S(2)}) collective-permute-start(f32[2,128]{1,0:T(2,128)S(1)} %bitcast.910), channel_id=1, source_target_pairs={{0,2},{1,3},{2,0},{3,1},{4,6},{5,7},{6,4},{7,5},{8,10},{9,11},{10,... | collective-permute-start | bytes 3080 | tf_op jit(solution)/shard_map/ppermute | solution.py:68
  2.6 53.9 %collective-permute-start.14 = (f32[2,128]{1,0:T(2,128)S(1)}, f32[2,128]{1,0:T(2,128)}, u32[]{:S(2)}, u32[]{:S(2)}) collective-permute-start(f32[2,128]{1,0:T(2,128)S(1)} %bitcast.911), channel_id=1, source_target_pairs={{0,1},{1,0},{2,3},{3,2},{4,5},{5,4},{6,7},{7,6},{8,9},{9,8},{10,11... | collective-permute-start | bytes 3080 | tf_op jit(solution)/shard_map/ppermute | solution.py:68
  11.4 70.2 %collective-permute-start.36 = (bf16[48,2304]{1,0:T(8,128)(2,1)}, bf16[48,2304]{1,0:T(8,128)(2,1)}, u32[]{:S(2)}, u32[]{:S(2)}) collective-permute-start(bf16[48,2304]{1,0:T(8,128)(2,1)} %get-tuple-element.249), channel_id=1, source_target_pairs={{0,1},{1,0},{2,3},{3,2},{4,5},{5,4},{6,7},{7,6},{8,9},{9,8},{10,11... | collective-permute-start | bytes 663560 | tf_op jit(solution)/shard_map/ppermute | solution.py:68
  11.5 71.4 %collective-permute-start.37 = (bf16[48,2304]{1,0:T(8,128)(2,1)}, bf16[48,2304]{1,0:T(8,128)(2,1)}, u32[]{:S(2)}, u32[]{:S(2)}) collective-permute-start(bf16[48,2304]{1,0:T(8,128)(2,1)} %get-tuple-element.248), channel_id=1, source_target_pairs={{0,2},{1,3},{2,0},{3,1},{4,6},{5,7},{6,4},{7,5},{8,10},{9,11},{10,... | collective-permute-start | bytes 663560 | tf_op jit(solution)/shard_map/ppermute | solution.py:68
  16.2 47.5 %collective-permute-start.1 = (bf16[48,1152]{1,0:T(8,128)(2,1)}, bf16[48,1152]{1,0:T(8,128)(2,1)}, u32[]{:S(2)}, u32[]{:S(2)}) collective-permute-start(bf16[48,1152]{1,0:T(8,128)(2,1)} %get-tuple-element.280), channel_id=1, source_target_pairs={{0,2},{1,3},{2,0},{3,1},{4,6},{5,7},{6,4},{7,5},{8,10},{9,11},{10,... | collective-permute-start | bytes 331784 | tf_op jit(solution)/shard_map/ppermute | solution.py:68
  82.9 429.6 %collective-permute-start.95 = (bf16[256,1536]{1,0:T(8,128)(2,1)}, bf16[256,1536]{1,0:T(8,128)(2,1)}, u32[]{:S(2)}, u32[]{:S(2)}) collective-permute-start(bf16[256,1536]{1,0:T(8,128)(2,1)} %bitcast.153), channel_id=1, source_target_pairs={{0,2},{1,3},{2,0},{3,1},{4,6},{5,7},{6,4},{7,5},{8,10},{9,11},{10,... | collective-permute-start | bytes 2359304 | tf_op jit(solution)/shard_map/ppermute | solution.py:68
  146.9 45.8 %collective-permute-start.11 = (bf16[256,1536]{1,0:T(8,128)(2,1)S(1)}, bf16[256,1536]{1,0:T(8,128)(2,1)}, u32[]{:S(2)}, u32[]{:S(2)}) collective-permute-start(bf16[256,1536]{1,0:T(8,128)(2,1)S(1)} %fusion.34), channel_id=1, source_target_pairs={{0,2},{1,3},{2,0},{3,1},{4,6},{5,7},{6,4},{7,5},{8,10},{9,11},{10,... | collective-permute-start | bytes 2359304 | tf_op jit(solution)/shard_map/ppermute | solution.py:68
  148.6 49.2 %collective-permute-start.40 = (bf16[192,2304]{1,0:T(8,128)(2,1)S(1)}, bf16[192,2304]{1,0:T(8,128)(2,1)}, u32[]{:S(2)}, u32[]{:S(2)}) collective-permute-start(bf16[192,2304]{1,0:T(8,128)(2,1)S(1)} %bitcast.817), channel_id=1, source_target_pairs={{0,4},{4,12},{12,20},{20,28},{28,24},{24,16},{16,8},{8,0},{1,5},{5... | collective-permute-start | bytes 2654216 | tf_op jit(solution)/shard_map/ppermute | solution.py:120
  149.0 46.8 %collective-permute-start.28 = (bf16[208,1536]{1,0:T(8,128)(2,1)}, bf16[208,1536]{1,0:T(8,128)(2,1)}, u32[]{:S(2)}, u32[]{:S(2)}) collective-permute-start(bf16[208,1536]{1,0:T(8,128)(2,1)} %collective-permute-done.26), channel_id=1, source_target_pairs={{4,0},{12,4},{20,12},{28,20},{24,28},{16,24},{8,16},{0,8},{5,1},{1... | collective-permute-start | bytes 1916936 | tf_op jit(solution)/shard_map/ppermute | solution.py:120
  197.7 48.9 %collective-permute-start.29 = (bf16[208,1536]{1,0:T(8,128)(2,1)}, bf16[208,1536]{1,0:T(8,128)(2,1)}, u32[]{:S(2)}, u32[]{:S(2)}) collective-permute-start(bf16[208,1536]{1,0:T(8,128)(2,1)} %collective-permute-done.28), channel_id=1, source_target_pairs={{4,0},{12,4},{20,12},{28,20},{24,28},{16,24},{8,16},{0,8},{5,1},{1... | collective-permute-start | bytes 1916936 | tf_op jit(solution)/shard_map/ppermute | solution.py:120
  209.3 60.3 %collective-permute-start.42 = (bf16[192,2304]{1,0:T(8,128)(2,1)}, bf16[192,2304]{1,0:T(8,128)(2,1)}, u32[]{:S(2)}, u32[]{:S(2)}) collective-permute-start(bf16[192,2304]{1,0:T(8,128)(2,1)} %collective-permute-done.40), channel_id=1, source_target_pairs={{0,4},{4,12},{12,20},{20,28},{28,24},{24,16},{16,8},{8,0},{1,5},{5... | collective-permute-start | bytes 2654216 | tf_op jit(solution)/shard_map/ppermute | solution.py:120
  269.6 53.5 %collective-permute-start.30 = (bf16[256,1536]{1,0:T(8,128)(2,1)S(1)}, bf16[256,1536]{1,0:T(8,128)(2,1)S(1)}, u32[]{:S(2)}, u32[]{:S(2)}) collective-permute-start(bf16[256,1536]{1,0:T(8,128)(2,1)S(1)} %get-tuple-element.197), channel_id=1, source_target_pairs={{0,1},{1,0},{2,3},{3,2},{4,5},{5,4},{6,7},{7,6},{8,9},{9,8},{10,11... | collective-permute-start | bytes 2359304 | tf_op jit(solution)/shard_map/ppermute | solution.py:68
  321.4 43.1 %collective-permute-start.68 = (bf16[208,1536]{1,0:T(8,128)(2,1)S(1)}, bf16[208,1536]{1,0:T(8,128)(2,1)S(1)}, u32[]{:S(2)}, u32[]{:S(2)}) collective-permute-start(bf16[208,1536]{1,0:T(8,128)(2,1)S(1)} %copy-done.88), channel_id=1, source_target_pairs={{0,4},{4,12},{12,20},{20,28},{28,24},{24,16},{16,8},{8,0},{1,5},{5... | collective-permute-start | bytes 1916936 | tf_op jit(solution)/shard_map/ppermute | solution.py:122
  364.6 41.2 %collective-permute-start.58 = (bf16[192,1152]{1,0:T(8,128)(2,1)S(1)}, bf16[192,1152]{1,0:T(8,128)(2,1)S(1)}, u32[]{:S(2)}, u32[]{:S(2)}) collective-permute-start(bf16[192,1152]{1,0:T(8,128)(2,1)S(1)} %collective-permute-done.57), channel_id=1, source_target_pairs={{0,4},{4,12},{12,20},{20,28},{28,24},{24,16},{16,8},{8,0},{1,5},{5... | collective-permute-start | bytes 1327112 | tf_op jit(solution)/shard_map/ppermute | solution.py:120
  410.5 93.3 %collective-permute-start.84 = (bf16[192,2304]{1,0:T(8,128)(2,1)}, bf16[192,2304]{1,0:T(8,128)(2,1)}, u32[]{:S(2)}, u32[]{:S(2)}) collective-permute-start(bf16[192,2304]{1,0:T(8,128)(2,1)} %bitcast.814), channel_id=1, source_target_pairs={{4,0},{12,4},{20,12},{28,20},{24,28},{16,24},{8,16},{0,8},{5,1},{1... | collective-permute-start | bytes 2654216 | tf_op jit(solution)/shard_map/ppermute | solution.py:122
  448.7 56.0 %collective-permute-start.85 = (bf16[192,2304]{1,0:T(8,128)(2,1)S(1)}, bf16[192,2304]{1,0:T(8,128)(2,1)}, u32[]{:S(2)}, u32[]{:S(2)}) collective-permute-start(bf16[192,2304]{1,0:T(8,128)(2,1)S(1)} %bitcast.815), channel_id=1, source_target_pairs={{0,4},{4,12},{12,20},{20,28},{28,24},{24,16},{16,8},{8,0},{1,5},{5... | collective-permute-start | bytes 2654216 | tf_op jit(solution)/shard_map/ppermute | solution.py:120
  512.5 67.1 %collective-permute-start.94 = (bf16[256,1536]{1,0:T(8,128)(2,1)}, bf16[256,1536]{1,0:T(8,128)(2,1)}, u32[]{:S(2)}, u32[]{:S(2)}) collective-permute-start(bf16[256,1536]{1,0:T(8,128)(2,1)} %bitcast.153), channel_id=1, source_target_pairs={{0,1},{1,0},{2,3},{3,2},{4,5},{5,4},{6,7},{7,6},{8,9},{9,8},{10,11... | collective-permute-start | bytes 2359304 | tf_op jit(solution)/shard_map/ppermute | solution.py:68
  525.4 54.2 %collective-permute-start.96 = (bf16[256,1536]{1,0:T(8,128)(2,1)}, bf16[256,1536]{1,0:T(8,128)(2,1)}, u32[]{:S(2)}, u32[]{:S(2)}) collective-permute-start(bf16[256,1536]{1,0:T(8,128)(2,1)} %collective-permute-done.95), channel_id=1, source_target_pairs={{0,1},{1,0},{2,3},{3,2},{4,5},{5,4},{6,7},{7,6},{8,9},{9,8},{10,11... | collective-permute-start | bytes 2359304 | tf_op jit(solution)/shard_map/ppermute | solution.py:68
  603.6 57.4 %collective-permute-start.91 = (bf16[256,1536]{1,0:T(8,128)(2,1)}, bf16[256,1536]{1,0:T(8,128)(2,1)}, u32[]{:S(2)}, u32[]{:S(2)}) collective-permute-start(bf16[256,1536]{1,0:T(8,128)(2,1)} %get-tuple-element.191), channel_id=1, source_target_pairs={{0,1},{1,0},{2,3},{3,2},{4,5},{5,4},{6,7},{7,6},{8,9},{9,8},{10,11... | collective-permute-start | bytes 2359304 | tf_op jit(solution)/shard_map/ppermute | solution.py:68
  622.5 44.5 %collective-permute-start.196 = (bf16[144,1536]{1,0:T(8,128)(2,1)}, bf16[144,1536]{1,0:T(8,128)(2,1)}, u32[]{:S(2)}, u32[]{:S(2)}) collective-permute-start(bf16[144,1536]{1,0:T(8,128)(2,1)} %get-tuple-element.173), channel_id=1, source_target_pairs={{0,4},{4,12},{12,20},{20,28},{28,24},{24,16},{16,8},{8,0},{1,5},{5... | collective-permute-start | bytes 1327112 | tf_op jit(solution)/shard_map/ppermute | solution.py:139
  673.1 47.3 %collective-permute-start.183 = (bf16[192,2304]{1,0:T(8,128)(2,1)}, bf16[192,2304]{1,0:T(8,128)(2,1)}, u32[]{:S(2)}, u32[]{:S(2)}) collective-permute-start(bf16[192,2304]{1,0:T(8,128)(2,1)} %get-tuple-element.162), channel_id=1, source_target_pairs={{0,4},{4,12},{12,20},{20,28},{28,24},{24,16},{16,8},{8,0},{1,5},{5... | collective-permute-start | bytes 2654216 | tf_op jit(solution)/shard_map/ppermute | solution.py:143
  725.3 54.0 %collective-permute-start.181 = (bf16[192,2304]{1,0:T(8,128)(2,1)}, bf16[192,2304]{1,0:T(8,128)(2,1)}, u32[]{:S(2)}, u32[]{:S(2)}) collective-permute-start(bf16[192,2304]{1,0:T(8,128)(2,1)} %get-tuple-element.159), channel_id=1, source_target_pairs={{4,0},{12,4},{20,12},{28,20},{24,28},{16,24},{8,16},{0,8},{5,1},{1... | collective-permute-start | bytes 2654216 | tf_op jit(solution)/shard_map/ppermute | solution.py:139
  726.0 53.4 %collective-permute-start.184 = (bf16[192,2304]{1,0:T(8,128)(2,1)}, bf16[192,2304]{1,0:T(8,128)(2,1)}, u32[]{:S(2)}, u32[]{:S(2)}) collective-permute-start(bf16[192,2304]{1,0:T(8,128)(2,1)} %get-tuple-element.160), channel_id=1, source_target_pairs={{0,4},{4,12},{12,20},{20,28},{28,24},{24,16},{16,8},{8,0},{1,5},{5... | collective-permute-start | bytes 2654216 | tf_op jit(solution)/shard_map/ppermute | solution.py:143
  782.9 258.5 %collective-permute-start.182 = (bf16[192,2304]{1,0:T(8,128)(2,1)}, bf16[192,2304]{1,0:T(8,128)(2,1)}, u32[]{:S(2)}, u32[]{:S(2)}) collective-permute-start(bf16[192,2304]{1,0:T(8,128)(2,1)} %get-tuple-element.157), channel_id=1, source_target_pairs={{4,0},{12,4},{20,12},{28,20},{24,28},{16,24},{8,16},{0,8},{5,1},{1... | collective-permute-start | bytes 2654216 | tf_op jit(solution)/shard_map/ppermute | solution.py:139
  933.2 108.7 %collective-permute-start.185 = (bf16[192,2304]{1,0:T(8,128)(2,1)}, bf16[192,2304]{1,0:T(8,128)(2,1)}, u32[]{:S(2)}, u32[]{:S(2)}) collective-permute-start(bf16[192,2304]{1,0:T(8,128)(2,1)} %get-tuple-element.158), channel_id=1, source_target_pairs={{0,4},{4,12},{12,20},{20,28},{28,24},{24,16},{16,8},{8,0},{1,5},{5... | collective-permute-start | bytes 2654216 | tf_op jit(solution)/shard_map/ppermute | solution.py:143
  962.3 84.2 %collective-permute-start.172 = (bf16[192,2304]{1,0:T(8,128)(2,1)}, bf16[192,2304]{1,0:T(8,128)(2,1)}, u32[]{:S(2)}, u32[]{:S(2)}) collective-permute-start(bf16[192,2304]{1,0:T(8,128)(2,1)} %get-tuple-element.151), channel_id=1, source_target_pairs={{4,0},{12,4},{20,12},{28,20},{24,28},{16,24},{8,16},{0,8},{5,1},{1... | collective-permute-start | bytes 2654216 | tf_op jit(solution)/shard_map/ppermute | solution.py:139
  991.2 55.4 %collective-permute-start.175 = (bf16[192,2304]{1,0:T(8,128)(2,1)}, bf16[192,2304]{1,0:T(8,128)(2,1)}, u32[]{:S(2)}, u32[]{:S(2)}) collective-permute-start(bf16[192,2304]{1,0:T(8,128)(2,1)} %get-tuple-element.152), channel_id=1, source_target_pairs={{0,4},{4,12},{12,20},{20,28},{28,24},{24,16},{16,8},{8,0},{1,5},{5... | collective-permute-start | bytes 2654216 | tf_op jit(solution)/shard_map/ppermute | solution.py:143
  1038.3 157.1 %collective-permute-start.168 = (f32[64,1536]{1,0:T(8,128)}, f32[64,1536]{1,0:T(8,128)}, u32[]{:S(2)}, u32[]{:S(2)}) collective-permute-start(f32[64,1536]{1,0:T(8,128)} %fusion.127), channel_id=1, source_target_pairs={{0,0},{4,1},{1,2},{5,3},{2,4},{6,5},{3,6},{7,7},{8,8},{12,9},{9,10... | collective-permute-start | bytes 1179656 | tf_op jit(solution)/shard_map/ppermute | solution.py:195
  1041.8 165.6 %collective-permute-start.147 = (bf16[192,1152]{1,0:T(8,128)(2,1)}, bf16[192,1152]{1,0:T(8,128)(2,1)}, u32[]{:S(2)}, u32[]{:S(2)}) collective-permute-start(bf16[192,1152]{1,0:T(8,128)(2,1)} %get-tuple-element.178), channel_id=1, source_target_pairs={{4,0},{12,4},{20,12},{28,20},{24,28},{16,24},{8,16},{0,8},{5,1},{1... | collective-permute-start | bytes 1327112 | tf_op jit(solution)/shard_map/ppermute | solution.py:143
  1106.5 58.1 %collective-permute-start.126 = (bf16[256,1536]{1,0:T(8,128)(2,1)}, bf16[256,1536]{1,0:T(8,128)(2,1)}, u32[]{:S(2)}, u32[]{:S(2)}) collective-permute-start(bf16[256,1536]{1,0:T(8,128)(2,1)} %get-tuple-element.184), channel_id=1, source_target_pairs={{0,1},{1,0},{2,3},{3,2},{4,5},{5,4},{6,7},{7,6},{8,9},{9,8},{10,11... | collective-permute-start | bytes 2359304 | tf_op jit(solution)/shard_map/ppermute | solution.py:68
  1107.1 54.9 %collective-permute-start.156 = (bf16[64,1536]{1,0:T(8,128)(2,1)}, bf16[64,1536]{1,0:T(8,128)(2,1)}, u32[]{:S(2)}, u32[]{:S(2)}) collective-permute-start(bf16[64,1536]{1,0:T(8,128)(2,1)} %get-tuple-element.199), channel_id=1, source_target_pairs={{4,0},{12,4},{20,12},{28,20},{24,28},{16,24},{8,16},{0,8},{5,1},{1... | collective-permute-start | bytes 589832 | tf_op jit(solution)/shard_map/ppermute | solution.py:139
  1107.4 55.2 %collective-permute-start.159 = (bf16[64,1536]{1,0:T(8,128)(2,1)}, bf16[64,1536]{1,0:T(8,128)(2,1)}, u32[]{:S(2)}, u32[]{:S(2)}) collective-permute-start(bf16[64,1536]{1,0:T(8,128)(2,1)} %get-tuple-element.200), channel_id=1, source_target_pairs={{0,4},{4,12},{12,20},{20,28},{28,24},{24,16},{16,8},{8,0},{1,5},{5... | collective-permute-start | bytes 589832 | tf_op jit(solution)/shard_map/ppermute | solution.py:143
  (352 other events, 6104.0 us)

commit v2 on v1

--- a/solution.py
+++ b/solution.py
@@ -93,57 +93,124 @@
 def ring_tables():
     n = lax.axis_size("seq")
     order = [0, 1, 3, 5, 7, 6, 4, 2] if n == 8 else list(range(n))
-    place = [0] * n
-    for i, dev in enumerate(order):
-        place[dev] = i
     right = [(order[i], order[(i + 1) % n]) for i in range(n)]
     left = [(b, a) for a, b in right]
-    position = jnp.asarray(place, jnp.int32)[lax.axis_index("seq")]
-    table = jnp.asarray(order, jnp.int32)
-    device = lambda offset: table[lax.rem(position + offset + n, n)]
+    s = lax.axis_index("seq")
+    if n == 8:
+        position = jnp.where(s % 2 == 1, s // 2 + 1, (8 - s // 2) % 8)
+        owner = lambda p: jnp.where(p == 0, 0, jnp.where(p <= 4, 2 * p - 1, 16 - 2 * p))
+    else:
+        position, owner = s, lambda p: p
+    device = lambda offset: owner(lax.rem(position + offset + n, n))
     return n, right, left, device
 
 
-def ring_gather(block, flip, after=None):
-    n, right, left, device = ring_tables()
-    if flip:
-        right, left = left, right
-    sign = -1 if flip else 1
-    if after is not None:
-        block, _ = lax.optimization_barrier((block, after))
-    out = jnp.zeros((n,) + block.shape, block.dtype)
-    put = lambda o, b, k: lax.dynamic_update_index_in_dim(o, b, device(k), 0)
-    out = put(out, block, 0)
-    a = b = block
-    marks = []
-    for hop in range(1, n // 2 + 1):
-        a = lax.ppermute(a, "seq", right)
-        if hop <= n - 1 - n // 2:
-            b = lax.ppermute(b, "seq", left)
-            out = put(out, b, sign * hop)
-        out = put(out, a, -sign * hop)
-        marks.append(a)
-    return out, marks
-
-
-def ring_scatter(stack, flip):
-    n, right, left, device = ring_tables()
-    if flip:
-        right, left = left, right
-    sign = -1 if flip else 1
-    chunk = lambda k: lax.dynamic_index_in_dim(stack, device(sign * k), 0, keepdims=False)
-    add = lambda x, y: (x.astype(f32) + y.astype(f32)).astype(bf16)
-    far, near = n // 2, n - 1 - n // 2
-    a, b = chunk(far), chunk(-near)
-    for hop in range(1, far + 1):
-        a = lax.ppermute(a, "seq", right)
-        if hop < far:
-            a = add(a, chunk(far - hop))
-        if hop <= near:
-            b = lax.ppermute(b, "seq", left)
-            if hop < near:
-                b = add(b, chunk(hop - near))
-    return chunk(0).astype(f32) + a.astype(f32) + b.astype(f32)
+class GatherJob:
+    def __init__(self, block, flip, place):
+        self.n, right, left, self.device = ring_tables()
+        self.routes = (left, right) if flip else (right, left)
+        self.sign = -1 if flip else 1
+        self.a = self.b = block
+        self.hop, self.place = 0, place
+        self.place(block, self.device(0))
+        self.done = False
+
+    def start(self):
+        self.hop += 1
+        flight = [lax.ppermute(self.a, "seq", self.routes[0])]
+        if self.hop <= self.n - 1 - self.n // 2:
+            flight.append(lax.ppermute(self.b, "seq", self.routes[1]))
+        return flight
+
+    def bytes(self):
+        return self.a.size * 2
+
+    def receive(self, flight):
+        self.a = flight[0]
+        self.place(self.a, self.device(-self.sign * self.hop))
+        if len(flight) > 1:
+            self.b = flight[1]
+            self.place(self.b, self.device(self.sign * self.hop))
+        self.done = self.hop == self.n // 2
+
+
+class ScatterJob:
+    def __init__(self, stack, flip, finish):
+        self.n, right, left, self.device = ring_tables()
+        self.routes = (left, right) if flip else (right, left)
+        self.sign = -1 if flip else 1
+        self.stack, self.finish = stack, finish
+        self.far, self.near = self.n // 2, self.n - 1 - self.n // 2
+        self.a, self.b = self.chunk(self.far), self.chunk(-self.near)
+        self.hop, self.done = 0, False
+
+    def chunk(self, k):
+        return lax.dynamic_index_in_dim(self.stack, self.device(self.sign * k), 0, keepdims=False)
+
+    def bytes(self):
+        return self.a.size * 2
+
+    def start(self):
+        self.hop += 1
+        flight = [lax.ppermute(self.a, "seq", self.routes[0])]
+        if self.hop <= self.near:
+            flight.append(lax.ppermute(self.b, "seq", self.routes[1]))
+        return flight
+
+    def receive(self, flight):
+        add = lambda x, y: (x.astype(f32) + y.astype(f32)).astype(bf16)
+        self.a = flight[0]
+        if self.hop < self.far:
+            self.a = add(self.a, self.chunk(self.far - self.hop))
+        if len(flight) > 1:
+            self.b = flight[1]
+            if self.hop < self.near:
+                self.b = add(self.b, self.chunk(self.hop - self.near))
+        if self.hop == self.far:
+            self.done = True
+            self.finish(self.chunk(0).astype(f32) + self.a.astype(f32) + self.b.astype(f32))
+
+
+def tie(*values):
+    return lax.optimization_barrier(values)
+
+
+def run(job):
+    while not job.done:
+        job.receive(job.start())
+
+
+class Pump:
+    def __init__(self):
+        self.waiting, self.active = [], []
+
+    def add(self, *jobs):
+        self.waiting += jobs
+
+    def step(self, value):
+        flights = [flight for _, flight in self.active]
+        heads = [(job.a, job.b) for job in self.waiting]
+        if flights or heads:
+            value, flights, heads = lax.optimization_barrier((value, flights, heads))
+        moved = []
+        for (job, _), flight in zip(self.active, flights):
+            job.receive(flight)
+            if not job.done:
+                moved.append(job)
+        for job, (a, b) in zip(self.waiting, heads):
+            job.a, job.b = a, b
+            moved.append(job)
+        self.waiting = []
+        self.active = [(job, job.start()) for job in moved]
+        return value
+
+    def finish(self):
+        for job, flight in self.active:
+            job.receive(flight)
+            run(job)
+        for job in self.waiting:
+            run(job)
+        self.active, self.waiting = [], []
 
 
 def shift_seq(x, distance):
@@ -499,12 +566,6 @@
     return block.reshape(rows, groups, TP, HEAD_W).transpose(2, 0, 1, 3).reshape(TP, rows, width // TP)
 
 
-def ff_columns(block):
-    rows, width = block.shape
-    n = lax.axis_size("seq")
-    return block.reshape(rows, n, TP, width // (n * TP)).transpose(2, 0, 1, 3).reshape(TP, rows, width // TP)
-
-
 def head_columns_back(pieces):
     groups = pieces[0].shape[1] // HEAD_W
     rows = pieces[0].shape[0]
@@ -512,129 +573,215 @@
     return stack.reshape(rows, -1)
 
 
+def ff_back_kernel(n, pieces_ref, gate_ref, up_ref):
+    part = gate_ref.shape[1] // (n * TP)
+    half = n * part
+    for w in range(TP):
+        for s in range(n):
+            to = (s * TP + w) * part
+            gate_ref[:, to : to + part] = pieces_ref[w, :, s * part : (s + 1) * part].astype(f32)
+            up_ref[:, to : to + part] = pieces_ref[w, :, half + s * part : half + (s + 1) * part].astype(f32)
+
+
 def ff_columns_back(pieces):
     n = lax.axis_size("seq")
-    rows, width = pieces[0].shape
-    stack = jnp.stack([p.reshape(rows, n, width // n) for p in pieces], axis=2)
-    return stack.reshape(rows, -1)
-
-
-def send_weights(shards, after):
-    (mix_gain, proj_gelu, proj_stream, conv_taps, lru_gates, decay_param, proj_out, mlp_gain, proj_gate, proj_up, proj_down) = shards
-    rp = proj_gelu.shape[0]
-    gr = lru_gates.shape[0] // TP
-    small = jnp.concatenate([mix_gain, mlp_gain, conv_taps.reshape(-1), decay_param])
-    top = jnp.pad(small, (0, (rp - gr) * HEAD_W - small.shape[0])).reshape(rp - gr, HEAD_W)
-    extra = jnp.concatenate([top, jnp.zeros((gr, HEAD_W), bf16)])
-    pieces = jnp.concatenate(
-        [head_columns(proj_gelu), head_columns(proj_stream), jnp.broadcast_to(extra, (TP, rp, HEAD_W))], axis=2
-    )
-    got = jnp.stack(wt_exchange(pieces))
-    gates = to_heads(lru_gates).reshape(TP, gr, HEAD_W)
-    width = got.shape[2] - HEAD_W
-    got = lax.dynamic_update_slice(got, gates, (0, rp - gr, width))
-    first, marks1 = ring_gather(got.reshape(TP * rp, width + HEAD_W), False, after)
-    rows = jnp.concatenate([proj_down, to_heads(proj_out)])
-    second, marks2 = ring_gather(rows, True, marks1[1])
-    wide = jnp.concatenate([ff_columns(proj_gate), ff_columns(proj_up)], axis=2)
-    wide = jnp.stack(wt_exchange(wide)).reshape(TP * rp, -1)
-    third, marks3 = ring_gather(wide, False, marks2[1])
-    return (first, second, third), marks3[1]
-
-
-def open_weights(gathered, sizes):
-    first, second, third = gathered
-    rp, gr, cp, fb = sizes
-    w = lax.axis_index("wt")
-    n = first.shape[0]
-    depth = n * TP * rp
-    width = first.shape[2] - HEAD_W
-    flat = first.reshape(depth, width + HEAD_W)
-    extra = flat[:, width:].reshape(n * TP, rp, HEAD_W)
-    small = extra[:, : rp - gr].reshape(n * TP, -1)
-    mix_gain = small[:, :rp].reshape(-1).astype(f32)
-    mlp_gain = small[:, rp : 2 * rp].reshape(-1).astype(f32)
-    at = 2 * rp
-
-    def own_heads(v):
-        v = v.reshape(v.shape[0], -1, TP, HEAD_W)
-        return lax.dynamic_index_in_dim(v, w, 2, keepdims=False).reshape(v.shape[0], -1).astype(f32)
-
-    taps = own_heads(small[:, at : at + CONV * cp].reshape(n * TP, CONV, cp).transpose(1, 0, 2).reshape(CONV, -1))
-    decay = own_heads(small[:, at + CONV * cp : at + (CONV + 1) * cp].reshape(1, -1))
-    gates = extra[:, rp - gr :].reshape(2, -1, HEAD_W, HEAD_W).transpose(1, 2, 0, 3)
-    gates = gates.reshape(-1, HEAD_W, 2 * HEAD_W)
-    return dict(
-        gelu=flat[:, : width // 2], stream=flat[:, width // 2 : width],
-        mix_gain=mix_gain, mlp_gain=mlp_gain, taps=taps, gates=gates,
-        decay=-DECAY * jax.nn.softplus(decay), slope=-DECAY * jax.nn.sigmoid(decay),
-        down=second[:, :fb].reshape(n * fb, -1), out=second[:, fb:].reshape(-1, second.shape[2]),
-        wide=third.reshape(depth, -1),
-    )
-
-
-def forward_block(x, keep, streams, wts):
+    _, rows, width = pieces.shape
+    out = jax.ShapeDtypeStruct((rows, TP * width // 2), f32)
+    return pl.pallas_call(
+        functools.partial(ff_back_kernel, n), out_shape=[out, out],
+        compiler_params=pltpu.CompilerParams(vmem_limit_bytes=24 * 2**20),
+        cost_estimate=pl.CostEstimate(flops=rows * width * 8, bytes_accessed=rows * width * 40, transcendentals=0),
+    )(pieces)
+
+
+def ff_kernel(n, gate_ref, up_ref, out_ref):
+    part = gate_ref.shape[1] // (n * TP)
+    half = n * part
+    for w in range(TP):
+        for s in range(n):
+            at = (s * TP + w) * part
+            out_ref[w, :, s * part : (s + 1) * part] = gate_ref[:, at : at + part]
+            out_ref[w, :, half + s * part : half + (s + 1) * part] = up_ref[:, at : at + part]
+
+
+def ff_columns(gate, up):
+    rows, width = gate.shape
+    return pl.pallas_call(
+        functools.partial(ff_kernel, lax.axis_size("seq")),
+        out_shape=jax.ShapeDtypeStruct((TP, rows, 2 * width // TP), bf16),
+        compiler_params=pltpu.CompilerParams(vmem_limit_bytes=24 * 2**20),
+        cost_estimate=pl.CostEstimate(flops=rows * width * 8, bytes_accessed=rows * width * 8, transcendentals=0),
+    )(gate, up)
+
+
+class Weights:
+    def __init__(self, shards, layer):
+        self.shards = [s[layer] for s in shards]
+        self.buffers = {}
+        self.flip = bool(layer % 2)
+
+    def slot(self, name, shape):
+        n = lax.axis_size("seq")
+        if name not in self.buffers:
+            self.buffers[name] = jnp.zeros((n,) + shape, bf16)
+
+    def put(self, name, block, at, column=0):
+        self.buffers[name] = lax.dynamic_update_slice(self.buffers[name], block[None], (at, 0, column))
+
+    def prepare_first(self):
+        (mix_gain, proj_gelu, proj_stream, conv_taps, lru_gates, decay_param, _, mlp_gain, _, _, _) = self.shards
+        rp = proj_gelu.shape[0]
+        gr = lru_gates.shape[0] // TP
+        small = jnp.concatenate([mix_gain, mlp_gain, conv_taps.reshape(-1), decay_param])
+        top = jnp.pad(small, (0, (rp - gr) * HEAD_W - small.shape[0])).reshape(rp - gr, HEAD_W)
+        extra = jnp.concatenate([top, jnp.zeros((gr, HEAD_W), bf16)])
+        pieces = jnp.concatenate(
+            [head_columns(proj_gelu), head_columns(proj_stream), jnp.broadcast_to(extra, (TP, rp, HEAD_W))], axis=2
+        )
+        got = jnp.stack(wt_exchange(pieces))
+        gates = to_heads(lru_gates).reshape(TP, gr, HEAD_W)
+        width = got.shape[2] - HEAD_W
+        self.first_block = lax.dynamic_update_slice(got, gates, (0, rp - gr, width)).reshape(TP * rp, width + HEAD_W)
+        return self.first_block
+
+    def prepare_out(self):
+        self.out_block = to_heads(self.shards[6])
+
+    def prepare_wide(self):
+        proj_gate, proj_up = self.shards[8], self.shards[9]
+        wide = jnp.stack(wt_exchange(ff_columns(proj_gate, proj_up)))
+        self.wide_block = wide.reshape(TP * proj_gate.shape[0], -1)
+
+    def first_job(self):
+        self.slot("first", self.first_block.shape)
+        return GatherJob(self.first_block, self.flip, lambda block, at: self.put("first", block, at))
+
+    def out_job(self):
+        self.slot("out", self.out_block.shape)
+        return GatherJob(self.out_block, not self.flip, lambda block, at: self.put("out", block, at))
+
+    def gather_down(self):
+        self.down = lax.all_gather(self.shards[10], "seq", tiled=True)
+
+    def gather_wide(self):
+        self.wide = lax.all_gather(self.wide_block, "seq", tiled=True)
+
+    def open_first(self, sizes):
+        rp, gr, cp, fb = sizes
+        first = self.buffers["first"]
+        w = lax.axis_index("wt")
+        n = first.shape[0]
+        depth = n * TP * rp
+        width = first.shape[2] - HEAD_W
+        flat = first.reshape(depth, width + HEAD_W)
+        extra = flat[:, width:].reshape(n * TP, rp, HEAD_W)
+        small = extra[:, : rp - gr].reshape(n * TP, -1)
+        at = 2 * rp
+
+        def own_heads(v):
+            v = v.reshape(v.shape[0], -1, TP, HEAD_W)
+            return lax.dynamic_index_in_dim(v, w, 2, keepdims=False).reshape(v.shape[0], -1).astype(f32)
+
+        self.taps = own_heads(small[:, at : at + CONV * cp].reshape(n * TP, CONV, cp).transpose(1, 0, 2).reshape(CONV, -1))
+        decay = own_heads(small[:, at + CONV * cp : at + (CONV + 1) * cp].reshape(1, -1))
+        gates = extra[:, rp - gr :].reshape(2, -1, HEAD_W, HEAD_W).transpose(1, 2, 0, 3)
+        self.gates = gates.reshape(-1, HEAD_W, 2 * HEAD_W)
+        self.mix_gain = small[:, :rp].reshape(-1).astype(f32)
+        self.mlp_gain = small[:, rp : 2 * rp].reshape(-1).astype(f32)
+        self.decay, self.slope = -DECAY * jax.nn.softplus(decay), -DECAY * jax.nn.sigmoid(decay)
+        self.gelu, self.stream = flat[:, : width // 2], flat[:, width // 2 : width]
+
+
+def forward_block(x, normed, keep, streams, wts, pump, following):
     width = x.shape[1]
-    normed = tp_gather(rms_norm(x, wts["mix_gain"]).astype(bf16))
+    if normed is None:
+        normed = tp_gather(rms_norm(x, wts.mix_gain).astype(bf16))
     tokens = normed.shape[0] // streams
     last = normed.reshape(streams, tokens, width)[:, tokens - REACH :].transpose(1, 0, 2)
     halo_in = shift_seq(last.reshape(REACH * streams, width), 1)
-    stream = dot(normed, wts["stream"], bf16)
-    branch = dot(normed, wts["gelu"])
-    halo = dot(halo_in, wts["stream"], bf16).astype(f32)
-    a, driven, conv, ends = mix(streams, stream, halo, keep, wts["taps"], wts["decay"], wts["gates"])
+    stream = dot(normed, wts.stream, bf16)
+    halo = dot(halo_in, wts.stream, bf16).astype(f32)
+    a, driven, conv, ends = mix(streams, stream, halo, keep, wts.taps, wts.decay, wts.gates)
+    branch = dot(normed, wts.gelu)
     start = carry_in(ends[0], ends[1], 1)
     h, merged = states(streams, a, driven, start, branch)
-    x1 = x + tp_scatter(dot(merged, wts["out"], bf16).reshape(TP, -1, width))
-    mlp_in = tp_gather(rms_norm(x1, wts["mlp_gain"]).astype(bf16))
-    wide = dot(mlp_in, wts["wide"])
+    wts.out = wts.buffers["out"].reshape(-1, width)
+    if following is not None:
+        pump.add(following.first_job(), following.out_job())
+        merged = pump.step(merged)
+    mixed = tp_scatter(dot(merged, wts.out, bf16).reshape(TP, -1, width))
+    mixed, wts.wide = tie(mixed, wts.wide)
+    mixed = pump.step(mixed)
+    x1 = x + mixed
+    mlp_in = tp_gather(rms_norm(x1, wts.mlp_gain).astype(bf16))
+    mlp_in = pump.step(mlp_in)
+    wide = pump.step(dot(mlp_in, wts.wide))
     half = wide.shape[1] // 2
     product = (gelu(wide[:, :half]) * wide[:, half:]).astype(bf16)
-    x2 = x1 + tp_scatter(dot(product, wts["down"], bf16).reshape(TP, -1, width))
     kept = dict(
         x=x, normed=normed, stream=stream, branch=branch, halo=halo, a=a, conv=conv, whole=ends[0], start=start, h=h,
         merged=merged, x1=x1, mlp_in=mlp_in, wide=wide, product=product,
     )
-    return x2, kept
-
-
-def mlp_back(gx, g_down, wts, kept):
+    return kept
+
+
+def block_end(kept, wts):
+    product = kept["product"]
+    width = kept["x1"].shape[1]
+    return kept["x1"] + tp_scatter(dot(product, wts.down, bf16).reshape(TP, -1, width))
+
+
+def mlp_back(gx, g_down, wts, kept, results, rp, pump, above):
     width = gx.shape[1]
     n = lax.axis_size("seq")
     grad_down = dot_tokens(kept["product"], g_down)
-    d_product = dot_t(g_down, wts["down"])
+    g_down, grad_down = tie(g_down, grad_down)
+    d_product = dot_t(g_down, wts.down)
     wide = kept["wide"]
     half = wide.shape[1] // 2
     value, slope = gelu_and_slope(wide[:, :half])
     d_wide = jnp.concatenate([(d_product * wide[:, half:] * slope).astype(bf16), (d_product * value).astype(bf16)], axis=1)
-    grad_wide = dot_tokens(kept["mlp_in"], d_wide)
-    d_mlp_in = tp_scatter(dot_t(d_wide, wts["wide"], bf16).reshape(TP, -1, width))
-    dv, d_gain = rms_norm_back(kept["x1"], wts["mlp_gain"], d_mlp_in)
-    down = ring_scatter(grad_down.reshape(n, -1, width), False)
-    wide = ring_scatter(grad_wide.reshape(n, -1, grad_wide.shape[1]), True)
-    return gx + dv, d_gain, down, wide
-
-
-def mixer_back(d_x1, keep, streams, wts, kept, d_mlp_gain, d_mix_gain, sizes):
+    grad_wide = dot_tokens(kept["mlp_in"], d_wide).reshape(n, -1, 2 * half)
+    d_wide, grad_wide, grad_down = tie(d_wide, grad_wide, grad_down)
+    if above is not None:
+        d_wide, above["wide"] = tie(d_wide, above["wide"])
+    part = dot_t(d_wide, wts.wide, bf16).reshape(TP, -1, width)
+    d_mlp_in = tp_scatter(pump.step(part))
+    d_mlp_in = pump.step(d_mlp_in)
+    results["wide"] = lax.psum_scatter(grad_wide, "seq", scatter_dimension=0)
+    if above is not None:
+        d_mlp_in, grad_down = tie(d_mlp_in, grad_down)
+    results["down"] = lax.psum_scatter(grad_down.reshape(n, -1, width), "seq", scatter_dimension=0).astype(f32)
+    dv, d_gain = rms_norm_back(kept["x1"], wts.mlp_gain, d_mlp_in)
+    return gx + dv, d_gain
+
+
+def mixer_back(d_x1, keep, streams, wts, kept, d_mlp_gain, d_mix_gain, sizes, results, above, pump, end=None):
     rp, gr, cp, fb = sizes
     width = d_x1.shape[1]
     n, w = lax.axis_size("seq"), lax.axis_index("wt")
-    g_branch = tp_gather(d_x1.astype(bf16))
-    d_merged = dot_t(g_branch, wts["out"])
+    g_branch = pump.step(tp_gather(d_x1.astype(bf16)))
+    d_merged = dot_t(g_branch, wts.out)
     grad_out = dot_tokens(kept["merged"], g_branch)
+    if end is not None:
+        pump.add(ScatterJob(grad_out.reshape(n, -1, width), True, lambda total: results.update(out=from_heads(total))))
     dh, d_branch, ends = states_back(streams, d_merged, kept["branch"], kept["a"], kept["h"])
+    if end is not None:
+        ends = end(ends)
+    ends = pump.step(ends)
     back = carry_in(kept["whole"], ends, -1)
+    back = pump.step(back)
     d_stream, tail, head, d_gates, d_taps, d_decay = mix_back(
         streams, dh, kept["a"], kept["h"], kept["start"], back, kept["conv"], kept["stream"], kept["halo"], keep,
-        wts["taps"], wts["decay"], wts["slope"], wts["gates"],
+        wts.taps, wts.decay, wts.slope, wts.gates,
     )
+    d_stream, head = pump.step((d_stream, head))
     tail = (tail + shift_seq(head, -1)).astype(bf16)
     tokens = d_stream.shape[0] // streams
     d_stream = lax.dynamic_update_slice(
         d_stream.reshape(streams, tokens, -1), tail.reshape(REACH, streams, -1).transpose(1, 0, 2), (0, tokens - REACH, 0)
     ).reshape(d_stream.shape)
-    both = jnp.concatenate([d_branch, d_stream], axis=1)
-    grad_both = dot_tokens(kept["normed"], both)
+    part = (dot_t(d_branch, wts.gelu) + dot_t(d_stream, wts.stream)).astype(bf16).reshape(TP, -1, width)
 
     def full(v):
         lines = v.reshape(v.shape[0], -1, 1, HEAD_W)
@@ -651,87 +798,116 @@
     small = jnp.pad(small, ((0, 0), (0, (rp - gr) * HEAD_W - used))).reshape(n * TP, rp - gr, HEAD_W)
     gates = d_gates.reshape(-1, HEAD_W, 2, HEAD_W).transpose(2, 0, 1, 3).reshape(n * TP, gr, HEAD_W).astype(bf16)
     extra = jnp.concatenate([small, gates], axis=1).reshape(n, TP * rp, HEAD_W)
-    both_sum = ring_scatter(
-        jnp.concatenate([grad_both.reshape(n, TP * rp, -1), extra], axis=2), False
-    )
-    out = from_heads(ring_scatter(grad_out.reshape(n, -1, width), True))
-    d_normed = tp_scatter(
-        (dot_t(d_branch, wts["gelu"]) + dot_t(d_stream, wts["stream"])).astype(bf16).reshape(TP, -1, width)
-    )
-    dv, d_gain = rms_norm_back(kept["x"], wts["mix_gain"], d_normed)
-    return d_x1 + dv, d_gain, both_sum, out, used
-
-
-def finish_wide(wide, rp):
-    pieces = wt_exchange(wide.astype(bf16).reshape(TP, rp, -1))
-    half = wide.shape[1] // 2
-    return (
-        ff_columns_back([p[:, :half] for p in pieces]).astype(f32),
-        ff_columns_back([p[:, half:] for p in pieces]).astype(f32),
-    )
-
-
-def finish_both(both, sizes, used):
-    rp, gr, cp, fb = sizes
-    width = both.shape[1] - HEAD_W
-    stack = both.reshape(TP, rp, -1)
-    gates = from_heads(stack[:, rp - gr :, width:].reshape(TP * gr, HEAD_W))
-    pieces = wt_exchange(both.astype(bf16).reshape(TP, rp, -1))
-    half = width // 2
-    gelu_part = head_columns_back([p[:, :half] for p in pieces]).astype(f32)
-    stream_part = head_columns_back([p[:, half:width] for p in pieces]).astype(f32)
-    small = sum(p[: rp - gr, width:].astype(f32) for p in pieces).reshape(-1)[:used]
-    d_mix, d_mlp = small[:rp], small[rp : 2 * rp]
-    d_taps = small[2 * rp : 2 * rp + CONV * cp].reshape(CONV, cp)
-    d_decay = small[2 * rp + CONV * cp :]
-    return gelu_part, stream_part, gates, d_mix, d_mlp, d_taps, d_decay
+    grad_gelu = dot_tokens(kept["normed"], d_branch).reshape(n, TP * rp, -1)
+    grad_stream = dot_tokens(kept["normed"], d_stream).reshape(n, TP * rp, -1)
+    half = grad_gelu.shape[2]
+
+    def finish(both):
+        stack = both.reshape(TP, rp, -1)
+        results["gates"] = from_heads(stack[:, rp - gr :, 2 * half :].reshape(TP * gr, HEAD_W))
+        pieces = wt_exchange(both.astype(bf16).reshape(TP, rp, -1))
+        results["gelu"] = head_columns_back([p[:, :half] for p in pieces]).astype(f32)
+        results["stream"] = head_columns_back([p[:, half : 2 * half] for p in pieces]).astype(f32)
+        sums = sum(p[: rp - gr, 2 * half :].astype(f32) for p in pieces).reshape(-1)[:used]
+        above["mix_gain"], results["mlp_gain"] = sums[:rp], sums[rp : 2 * rp]
+        results["taps"] = sums[2 * rp : 2 * rp + CONV * cp].reshape(CONV, cp)
+        results["decay"] = sums[2 * rp + CONV * cp :]
+
+    if end is None:
+        part, grad_out, results["wide"] = tie(part, grad_out, results["wide"])
+        run(ScatterJob(grad_out.reshape(n, -1, width), True, lambda total: results.update(out=from_heads(total))))
+    run(ScatterJob(jnp.concatenate([grad_gelu, grad_stream, extra], axis=2), False, finish))
+    d_normed = pump.step(tp_scatter(part))
+    dv, d_gain = rms_norm_back(kept["x"], wts.mix_gain, d_normed)
+    return d_x1 + dv, d_gain
 
 
 def per_device(block_in, start_flags, out_grad, *shards):
     layers = shards[0].shape[0]
-    n = lax.axis_size("seq")
     micro, _, tokens, width = block_in.shape
     streams = micro * TP
-    lead = REACH * streams
     sizes = (shards[1].shape[1], shards[4].shape[1] // TP, shards[5].shape[1], shards[10].shape[1])
     rp = sizes[0]
 
-    gathered, mark = [], None
-    for layer in range(layers):
-        sent, mark = send_weights([s[layer] for s in shards], mark)
-        gathered.append(sent)
-
+    weights = [Weights(shards, layer) for layer in range(layers)]
+    zero, pump = weights[0], Pump()
+    zero.prepare_first()
+    zero.prepare_out()
+    pump.add(zero.first_job(), zero.out_job())
+    rest = [w.shards for w in weights]
+    block_in, start_flags, out_grad, rest = pump.step((block_in, start_flags, out_grad, rest))
+    for w, shards_then in zip(weights, rest):
+        w.shards = shards_then
     flags = tp_gather(start_flags[:, 0].astype(f32))
+    x_in = block_in[:, 0].reshape(micro * tokens, width)
+    grad = out_grad[:, 0].reshape(micro * tokens, width)
+    x_all = tp_gather(x_in)
     keep = 1.0 - flags.T
     behind = 1.0 - shift_seq(flags[:, tokens - REACH :].T, 1)
     keep = jnp.concatenate([behind, keep, jnp.ones((REACH, streams), f32)]).reshape(-1, 1)
     keep = jnp.broadcast_to(keep, (keep.shape[0], HEAD_W))
 
-    x = block_in[:, 0].astype(f32).reshape(micro * tokens, width)
-    grad = out_grad[:, 0].reshape(micro * tokens, width)
-    wts, kept = [], []
+    x = x_in.astype(f32)
+    kept = []
+    zero.prepare_wide()
+    for _ in range(3):
+        zero.wide_block = pump.step(zero.wide_block)
+    zero.wide_block, x_all, rest = pump.step((zero.wide_block, x_all, [w.shards for w in weights]))
+    pump.finish()
+    zero.gather_wide()
+    for w, shards_then in zip(weights, rest):
+        w.shards = shards_then
+    zero.gather_down()
+    for wts in weights[1:]:
+        wts.prepare_first()
+        wts.prepare_out()
+        wts.prepare_wide()
+        wts.gather_wide()
+        wts.gather_down()
     for layer in range(layers):
-        wts.append(open_weights(gathered[layer], sizes))
-        x, saved = forward_block(x, keep, streams, wts[layer])
+        wts = weights[layer]
+        wts.open_first(sizes)
+        normed = rms_norm(x_all.astype(f32), wts.mix_gain).astype(bf16) if layer == 0 else None
+        following = weights[layer + 1] if layer < layers - 1 else None
+        saved = forward_block(x, normed, keep, streams, wts, pump, following)
+        if layer < layers - 1:
+            x = pump.step(block_end(saved, wts))
+            pump.finish()
         kept.append(saved)
+        if layer == 0:
+            grad_then, saved["wide"] = tie(grad, saved["wide"])
+            g_down = tp_gather(grad_then)
 
     gx = grad.astype(f32)
     d_mix = jnp.zeros((width,), f32)
-    results = [None] * layers
+    results = [dict() for _ in range(layers)]
+    spare, outcome = {}, []
+
+    def last(ends):
+        ends, kept[-1]["product"] = tie(ends, kept[-1]["product"])
+        outcome.append(block_end(kept[-1], weights[-1]))
+        return ends
+
     for layer in reversed(range(layers)):
-        g_down = tp_gather(gx.astype(bf16))
-        d_x1, d_mlp, down, wide = mlp_back(gx, g_down, wts[layer], kept[layer])
-        gate_part, up_part = finish_wide(wide, rp)
-        gx, d_mix_next, both, out, used = mixer_back(d_x1, keep, streams, wts[layer], kept[layer], d_mlp, d_mix, sizes)
-        gelu_part, stream_part, gates, mix_part, mlp_part, taps, decay = finish_both(both, sizes, used)
         if layer != layers - 1:
-            results[layer + 1][0] = mix_part
-        results[layer] = [None, gelu_part, stream_part, taps, gates, decay, out, mlp_part, gate_part, up_part, down]
-        d_mix = d_mix_next
-    results[0][0] = vector_scatter(d_mix.reshape(n, TP, rp))
+            g_down = pump.step(tp_gather(gx.astype(bf16)))
+            g_down, results[layer + 1]["down"] = tie(g_down, results[layer + 1]["down"])
+        d_x1, d_mlp = mlp_back(
+            gx, g_down, weights[layer], kept[layer], results[layer], rp, pump, results[layer + 1] if layer < layers - 1 else None
+        )
+        above = spare if layer == layers - 1 else results[layer + 1]
+        gx, d_mix = mixer_back(
+            d_x1, keep, streams, weights[layer], kept[layer], d_mlp, d_mix, sizes, results[layer], above, pump, last if layer == layers - 1 else None
+        )
+    pump.finish()
+    for found in results:
+        pieces = wt_exchange(found.pop("wide").reshape(TP, rp, -1))
+        found["gate"], found["up"] = ff_columns_back(jnp.stack(pieces))
+    results[0]["mix_gain"] = vector_scatter(d_mix.reshape(-1, TP, rp))
     shape = (micro, 1, tokens, width)
-    stacked = [jnp.stack([results[layer][k] for layer in range(layers)]) for k in range(11)]
-    return (x.astype(bf16).reshape(shape), gx.astype(bf16).reshape(shape), *stacked)
+    names = ("mix_gain", "gelu", "stream", "taps", "gates", "decay", "out", "mlp_gain", "gate", "up", "down")
+    stacked = [jnp.stack([results[layer][k] for layer in range(layers)]) for k in names]
+    return (outcome[0].astype(bf16).reshape(shape), gx.astype(bf16).reshape(shape), *stacked)
 
 
 def solution(mesh):

time: 1290 us -> 1130 us (0.88)
  local copies, waits for them, and re-layouts: 170 us -> 93.4 us
  waiting for transfers between devices: 473 us -> 423 us
  starting transfers between devices: 266 us -> 238 us
  matrix products: 160 us -> 186 us
  other arithmetic: 114 us -> 93.2 us
    ppermute x98 -> x56, waiting for transfers between devices: 307 us -> 157 us  [the longest x32 119 us: start(): flight = [lax.ppermute(self.a, 'seq', self.routes[0])]]
    ppermute x77, waiting for transfers between devices: 105 us -> 247 us  [swap(): return lax.ppermute(x, 'wt', [(i, i ^ k) for i in range(TP)])]
    another operation x37 -> x6, local copies, waits for them, and re-layouts: 49 us -> 4.74 us  [the longest x20 35.7 us: ff_columns_back(): stack = jnp.stack([p.reshape(rows, n, width // n) for p in pieces], axis=2)]
    convert_element_type x37 -> x26, other arithmetic: 46.7 us -> 21.1 us  [the longest x12 5.63 us: receive(): add = lambda x, y: (x.astype(f32) + y.astype(f32)).astype(bf16)]
    ppermute x77, starting transfers between devices: 119 us -> 94.5 us  [swap(): return lax.ppermute(x, 'wt', [(i, i ^ k) for i in range(TP)])]
    ppermute x21, waiting for transfers between devices: 33.5 us -> 15.4 us  [shift_seq(): lax.ppermute(x, 'seq', [(i, i + distance) for i in range(n) if 0 <= i + d...]
    slice x40 -> x25, local copies, waits for them, and re-layouts: 22.9 us -> 6.58 us  [the longest x3 3.9 us: __init__(): self.shards = [s[layer] for s in shards]]
    convert_element_type x12 -> x8, local copies, waits for them, and re-layouts: 14.4 us -> 0.81 us  [the longest x2 0.26 us: finish(): head_columns_back([p[:, half:2 * half] for p in pieces]).astype(f32)]
  transfers between devices with their start and end apart: 203 -> 169, of which waited for: 70 -> 73; matrix products, arithmetic and copies ran while one was open for 31% -> 29% of each run, Pallas kernels for 5% -> 6%
where the time goes in v2:
time: 1130 us; the launch traced here: 1120 us
  waiting for transfers between devices  423 us (37%)
  starting transfers between devices  238 us (21%)
  matrix products  186 us (16%)
  local copies, waits for them, and re-layouts  93.4 us (8%)
  other arithmetic  93.2 us (8%)
  Pallas kernels  65.4 us (6%)
  between operations  18.5 us (2%)
    ppermute x77, waiting for transfers between devices, swap(): return lax.ppermute(x, 'wt', [(i, i ^ k) for i in range(TP)])  247 us
    ppermute x32, waiting for transfers between devices, start(): flight = [lax.ppermute(self.a, 'seq', self.routes[0])]  119 us
    ppermute x77, starting transfers between devices, swap(): return lax.ppermute(x, 'wt', [(i, i ^ k) for i in range(TP)])  94.5 us
    dot_general x10, matrix products, dot_t(): lax.dot_general(left, right, (((1,), (1,)), ((), ())), preferred_element_...  73.8 us
    dot_general x10, matrix products, dot_tokens(): lax.dot_general(left, right, (((0,), (0,)), ((), ())), preferred_element_...  58.8 us
    dot_general x12, matrix products, dot(): lax.dot_general(left, right, (((1,), (0,)), ((), ())), preferred_element_...  53.5 us
    ppermute x21, starting transfers between devices, shift_seq(): lax.ppermute(x, 'seq', [(i, i + distance) for i in range(n) if 0 <= i + d...  52.8 us
    ppermute x32, starting transfers between devices, start(): flight = [lax.ppermute(self.a, 'seq', self.routes[0])]  44.4 us
  transfers between devices with their start and end apart: 169, of which 73 were waited for; matrix products, arithmetic and copies ran while one was open for 29% of the time, Pallas kernels for 6%

profile of v2, /device:TPU:3, one launch (start us, length us, event | category | flops | bytes accessed | tf_op | source)
XLA Modules:
  0.0 1117.7 jit_solution(9016920276256008860)
XLA Ops:
  50.7 8.8 collective-permute-done.20
  70.0 12.0 %collective-permute-done.17 = bf16[64,1536]{1,0:T(8,128)(2,1)S(1)} collective-permute-done((bf16[64,1536]{1,0:T(8,128)(2,1)S(1)}, bf16[64,1536]{1,0:T(8,128)(2,1)S(1)}, u32[]{:S(2)}, u32[]{:S(2)}) %collective-permute-start.17) | collective-permute-done | bytes 196640 | tf_op jit(solution)/shard_map/ppermute | solution.py:120
  161.4 8.8 shard_map.238
  210.6 16.6 %collective-permute-done.39 = bf16[256,1536]{1,0:T(8,128)(2,1)} collective-permute-done((bf16[256,1536]{1,0:T(8,128)(2,1)S(1)}, bf16[256,1536]{1,0:T(8,128)(2,1)}, u32[]{:S(2)}, u32[]{:S(2)}) %collective-permute-start.39) | collective-permute-done | bytes 786464 | tf_op jit(solution)/shard_map/ppermute | solution.py:68
  239.1 10.2 collective-permute-done.45
  254.5 10.5 collective-permute-done.50
  275.7 16.0 %collective-permute-done.53 = bf16[64,1536]{1,0:T(8,128)(2,1)S(1)} collective-permute-done((bf16[64,1536]{1,0:T(8,128)(2,1)S(1)}, bf16[64,1536]{1,0:T(8,128)(2,1)S(1)}, u32[]{:S(2)}, u32[]{:S(2)}) %collective-permute-start.53) | collective-permute-done | bytes 196640 | tf_op jit(solution)/shard_map/ppermute | solution.py:120
  291.7 10.1 collective-permute-done.54
  318.9 15.1 %collective-permute-done.57 = bf16[256,1536]{1,0:T(8,128)(2,1)S(1)} collective-permute-done((bf16[256,1536]{1,0:T(8,128)(2,1)S(1)}, bf16[256,1536]{1,0:T(8,128)(2,1)S(1)}, u32[]{:S(2)}, u32[]{:S(2)}) %collective-permute-start.57) | collective-permute-done | bytes 786464 | tf_op jit(solution)/shard_map/ppermute | solution.py:68
  334.4 11.9 %collective-permute-done.58 = bf16[192,1152]{1,0:T(8,128)(2,1)S(1)} collective-permute-done((bf16[192,1152]{1,0:T(8,128)(2,1)S(1)}, bf16[192,1152]{1,0:T(8,128)(2,1)S(1)}, u32[]{:S(2)}, u32[]{:S(2)}) %collective-permute-start.58) | collective-permute-done | bytes 442400 | tf_op jit(solution)/shard_map/ppermute | solution.py:120
  354.1 14.7 %collective-permute-done.61 = bf16[256,1536]{1,0:T(8,128)(2,1)} collective-permute-done((bf16[256,1536]{1,0:T(8,128)(2,1)}, bf16[256,1536]{1,0:T(8,128)(2,1)}, u32[]{:S(2)}, u32[]{:S(2)}) %collective-permute-start.61) | collective-permute-done | bytes 786464 | tf_op jit(solution)/shard_map/ppermute | solution.py:68
  384.9 8.9 shard_map.240
  431.6 17.4 %collective-permute-done.70 = bf16[256,1536]{1,0:T(8,128)(2,1)} collective-permute-done((bf16[256,1536]{1,0:T(8,128)(2,1)}, bf16[256,1536]{1,0:T(8,128)(2,1)}, u32[]{:S(2)}, u32[]{:S(2)}) %collective-permute-start.70) | collective-permute-done | bytes 786464 | tf_op jit(solution)/shard_map/ppermute | solution.py:68
  467.8 14.8 %collective-permute-done.78 = bf16[256,1536]{1,0:T(8,128)(2,1)S(1)} collective-permute-done((bf16[256,1536]{1,0:T(8,128)(2,1)S(1)}, bf16[256,1536]{1,0:T(8,128)(2,1)S(1)}, u32[]{:S(2)}, u32[]{:S(2)}) %collective-permute-start.78) | collective-permute-done | bytes 786464 | tf_op jit(solution)/shard_map/ppermute | solution.py:68
  505.4 11.1 multiply_convert_fusion.3
  519.8 9.9 convolution_convert_fusion.1
  529.7 11.6 %convolution_convert_fusion.5 = bf16[1024,1536]{1,0:T(8,128)(2,1)S(1)} fusion(bf16[1024,2304]{1,0:T(8,128)(2,1)} %pad_maximum_fusion, bf16[1536,2304]{1,0:T(8,128)(2,1)} %all-gather.9.cloned.1.call-done), kind=kOutput, calls=%fused_computation.34 | convolution fusion | flops 7249330176 | bytes 14942208 | tf_op jit(solution)/shard_map/dot_general | solution.py:27
  544.9 18.0 %collective-permute-done.82 = bf16[256,1536]{1,0:T(8,128)(2,1)S(1)} collective-permute-done((bf16[256,1536]{1,0:T(8,128)(2,1)S(1)}, bf16[256,1536]{1,0:T(8,128)(2,1)S(1)}, u32[]{:S(2)}, u32[]{:S(2)}) %collective-permute-start.82) | collective-permute-done | bytes 786464 | tf_op jit(solution)/shard_map/ppermute | solution.py:68
  567.9 16.0 %collective-permute-done.84 = bf16[256,1536]{1,0:T(8,128)(2,1)} collective-permute-done((bf16[256,1536]{1,0:T(8,128)(2,1)}, bf16[256,1536]{1,0:T(8,128)(2,1)}, u32[]{:S(2)}, u32[]{:S(2)}) %collective-permute-start.84) | collective-permute-done | bytes 786464 | tf_op jit(solution)/shard_map/ppermute | solution.py:68
  620.4 14.7 %shard_map.244 = (bf16[1024,512]{1,0:T(8,128)(2,1)S(1)}, f32[24,512]{1,0:T(8,128)S(1)}, f32[24,512]{1,0:T(8,128)S(1)}, f32[4,128,256]{2,1,0:T(8,128)S(1)}, f32[4,512]{1,0:T(4,128)S(1)}, /*index=5*/f32[1,512]{1,0:T(1,128)S(1)}) custom-call(f32[1024,512]{1,0:T(8,128)S(1)} %get-tuple-element.259.dh_ref, f32[1024,512]{1,0:T(8,128)S(1)} %get-tuple-element.239.a_ref, ...), custom_call_target="tpu_custom_call" | custom-call | flops 629145600 | bytes 11534336 | tf_op jit(solution)/shard_map/pallas_call | solution.py:542
  660.8 15.0 %collective-permute-done.100 = bf16[256,1536]{1,0:T(8,128)(2,1)S(1)} collective-permute-done((bf16[256,1536]{1,0:T(8,128)(2,1)S(1)}, bf16[256,1536]{1,0:T(8,128)(2,1)S(1)}, u32[]{:S(2)}, u32[]{:S(2)}) %collective-permute-start.100) | collective-permute-done | bytes 786464 | tf_op jit(solution)/shard_map/ppermute | solution.py:68
  680.7 15.3 %collective-permute-done.104 = bf16[256,1536]{1,0:T(8,128)(2,1)S(1)} collective-permute-done((bf16[256,1536]{1,0:T(8,128)(2,1)S(1)}, bf16[256,1536]{1,0:T(8,128)(2,1)S(1)}, u32[]{:S(2)}, u32[]{:S(2)}) %collective-permute-start.104) | collective-permute-done | bytes 786464 | tf_op jit(solution)/shard_map/ppermute | solution.py:68
  710.1 8.4 convolution_convert_fusion.2
  728.6 10.0 convolution_convert_fusion
  752.5 11.5 %convolution_convert_fusion.4 = bf16[1024,1536]{1,0:T(8,128)(2,1)S(1)} fusion(bf16[1024,2304]{1,0:T(8,128)(2,1)} %pad_maximum_fusion.1, bf16[1536,2304]{1,0:T(8,128)(2,1)} %all-gather.5.cloned.1.call-done), kind=kOutput, calls=%fused_computation.33 | convolution fusion | flops 7249330176 | bytes 14942208 | tf_op jit(solution)/shard_map/dot_general | solution.py:27
  784.3 8.4 collective-permute-done.88
  795.9 13.7 %collective-permute-done.109 = bf16[256,1536]{1,0:T(8,128)(2,1)} collective-permute-done((bf16[256,1536]{1,0:T(8,128)(2,1)}, bf16[256,1536]{1,0:T(8,128)(2,1)}, u32[]{:S(2)}, u32[]{:S(2)}) %collective-permute-start.109) | collective-permute-done | bytes 786464 | tf_op jit(solution)/shard_map/ppermute | solution.py:68
  824.1 9.4 collective-permute-done.111
  880.2 15.4 %shard_map.246 = (bf16[1024,512]{1,0:T(8,128)(2,1)S(1)}, f32[24,512]{1,0:T(8,128)S(1)}, f32[24,512]{1,0:T(8,128)}, f32[4,128,256]{2,1,0:T(8,128)S(1)}, f32[4,512]{1,0:T(4,128)S(1)}, /*index=5*/f32[1,512]{1,0:T(1,128)S(1)}) custom-call(f32[1024,512]{1,0:T(8,128)S(1)} %get-tuple-element.290.dh_ref, f32[1024,512]{1,0:T(8,128)S(1)} %copy-done.1, ...), custom_call_target="tpu_custom_call" | custom-call | flops 629145600 | bytes 11534336 | tf_op jit(solution)/shard_map/pallas_call | solution.py:542
  930.5 12.4 %collective-permute-done.126 = bf16[192,1152]{1,0:T(8,128)(2,1)S(1)} collective-permute-done((bf16[192,1152]{1,0:T(8,128)(2,1)S(1)}, bf16[192,1152]{1,0:T(8,128)(2,1)S(1)}, u32[]{:S(2)}, u32[]{:S(2)}) %collective-permute-start.126) | collective-permute-done | bytes 442400 | tf_op jit(solution)/shard_map/ppermute | solution.py:155
  979.9 8.5 collective-permute-done.128
  1074.2 10.9 collective-permute-done.120
  (1057 shorter events, 703.0 us)
Async XLA Ops:
  7.2 221.9 %all-gather.5.cloned.1.call-start = ((), (), s32[]{:S(2)}) async-start(), calls=%async_computation.4 | async-start | bytes 7962624 | tf_op jit(solution)/shard_map/all_gather | solution.py:667
  49.0 39.8 %collective-permute-start.19 = (bf16[256,1536]{1,0:T(8,128)(2,1)S(1)}, bf16[256,1536]{1,0:T(8,128)(2,1)S(1)}, u32[]{:S(2)}, u32[]{:S(2)}) collective-permute-start(bf16[256,1536]{1,0:T(8,128)(2,1)S(1)} %bitcast.614), channel_id=1, source_target_pairs={{0,1},{1,0},{2,3},{3,2},{4,5},{5,4},{6,7},{7,6},{8,9},{9,8},{10,11... | collective-permute-start | bytes 2359304 | tf_op jit(solution)/shard_map/ppermute | solution.py:68
  59.4 29.3 %collective-permute-start.21 = (bf16[256,1536]{1,0:T(8,128)(2,1)S(1)}, bf16[256,1536]{1,0:T(8,128)(2,1)S(1)}, u32[]{:S(2)}, u32[]{:S(2)}) collective-permute-start(bf16[256,1536]{1,0:T(8,128)(2,1)S(1)} %collective-permute-done.20), channel_id=1, source_target_pairs={{0,1},{1,0},{2,3},{3,2},{4,5},{5,4},{6,7},{7,6},{8,9},{9,8},{10,11... | collective-permute-start | bytes 2359304 | tf_op jit(solution)/shard_map/ppermute | solution.py:68
  96.3 208.2 %all-gather.7.cloned.1.call-start = ((), (), s32[]{:S(2)}) async-start(), calls=%async_computation.5 | async-start | bytes 3981312 | tf_op jit(solution)/shard_map/all_gather | solution.py:664
  134.2 49.0 %collective-permute-start.33 = (bf16[48,1152]{1,0:T(8,128)(2,1)}, bf16[48,1152]{1,0:T(8,128)(2,1)}, u32[]{:S(2)}, u32[]{:S(2)}) collective-permute-start(bf16[48,1152]{1,0:T(8,128)(2,1)} %get-tuple-element.481), channel_id=1, source_target_pairs={{0,1},{1,0},{2,3},{3,2},{4,5},{5,4},{6,7},{7,6},{8,9},{9,8},{10,11... | collective-permute-start | bytes 331784 | tf_op jit(solution)/shard_map/ppermute | solution.py:68
  135.0 49.5 %collective-permute-start.34 = (bf16[48,1152]{1,0:T(8,128)(2,1)}, bf16[48,1152]{1,0:T(8,128)(2,1)}, u32[]{:S(2)}, u32[]{:S(2)}) collective-permute-start(bf16[48,1152]{1,0:T(8,128)(2,1)} %get-tuple-element.480), channel_id=1, source_target_pairs={{0,2},{1,3},{2,0},{3,1},{4,6},{5,7},{6,4},{7,5},{8,10},{9,11},{10,... | collective-permute-start | bytes 331784 | tf_op jit(solution)/shard_map/ppermute | solution.py:68
  135.2 49.4 %collective-permute-start.35 = (bf16[48,1152]{1,0:T(8,128)(2,1)}, bf16[48,1152]{1,0:T(8,128)(2,1)}, u32[]{:S(2)}, u32[]{:S(2)}) collective-permute-start(bf16[48,1152]{1,0:T(8,128)(2,1)} %get-tuple-element.479), channel_id=1, source_target_pairs={{0,3},{1,2},{2,1},{3,0},{4,7},{5,6},{6,5},{7,4},{8,11},{9,10},{10,... | collective-permute-start | bytes 331784 | tf_op jit(solution)/shard_map/ppermute | solution.py:68
  156.8 295.1 %all-gather.9.cloned.1.call-start = ((), (), s32[]{:S(2)}) async-start(), calls=%async_computation.6 | async-start | bytes 7962624 | tf_op jit(solution)/shard_map/all_gather | solution.py:667
  210.5 294.9 %all-gather.11.cloned.1.call-start = ((), (), s32[]{:S(2)}) async-start(), calls=%async_computation.7 | async-start | bytes 3981312 | tf_op jit(solution)/shard_map/all_gather | solution.py:664
  233.2 31.7 %collective-permute-start.47 = (bf16[192,1152]{1,0:T(8,128)(2,1)}, bf16[192,1152]{1,0:T(8,128)(2,1)S(1)}, u32[]{:S(2)}, u32[]{:S(2)}) collective-permute-start(bf16[192,1152]{1,0:T(8,128)(2,1)} %collective-permute-done.40), channel_id=1, source_target_pairs={{4,0},{12,4},{20,12},{28,20},{24,28},{16,24},{8,16},{0,8},{5,1},{1... | collective-permute-start | bytes 1327112 | tf_op jit(solution)/shard_map/ppermute | solution.py:120
  233.2 31.7 %collective-permute-start.48 = (bf16[192,1152]{1,0:T(8,128)(2,1)}, bf16[192,1152]{1,0:T(8,128)(2,1)S(1)}, u32[]{:S(2)}, u32[]{:S(2)}) collective-permute-start(bf16[192,1152]{1,0:T(8,128)(2,1)} %collective-permute-done.41), channel_id=1, source_target_pairs={{0,4},{4,12},{12,20},{20,28},{28,24},{24,16},{16,8},{8,0},{1,5},{5... | collective-permute-start | bytes 1327112 | tf_op jit(solution)/shard_map/ppermute | solution.py:122
  265.0 36.8 %collective-permute-start.51 = (bf16[192,1152]{1,0:T(8,128)(2,1)S(1)}, bf16[192,1152]{1,0:T(8,128)(2,1)S(1)}, u32[]{:S(2)}, u32[]{:S(2)}) collective-permute-start(bf16[192,1152]{1,0:T(8,128)(2,1)S(1)} %collective-permute-done.47), channel_id=1, source_target_pairs={{4,0},{12,4},{20,12},{28,20},{24,28},{16,24},{8,16},{0,8},{5,1},{1... | collective-permute-start | bytes 1327112 | tf_op jit(solution)/shard_map/ppermute | solution.py:120
  265.1 36.7 %collective-permute-start.52 = (bf16[192,1152]{1,0:T(8,128)(2,1)S(1)}, bf16[192,1152]{1,0:T(8,128)(2,1)S(1)}, u32[]{:S(2)}, u32[]{:S(2)}) collective-permute-start(bf16[192,1152]{1,0:T(8,128)(2,1)S(1)} %collective-permute-done.48), channel_id=1, source_target_pairs={{0,4},{4,12},{12,20},{20,28},{28,24},{24,16},{16,8},{8,0},{1,5},{5... | collective-permute-start | bytes 1327112 | tf_op jit(solution)/shard_map/ppermute | solution.py:122
  266.5 35.2 %collective-permute-start.54 = (bf16[64,1536]{1,0:T(8,128)(2,1)S(1)}, bf16[64,1536]{1,0:T(8,128)(2,1)S(1)}, u32[]{:S(2)}, u32[]{:S(2)}) collective-permute-start(bf16[64,1536]{1,0:T(8,128)(2,1)S(1)} %collective-permute-done.50), channel_id=1, source_target_pairs={{4,0},{12,4},{20,12},{28,20},{24,28},{16,24},{8,16},{0,8},{5,1},{1... | collective-permute-start | bytes 589832 | tf_op jit(solution)/shard_map/ppermute | solution.py:122
  314.1 32.2 %collective-permute-start.58 = (bf16[192,1152]{1,0:T(8,128)(2,1)S(1)}, bf16[192,1152]{1,0:T(8,128)(2,1)S(1)}, u32[]{:S(2)}, u32[]{:S(2)}) collective-permute-start(bf16[192,1152]{1,0:T(8,128)(2,1)S(1)} %collective-permute-done.51), channel_id=1, source_target_pairs={{4,0},{12,4},{20,12},{28,20},{24,28},{16,24},{8,16},{0,8},{5,1},{1... | collective-permute-start | bytes 1327112 | tf_op jit(solution)/shard_map/ppermute | solution.py:120
  430.7 277.2 %reduce-scatter.5.cloned.1.call-start = ((), (), s32[]{:S(2)}) async-start(), calls=%async_computation.8 | async-start | bytes 3981312 | tf_op jit(solution)/shard_map/reduce_scatter | solution.py:754
  430.8 35.0 %collective-permute-start.75 = (bf16[256,1536]{1,0:T(8,128)(2,1)}, bf16[256,1536]{1,0:T(8,128)(2,1)}, u32[]{:S(2)}, u32[]{:S(2)}) collective-permute-start(bf16[256,1536]{1,0:T(8,128)(2,1)} %bitcast.631), channel_id=1, source_target_pairs={{0,2},{1,3},{2,0},{3,1},{4,6},{5,7},{6,4},{7,5},{8,10},{9,11},{10,... | collective-permute-start | bytes 2359304 | tf_op jit(solution)/shard_map/ppermute | solution.py:68
  455.4 28.4 %collective-permute-start.74 = (bf16[256,1536]{1,0:T(8,128)(2,1)S(1)}, bf16[256,1536]{1,0:T(8,128)(2,1)S(1)}, u32[]{:S(2)}, u32[]{:S(2)}) collective-permute-start(bf16[256,1536]{1,0:T(8,128)(2,1)S(1)} %bitcast.632), channel_id=1, source_target_pairs={{0,1},{1,0},{2,3},{3,2},{4,5},{5,4},{6,7},{7,6},{8,9},{9,8},{10,11... | collective-permute-start | bytes 2359304 | tf_op jit(solution)/shard_map/ppermute | solution.py:68
  529.7 222.9 %reduce-scatter.7.cloned.1.call-start = ((), (), s32[]{:S(2)}) async-start(), calls=%async_computation.9 | async-start | bytes 7962624 | tf_op jit(solution)/shard_map/reduce_scatter | solution.py:751
  586.0 449.4 %reduce-scatter.9.cloned.1.call-start = ((), (), s32[]{:S(2)}) async-start(), calls=%async_computation.10 | async-start | bytes 7962624 | tf_op jit(solution)/shard_map/reduce_scatter | solution.py:751
  738.7 365.3 %reduce-scatter.11.cloned.1.call-start = ((), (), s32[]{:S(2)}) async-start(), calls=%async_computation.11 | async-start | bytes 3981312 | tf_op jit(solution)/shard_map/reduce_scatter | solution.py:754
  752.3 32.0 %collective-permute-start.86 = (bf16[256,1536]{1,0:T(8,128)(2,1)}, bf16[256,1536]{1,0:T(8,128)(2,1)S(1)}, u32[]{:S(2)}, u32[]{:S(2)}) collective-permute-start(bf16[256,1536]{1,0:T(8,128)(2,1)} %get-tuple-element.398), channel_id=1, source_target_pairs={{0,1},{1,0},{2,3},{3,2},{4,5},{5,4},{6,7},{7,6},{8,9},{9,8},{10,11... | collective-permute-start | bytes 2359304 | tf_op jit(solution)/shard_map/ppermute | solution.py:68
  779.0 30.5 %collective-permute-start.109 = (bf16[256,1536]{1,0:T(8,128)(2,1)}, bf16[256,1536]{1,0:T(8,128)(2,1)}, u32[]{:S(2)}, u32[]{:S(2)}) collective-permute-start(bf16[256,1536]{1,0:T(8,128)(2,1)} %add_convert_fusion.2), channel_id=1, source_target_pairs={{0,2},{1,3},{2,0},{3,1},{4,6},{5,7},{6,4},{7,5},{8,10},{9,11},{10,... | collective-permute-start | bytes 2359304 | tf_op jit(solution)/shard_map/ppermute | solution.py:68
  817.4 29.6 %collective-permute-start.160 = (bf16[48,2304]{1,0:T(8,128)(2,1)S(1)}, bf16[48,2304]{1,0:T(8,128)(2,1)S(1)}, u32[]{:S(2)}, u32[]{:S(2)}) collective-permute-start(bf16[48,2304]{1,0:T(8,128)(2,1)S(1)} %get-tuple-element.433), channel_id=1, source_target_pairs={{0,3},{1,2},{2,1},{3,0},{4,7},{5,6},{6,5},{7,4},{8,11},{9,10},{10,... | collective-permute-start | bytes 663560 | tf_op jit(solution)/shard_map/ppermute | solution.py:68
  820.6 274.7 %collective-permute-start.154 = (f32[64,1536]{1,0:T(8,128)}, f32[64,1536]{1,0:T(8,128)}, u32[]{:S(2)}, u32[]{:S(2)}) collective-permute-start(f32[64,1536]{1,0:T(8,128)} %fusion.67), channel_id=1, source_target_pairs={{0,0},{4,1},{1,2},{5,3},{2,4},{6,5},{3,6},{7,7},{8,8},{12,9},{9,10... | collective-permute-start | bytes 1179656 | tf_op jit(solution)/shard_map/ppermute | solution.py:262
  906.0 42.0 %collective-permute-start.140 = (bf16[192,1152]{1,0:T(8,128)(2,1)}, bf16[192,1152]{1,0:T(8,128)(2,1)}, u32[]{:S(2)}, u32[]{:S(2)}) collective-permute-start(bf16[192,1152]{1,0:T(8,128)(2,1)} %get-tuple-element.385), channel_id=1, source_target_pairs={{4,0},{12,4},{20,12},{28,20},{24,28},{16,24},{8,16},{0,8},{5,1},{1... | collective-permute-start | bytes 1327112 | tf_op jit(solution)/shard_map/ppermute | solution.py:157
  913.9 29.0 %collective-permute-start.126 = (bf16[192,1152]{1,0:T(8,128)(2,1)S(1)}, bf16[192,1152]{1,0:T(8,128)(2,1)S(1)}, u32[]{:S(2)}, u32[]{:S(2)}) collective-permute-start(bf16[192,1152]{1,0:T(8,128)(2,1)S(1)} %get-tuple-element.390), channel_id=1, source_target_pairs={{0,4},{4,12},{12,20},{20,28},{28,24},{24,16},{16,8},{8,0},{1,5},{5... | collective-permute-start | bytes 1327112 | tf_op jit(solution)/shard_map/ppermute | solution.py:155
  914.6 47.1 %collective-permute-start.130 = (bf16[192,1152]{1,0:T(8,128)(2,1)S(1)}, bf16[192,1152]{1,0:T(8,128)(2,1)S(1)}, u32[]{:S(2)}, u32[]{:S(2)}) collective-permute-start(bf16[192,1152]{1,0:T(8,128)(2,1)S(1)} %get-tuple-element.391), channel_id=1, source_target_pairs={{4,0},{12,4},{20,12},{28,20},{24,28},{16,24},{8,16},{0,8},{5,1},{1... | collective-permute-start | bytes 1327112 | tf_op jit(solution)/shard_map/ppermute | solution.py:157
  925.2 31.0 %collective-permute-start.137 = (bf16[192,1152]{1,0:T(8,128)(2,1)S(1)}, bf16[192,1152]{1,0:T(8,128)(2,1)S(1)}, u32[]{:S(2)}, u32[]{:S(2)}) collective-permute-start(bf16[192,1152]{1,0:T(8,128)(2,1)S(1)} %fusion.56), channel_id=1, source_target_pairs={{0,4},{4,12},{12,20},{20,28},{28,24},{24,16},{16,8},{8,0},{1,5},{5... | collective-permute-start | bytes 1327112 | tf_op jit(solution)/shard_map/ppermute | solution.py:155
  975.6 31.7 %collective-permute-start.139 = (bf16[192,1152]{1,0:T(8,128)(2,1)S(1)}, bf16[192,1152]{1,0:T(8,128)(2,1)S(1)}, u32[]{:S(2)}, u32[]{:S(2)}) collective-permute-start(bf16[192,1152]{1,0:T(8,128)(2,1)S(1)} %get-tuple-element.380), channel_id=1, source_target_pairs={{0,4},{4,12},{12,20},{20,28},{28,24},{24,16},{16,8},{8,0},{1,5},{5... | collective-permute-start | bytes 1327112 | tf_op jit(solution)/shard_map/ppermute | solution.py:155
  977.6 29.7 %collective-permute-start.142 = (bf16[192,1152]{1,0:T(8,128)(2,1)S(1)}, bf16[192,1152]{1,0:T(8,128)(2,1)S(1)}, u32[]{:S(2)}, u32[]{:S(2)}) collective-permute-start(bf16[192,1152]{1,0:T(8,128)(2,1)S(1)} %get-tuple-element.381), channel_id=1, source_target_pairs={{4,0},{12,4},{20,12},{28,20},{24,28},{16,24},{8,16},{0,8},{5,1},{1... | collective-permute-start | bytes 1327112 | tf_op jit(solution)/shard_map/ppermute | solution.py:157
  988.6 29.2 %collective-permute-start.129 = (bf16[192,1152]{1,0:T(8,128)(2,1)S(1)}, bf16[192,1152]{1,0:T(8,128)(2,1)S(1)}, u32[]{:S(2)}, u32[]{:S(2)}) collective-permute-start(bf16[192,1152]{1,0:T(8,128)(2,1)S(1)} %get-tuple-element.386), channel_id=1, source_target_pairs={{0,4},{4,12},{12,20},{20,28},{28,24},{24,16},{16,8},{8,0},{1,5},{5... | collective-permute-start | bytes 1327112 | tf_op jit(solution)/shard_map/ppermute | solution.py:155
  (307 other events, 3754.7 us)
Sparse Core Ops, SparseCore 0:
  96.4 119.3 all-gather.4
  218.0 81.6 all-gather.6
  301.9 120.9 all-gather.8
  430.9 63.5 all-gather.10
  529.8 78.5 reduce-scatter.4
  611.9 140.6 reduce-scatter.6
  756.7 133.0 reduce-scatter.8
  893.4 117.0 reduce-scatter.10

commit v3 on v2

--- a/solution.py
+++ b/solution.py
@@ -186,6 +186,17 @@
 
     def add(self, *jobs):
         self.waiting += jobs
+
+    def hold(self, value):
+        flights = [flight for _, flight in self.active]
+        if flights:
+            value, flights = lax.optimization_barrier((value, flights))
+        for (job, _), flight in zip(self.active, flights):
+            job.receive(flight)
+            if not job.done:
+                self.waiting.append(job)
+        self.active = []
+        return value
 
     def step(self, value):
         flights = [flight for _, flight in self.active]
@@ -203,6 +214,15 @@
         self.waiting = []
         self.active = [(job, job.start()) for job in moved]
         return value
+
+    def complete(self, jobs):
+        for job, flight in self.active:
+            if job in jobs:
+                job.receive(flight)
+        self.active = [(job, flight) for job, flight in self.active if job not in jobs]
+        self.waiting = [job for job in self.waiting if job not in jobs]
+        for job in jobs:
+            run(job)
 
     def finish(self):
         for job, flight in self.active:
@@ -566,11 +586,24 @@
     return block.reshape(rows, groups, TP, HEAD_W).transpose(2, 0, 1, 3).reshape(TP, rows, width // TP)
 
 
+def head_back_kernel(groups, pieces_ref, gelu_ref, stream_ref):
+    half = groups * HEAD_W
+    for w in range(TP):
+        for g in range(groups):
+            to = (g * TP + w) * HEAD_W
+            gelu_ref[:, to : to + HEAD_W] = pieces_ref[w, :, g * HEAD_W : (g + 1) * HEAD_W].astype(f32)
+            stream_ref[:, to : to + HEAD_W] = pieces_ref[w, :, half + g * HEAD_W : half + (g + 1) * HEAD_W].astype(f32)
+
+
 def head_columns_back(pieces):
-    groups = pieces[0].shape[1] // HEAD_W
-    rows = pieces[0].shape[0]
-    stack = jnp.stack([p.reshape(rows, groups, HEAD_W) for p in pieces], axis=2)
-    return stack.reshape(rows, -1)
+    _, rows, width = pieces.shape
+    groups = (width - HEAD_W) // (2 * HEAD_W)
+    out = jax.ShapeDtypeStruct((rows, TP * groups * HEAD_W), f32)
+    return pl.pallas_call(
+        functools.partial(head_back_kernel, groups), out_shape=[out, out],
+        compiler_params=pltpu.CompilerParams(vmem_limit_bytes=24 * 2**20),
+        cost_estimate=pl.CostEstimate(flops=rows * width * 8, bytes_accessed=rows * width * 40, transcendentals=0),
+    )(pieces)
 
 
 def ff_back_kernel(n, pieces_ref, gate_ref, up_ref):
@@ -747,7 +780,6 @@
         d_wide, above["wide"] = tie(d_wide, above["wide"])
     part = dot_t(d_wide, wts.wide, bf16).reshape(TP, -1, width)
     d_mlp_in = tp_scatter(pump.step(part))
-    d_mlp_in = pump.step(d_mlp_in)
     results["wide"] = lax.psum_scatter(grad_wide, "seq", scatter_dimension=0)
     if above is not None:
         d_mlp_in, grad_down = tie(d_mlp_in, grad_down)
@@ -756,26 +788,23 @@
     return gx + dv, d_gain
 
 
-def mixer_back(d_x1, keep, streams, wts, kept, d_mlp_gain, d_mix_gain, sizes, results, above, pump, end=None):
+def mixer_back(d_x1, keep, streams, wts, kept, d_mlp_gain, d_mix_gain, sizes, results, pump, end=None):
     rp, gr, cp, fb = sizes
     width = d_x1.shape[1]
     n, w = lax.axis_size("seq"), lax.axis_index("wt")
-    g_branch = pump.step(tp_gather(d_x1.astype(bf16)))
+    g_branch = tp_gather(d_x1.astype(bf16))
     d_merged = dot_t(g_branch, wts.out)
     grad_out = dot_tokens(kept["merged"], g_branch)
-    if end is not None:
-        pump.add(ScatterJob(grad_out.reshape(n, -1, width), True, lambda total: results.update(out=from_heads(total))))
     dh, d_branch, ends = states_back(streams, d_merged, kept["branch"], kept["a"], kept["h"])
     if end is not None:
         ends = end(ends)
-    ends = pump.step(ends)
+    ends = pump.hold(ends)
     back = carry_in(kept["whole"], ends, -1)
     back = pump.step(back)
     d_stream, tail, head, d_gates, d_taps, d_decay = mix_back(
         streams, dh, kept["a"], kept["h"], kept["start"], back, kept["conv"], kept["stream"], kept["halo"], keep,
         wts.taps, wts.decay, wts.slope, wts.gates,
     )
-    d_stream, head = pump.step((d_stream, head))
     tail = (tail + shift_seq(head, -1)).astype(bf16)
     tokens = d_stream.shape[0] // streams
     d_stream = lax.dynamic_update_slice(
@@ -794,32 +823,38 @@
         ],
         axis=1,
     ).astype(bf16)
-    used = small.shape[1]
-    small = jnp.pad(small, ((0, 0), (0, (rp - gr) * HEAD_W - used))).reshape(n * TP, rp - gr, HEAD_W)
+    small = jnp.pad(small, ((0, 0), (0, (rp - gr) * HEAD_W - small.shape[1]))).reshape(n * TP, rp - gr, HEAD_W)
     gates = d_gates.reshape(-1, HEAD_W, 2, HEAD_W).transpose(2, 0, 1, 3).reshape(n * TP, gr, HEAD_W).astype(bf16)
     extra = jnp.concatenate([small, gates], axis=1).reshape(n, TP * rp, HEAD_W)
     grad_gelu = dot_tokens(kept["normed"], d_branch).reshape(n, TP * rp, -1)
     grad_stream = dot_tokens(kept["normed"], d_stream).reshape(n, TP * rp, -1)
-    half = grad_gelu.shape[2]
-
-    def finish(both):
-        stack = both.reshape(TP, rp, -1)
-        results["gates"] = from_heads(stack[:, rp - gr :, 2 * half :].reshape(TP * gr, HEAD_W))
-        pieces = wt_exchange(both.astype(bf16).reshape(TP, rp, -1))
-        results["gelu"] = head_columns_back([p[:, :half] for p in pieces]).astype(f32)
-        results["stream"] = head_columns_back([p[:, half : 2 * half] for p in pieces]).astype(f32)
-        sums = sum(p[: rp - gr, 2 * half :].astype(f32) for p in pieces).reshape(-1)[:used]
-        above["mix_gain"], results["mlp_gain"] = sums[:rp], sums[rp : 2 * rp]
-        results["taps"] = sums[2 * rp : 2 * rp + CONV * cp].reshape(CONV, cp)
-        results["decay"] = sums[2 * rp + CONV * cp :]
-
+
+    both = ScatterJob(
+        jnp.concatenate([grad_gelu, grad_stream, extra], axis=2), False, lambda total: results.update(raw=total)
+    )
     if end is None:
-        part, grad_out, results["wide"] = tie(part, grad_out, results["wide"])
-        run(ScatterJob(grad_out.reshape(n, -1, width), True, lambda total: results.update(out=from_heads(total))))
-    run(ScatterJob(jnp.concatenate([grad_gelu, grad_stream, extra], axis=2), False, finish))
-    d_normed = pump.step(tp_scatter(part))
+        part, results["wide"] = tie(part, results["wide"])
+    pump.add(
+        both,
+        ScatterJob(grad_out.reshape(n, -1, width), True, lambda total: results.update(out=from_heads(total))),
+    )
+    d_normed = tp_scatter(pump.step(part))
+    if end is None:
+        d_normed = pump.step(d_normed)
     dv, d_gain = rms_norm_back(kept["x"], wts.mix_gain, d_normed)
-    return d_x1 + dv, d_gain
+    return d_x1 + dv, d_gain, both
+
+
+def finish_both(raw, results, above, sizes):
+    rp, gr, cp, fb = sizes
+    width = raw.shape[1] - HEAD_W
+    results["gates"] = from_heads(raw.reshape(TP, rp, -1)[:, rp - gr :, width:].reshape(TP * gr, HEAD_W))
+    pieces = jnp.stack(wt_exchange(raw.astype(bf16).reshape(TP, rp, -1)))
+    results["gelu"], results["stream"] = head_columns_back(pieces)
+    sums = jnp.sum(pieces[:, : rp - gr, width:].astype(f32), axis=0).reshape(-1)
+    above["mix_gain"], results["mlp_gain"] = sums[:rp], sums[rp : 2 * rp]
+    results["taps"] = sums[2 * rp : 2 * rp + CONV * cp].reshape(CONV, cp)
+    results["decay"] = sums[2 * rp + CONV * cp : 2 * rp + (CONV + 1) * cp]
 
 
 def per_device(block_in, start_flags, out_grad, *shards):
@@ -881,7 +916,7 @@
     gx = grad.astype(f32)
     d_mix = jnp.zeros((width,), f32)
     results = [dict() for _ in range(layers)]
-    spare, outcome = {}, []
+    spare, outcome, jobs = {}, [], []
 
     def last(ends):
         ends, kept[-1]["product"] = tie(ends, kept[-1]["product"])
@@ -890,16 +925,25 @@
 
     for layer in reversed(range(layers)):
         if layer != layers - 1:
-            g_down = pump.step(tp_gather(gx.astype(bf16)))
+            g_down = tp_gather(gx.astype(bf16))
             g_down, results[layer + 1]["down"] = tie(g_down, results[layer + 1]["down"])
         d_x1, d_mlp = mlp_back(
             gx, g_down, weights[layer], kept[layer], results[layer], rp, pump, results[layer + 1] if layer < layers - 1 else None
         )
-        above = spare if layer == layers - 1 else results[layer + 1]
-        gx, d_mix = mixer_back(
-            d_x1, keep, streams, weights[layer], kept[layer], d_mlp, d_mix, sizes, results[layer], above, pump, last if layer == layers - 1 else None
+        gx, d_mix, both = mixer_back(
+            d_x1, keep, streams, weights[layer], kept[layer], d_mlp, d_mix, sizes, results[layer], pump, last if layer == layers - 1 else None
         )
+        jobs.append(both)
+    pump.complete(jobs[:-1])
+    held = [found.pop("raw") for found in results[1:]]
+    wide = [found["wide"] for found in results[1:]]
+    held, wide = pump.step(pump.step((held, wide)))
+    for layer in range(1, layers):
+        results[layer]["wide"] = wide[layer - 1]
     pump.finish()
+    for layer in reversed(range(layers)):
+        raw = held[layer - 1] if layer else results[0].pop("raw")
+        finish_both(raw, results[layer], results[layer + 1] if layer < layers - 1 else spare, sizes)
     for found in results:
         pieces = wt_exchange(found.pop("wide").reshape(TP, rp, -1))
         found["gate"], found["up"] = ff_columns_back(jnp.stack(pieces))

time: 1130 us -> 1110 us (0.982)
  starting transfers between devices: 238 us -> 207 us
  other arithmetic: 93.2 us -> 108 us
    ppermute x32, starting transfers between devices: 44.4 us -> 17.2 us  [start(): flight = [lax.ppermute(self.a, 'seq', self.routes[0])]]
    ppermute x77, waiting for transfers between devices: 247 us -> 265 us  [swap(): return lax.ppermute(x, 'wt', [(i, i ^ k) for i in range(TP)])]
    ppermute x32, waiting for transfers between devices: 119 us -> 104 us  [start(): flight = [lax.ppermute(self.a, 'seq', self.routes[0])]]
    convert_element_type x12, other arithmetic: 5.63 us -> 21 us  [receive(): add = lambda x, y: (x.astype(f32) + y.astype(f32)).astype(bf16)]
  transfers between devices with their start and end apart: 169 -> 169, of which waited for: 73 -> 60; matrix products, arithmetic and copies ran while one was open for 29% -> 30% of each run, Pallas kernels for 6% -> 6%
where the time goes in v3:
time: 1110 us; the launch traced here: 1100 us
  waiting for transfers between devices  429 us (39%)
  starting transfers between devices  207 us (19%)
  matrix products  181 us (16%)
  other arithmetic  108 us (10%)
  local copies, waits for them, and re-layouts  88.2 us (8%)
  Pallas kernels  66 us (6%)
  between operations  18.3 us (2%)
    ppermute x77, waiting for transfers between devices, swap(): return lax.ppermute(x, 'wt', [(i, i ^ k) for i in range(TP)])  265 us
    ppermute x32, waiting for transfers between devices, start(): flight = [lax.ppermute(self.a, 'seq', self.routes[0])]  104 us
    ppermute x77, starting transfers between devices, swap(): return lax.ppermute(x, 'wt', [(i, i ^ k) for i in range(TP)])  101 us
    dot_general x10, matrix products, dot_t(): lax.dot_general(left, right, (((1,), (1,)), ((), ())), preferred_element_...  72.2 us
    dot_general x10, matrix products, dot_tokens(): lax.dot_general(left, right, (((0,), (0,)), ((), ())), preferred_element_...  57.6 us
    dot_general x12, matrix products, dot(): lax.dot_general(left, right, (((1,), (0,)), ((), ())), preferred_element_...  51.2 us
    ppermute x21, starting transfers between devices, shift_seq(): lax.ppermute(x, 'seq', [(i, i + distance) for i in range(n) if 0 <= i + d...  48.6 us
    ppermute x24, waiting for transfers between devices, start(): flight.append(lax.ppermute(self.b, 'seq', self.routes[1]))  36.3 us
  transfers between devices with their start and end apart: 169, of which 60 were waited for; matrix products, arithmetic and copies ran while one was open for 30% of the time, Pallas kernels for 6%

profile of v3, /device:TPU:3, one launch (start us, length us, event | category | flops | bytes accessed | tf_op | source)
XLA Modules:
  0.0 1096.8 jit_solution(13462982661759285297)
XLA Ops:
  50.1 8.8 collective-permute-done.20
  69.4 12.0 %collective-permute-done.17 = bf16[64,1536]{1,0:T(8,128)(2,1)S(1)} collective-permute-done((bf16[64,1536]{1,0:T(8,128)(2,1)S(1)}, bf16[64,1536]{1,0:T(8,128)(2,1)S(1)}, u32[]{:S(2)}, u32[]{:S(2)}) %collective-permute-start.17) | collective-permute-done | bytes 196640 | tf_op jit(solution)/shard_map/ppermute | solution.py:120
  161.4 8.8 shard_map.238
  209.8 17.6 %collective-permute-done.39 = bf16[256,1536]{1,0:T(8,128)(2,1)} collective-permute-done((bf16[256,1536]{1,0:T(8,128)(2,1)}, bf16[256,1536]{1,0:T(8,128)(2,1)}, u32[]{:S(2)}, u32[]{:S(2)}) %collective-permute-start.39) | collective-permute-done | bytes 786464 | tf_op jit(solution)/shard_map/ppermute | solution.py:68
  240.3 12.3 %collective-permute-done.45 = bf16[256,1536]{1,0:T(8,128)(2,1)S(1)} collective-permute-done((bf16[256,1536]{1,0:T(8,128)(2,1)S(1)}, bf16[256,1536]{1,0:T(8,128)(2,1)S(1)}, u32[]{:S(2)}, u32[]{:S(2)}) %collective-permute-start.45) | collective-permute-done | bytes 786464 | tf_op jit(solution)/shard_map/ppermute | solution.py:68
  257.1 14.6 %collective-permute-done.50 = bf16[64,1536]{1,0:T(8,128)(2,1)S(1)} collective-permute-done((bf16[64,1536]{1,0:T(8,128)(2,1)S(1)}, bf16[64,1536]{1,0:T(8,128)(2,1)S(1)}, u32[]{:S(2)}, u32[]{:S(2)}) %collective-permute-start.50) | collective-permute-done | bytes 196640 | tf_op jit(solution)/shard_map/ppermute | solution.py:122
  282.5 14.8 %collective-permute-done.53 = bf16[64,1536]{1,0:T(8,128)(2,1)} collective-permute-done((bf16[64,1536]{1,0:T(8,128)(2,1)S(1)}, bf16[64,1536]{1,0:T(8,128)(2,1)}, u32[]{:S(2)}, u32[]{:S(2)}) %collective-permute-start.53) | collective-permute-done | bytes 196640 | tf_op jit(solution)/shard_map/ppermute | solution.py:120
  320.4 15.3 %collective-permute-done.57 = bf16[256,1536]{1,0:T(8,128)(2,1)S(1)} collective-permute-done((bf16[256,1536]{1,0:T(8,128)(2,1)S(1)}, bf16[256,1536]{1,0:T(8,128)(2,1)S(1)}, u32[]{:S(2)}, u32[]{:S(2)}) %collective-permute-start.57) | collective-permute-done | bytes 786464 | tf_op jit(solution)/shard_map/ppermute | solution.py:68
  336.1 9.6 collective-permute-done.58
  355.3 13.0 %collective-permute-done.61 = bf16[256,1536]{1,0:T(8,128)(2,1)} collective-permute-done((bf16[256,1536]{1,0:T(8,128)(2,1)}, bf16[256,1536]{1,0:T(8,128)(2,1)}, u32[]{:S(2)}, u32[]{:S(2)}) %collective-permute-start.61) | collective-permute-done | bytes 786464 | tf_op jit(solution)/shard_map/ppermute | solution.py:68
  386.7 8.8 shard_map.240
  433.9 17.4 %collective-permute-done.70 = bf16[256,1536]{1,0:T(8,128)(2,1)} collective-permute-done((bf16[256,1536]{1,0:T(8,128)(2,1)}, bf16[256,1536]{1,0:T(8,128)(2,1)}, u32[]{:S(2)}, u32[]{:S(2)}) %collective-permute-start.70) | collective-permute-done | bytes 786464 | tf_op jit(solution)/shard_map/ppermute | solution.py:68
  470.1 14.8 %collective-permute-done.78 = bf16[256,1536]{1,0:T(8,128)(2,1)S(1)} collective-permute-done((bf16[256,1536]{1,0:T(8,128)(2,1)S(1)}, bf16[256,1536]{1,0:T(8,128)(2,1)S(1)}, u32[]{:S(2)}, u32[]{:S(2)}) %collective-permute-start.78) | collective-permute-done | bytes 786464 | tf_op jit(solution)/shard_map/ppermute | solution.py:68
  505.9 11.1 %multiply_convert_fusion.3 = (bf16[1024,1152]{1,0:T(8,128)(2,1)S(1)}, bf16[1024,1152]{1,0:T(8,128)(2,1)S(1)}) fusion(f32[1024,2304]{1,0:T(8,128)} %copy-done.58, bf16[1024,1536]{1,0:T(8,128)(2,1)} %copy-done.110, bf16[1152,1536]{1,0:T(8,128)(2,1)} %all-gather.11.cloned.1.call-done), kind=kOutput, calls=%fused_computation.31 | convolution fusion | flops 3649830912 | bytes 20840448 | tf_op jit(solution)/shard_map/dot_general | solution.py:27
  520.3 9.9 convolution_convert_fusion.1
  530.2 11.6 %convolution_convert_fusion.5 = bf16[1024,1536]{1,0:T(8,128)(2,1)S(1)} fusion(bf16[1024,2304]{1,0:T(8,128)(2,1)} %pad_maximum_fusion, bf16[1536,2304]{1,0:T(8,128)(2,1)} %all-gather.9.cloned.1.call-done), kind=kOutput, calls=%fused_computation.34 | convolution fusion | flops 7249330176 | bytes 14942208 | tf_op jit(solution)/shard_map/dot_general | solution.py:27
  545.7 17.7 %collective-permute-done.82 = bf16[256,1536]{1,0:T(8,128)(2,1)S(1)} collective-permute-done((bf16[256,1536]{1,0:T(8,128)(2,1)S(1)}, bf16[256,1536]{1,0:T(8,128)(2,1)S(1)}, u32[]{:S(2)}, u32[]{:S(2)}) %collective-permute-start.82) | collective-permute-done | bytes 786464 | tf_op jit(solution)/shard_map/ppermute | solution.py:68
  568.8 15.7 %collective-permute-done.84 = bf16[256,1536]{1,0:T(8,128)(2,1)} collective-permute-done((bf16[256,1536]{1,0:T(8,128)(2,1)}, bf16[256,1536]{1,0:T(8,128)(2,1)}, u32[]{:S(2)}, u32[]{:S(2)}) %collective-permute-start.84) | collective-permute-done | bytes 786464 | tf_op jit(solution)/shard_map/ppermute | solution.py:68
  627.4 15.4 %shard_map.244 = (bf16[1024,512]{1,0:T(8,128)(2,1)S(1)}, f32[24,512]{1,0:T(8,128)S(1)}, f32[24,512]{1,0:T(8,128)}, f32[4,128,256]{2,1,0:T(8,128)S(1)}, f32[4,512]{1,0:T(4,128)S(1)}, /*index=5*/f32[1,512]{1,0:T(1,128)S(1)}) custom-call(f32[1024,512]{1,0:T(8,128)S(1)} %get-tuple-element.295.dh_ref, f32[1024,512]{1,0:T(8,128)S(1)} %get-tuple-element.275.a_ref, ...), custom_call_target="tpu_custom_call" | custom-call | flops 629145600 | bytes 11534336 | tf_op jit(solution)/shard_map/pallas_call | solution.py:562
  672.8 17.5 %collective-permute-done.96 = bf16[256,1536]{1,0:T(8,128)(2,1)S(1)} collective-permute-done((bf16[256,1536]{1,0:T(8,128)(2,1)S(1)}, bf16[256,1536]{1,0:T(8,128)(2,1)S(1)}, u32[]{:S(2)}, u32[]{:S(2)}) %collective-permute-start.96) | collective-permute-done | bytes 786464 | tf_op jit(solution)/shard_map/ppermute | solution.py:68
  695.5 15.1 %collective-permute-done.98 = bf16[256,1536]{1,0:T(8,128)(2,1)S(1)} collective-permute-done((bf16[256,1536]{1,0:T(8,128)(2,1)S(1)}, bf16[256,1536]{1,0:T(8,128)(2,1)S(1)}, u32[]{:S(2)}, u32[]{:S(2)}) %collective-permute-start.98) | collective-permute-done | bytes 786464 | tf_op jit(solution)/shard_map/ppermute | solution.py:68
  737.2 10.2 convolution_convert_fusion
  750.5 11.8 %convolution_convert_fusion.4 = bf16[1024,1536]{1,0:T(8,128)(2,1)S(1)} fusion(bf16[1024,2304]{1,0:T(8,128)(2,1)} %pad_maximum_fusion.1, bf16[1536,2304]{1,0:T(8,128)(2,1)} %all-gather.5.cloned.1.call-done), kind=kOutput, calls=%fused_computation.33 | convolution fusion | flops 7249330176 | bytes 14942208 | tf_op jit(solution)/shard_map/dot_general | solution.py:27
  762.3 16.3 %collective-permute-done.102 = bf16[64,1536]{1,0:T(8,128)(2,1)S(1)} collective-permute-done((bf16[64,1536]{1,0:T(8,128)(2,1)S(1)}, bf16[64,1536]{1,0:T(8,128)(2,1)S(1)}, u32[]{:S(2)}, u32[]{:S(2)}) %collective-permute-start.102) | collective-permute-done | bytes 196640 | tf_op jit(solution)/shard_map/ppermute | solution.py:155
  790.7 16.1 %collective-permute-done.106 = bf16[256,1536]{1,0:T(8,128)(2,1)S(1)} collective-permute-done((bf16[256,1536]{1,0:T(8,128)(2,1)S(1)}, bf16[256,1536]{1,0:T(8,128)(2,1)S(1)}, u32[]{:S(2)}, u32[]{:S(2)}) %collective-permute-start.106) | collective-permute-done | bytes 786464 | tf_op jit(solution)/shard_map/ppermute | solution.py:68
  810.8 12.9 %collective-permute-done.88 = bf16[256,1536]{1,0:T(8,128)(2,1)S(1)} collective-permute-done((bf16[256,1536]{1,0:T(8,128)(2,1)S(1)}, bf16[256,1536]{1,0:T(8,128)(2,1)S(1)}, u32[]{:S(2)}, u32[]{:S(2)}) %collective-permute-start.88) | collective-permute-done | bytes 786464 | tf_op jit(solution)/shard_map/ppermute | solution.py:68
  826.2 14.3 %collective-permute-done.108 = bf16[256,1536]{1,0:T(8,128)(2,1)} collective-permute-done((bf16[256,1536]{1,0:T(8,128)(2,1)}, bf16[256,1536]{1,0:T(8,128)(2,1)}, u32[]{:S(2)}, u32[]{:S(2)}) %collective-permute-start.108) | collective-permute-done | bytes 786464 | tf_op jit(solution)/shard_map/ppermute | solution.py:68
  900.3 14.7 %shard_map.246 = (bf16[1024,512]{1,0:T(8,128)(2,1)S(1)}, f32[24,512]{1,0:T(8,128)S(1)}, f32[24,512]{1,0:T(8,128)S(1)}, f32[4,128,256]{2,1,0:T(8,128)S(1)}, f32[4,512]{1,0:T(4,128)S(1)}, /*index=5*/f32[1,512]{1,0:T(1,128)S(1)}) custom-call(f32[1024,512]{1,0:T(8,128)S(1)} %get-tuple-element.322.dh_ref, f32[1024,512]{1,0:T(8,128)S(1)} %copy-done.1, ...), custom_call_target="tpu_custom_call" | custom-call | flops 629145600 | bytes 11534336 | tf_op jit(solution)/shard_map/pallas_call | solution.py:562
  938.1 8.9 collective-permute-start.155
  962.6 15.9 %collective-permute-done.125 = bf16[256,1536]{1,0:T(8,128)(2,1)S(1)} collective-permute-done((bf16[256,1536]{1,0:T(8,128)(2,1)S(1)}, bf16[256,1536]{1,0:T(8,128)(2,1)S(1)}, u32[]{:S(2)}, u32[]{:S(2)}) %collective-permute-start.125) | collective-permute-done | bytes 786464 | tf_op jit(solution)/shard_map/ppermute | solution.py:68
  978.8 12.2 %collective-permute-done.130 = bf16[64,1536]{1,0:T(8,128)(2,1)S(1)} collective-permute-done((bf16[64,1536]{1,0:T(8,128)(2,1)S(1)}, bf16[64,1536]{1,0:T(8,128)(2,1)S(1)}, u32[]{:S(2)}, u32[]{:S(2)}) %collective-permute-start.130) | collective-permute-done | bytes 196640 | tf_op jit(solution)/shard_map/ppermute | solution.py:155
  1026.5 13.2 %collective-permute-done.143 = bf16[64,1536]{1,0:T(8,128)(2,1)S(1)} collective-permute-done((bf16[64,1536]{1,0:T(8,128)(2,1)S(1)}, bf16[64,1536]{1,0:T(8,128)(2,1)S(1)}, u32[]{:S(2)}, u32[]{:S(2)}) %collective-permute-start.143) | collective-permute-done | bytes 196640 | tf_op jit(solution)/shard_map/ppermute | solution.py:155
  (1027 shorter events, 650.1 us)
Async XLA Ops:
  7.2 223.4 %all-gather.5.cloned.1.call-start = ((), (), s32[]{:S(2)}) async-start(), calls=%async_computation.4 | async-start | bytes 7962624 | tf_op jit(solution)/shard_map/all_gather | solution.py:700
  48.4 39.7 %collective-permute-start.19 = (bf16[256,1536]{1,0:T(8,128)(2,1)S(1)}, bf16[256,1536]{1,0:T(8,128)(2,1)S(1)}, u32[]{:S(2)}, u32[]{:S(2)}) collective-permute-start(bf16[256,1536]{1,0:T(8,128)(2,1)S(1)} %bitcast.626), channel_id=1, source_target_pairs={{0,1},{1,0},{2,3},{3,2},{4,5},{5,4},{6,7},{7,6},{8,9},{9,8},{10,11... | collective-permute-start | bytes 2359304 | tf_op jit(solution)/shard_map/ppermute | solution.py:68
  95.8 210.8 %all-gather.7.cloned.1.call-start = ((), (), s32[]{:S(2)}) async-start(), calls=%async_computation.5 | async-start | bytes 3981312 | tf_op jit(solution)/shard_map/all_gather | solution.py:697
  133.1 49.7 %collective-permute-start.33 = (bf16[48,1152]{1,0:T(8,128)(2,1)}, bf16[48,1152]{1,0:T(8,128)(2,1)}, u32[]{:S(2)}, u32[]{:S(2)}) collective-permute-start(bf16[48,1152]{1,0:T(8,128)(2,1)} %get-tuple-element.551), channel_id=1, source_target_pairs={{0,1},{1,0},{2,3},{3,2},{4,5},{5,4},{6,7},{7,6},{8,9},{9,8},{10,11... | collective-permute-start | bytes 331784 | tf_op jit(solution)/shard_map/ppermute | solution.py:68
  133.9 50.3 %collective-permute-start.34 = (bf16[48,1152]{1,0:T(8,128)(2,1)}, bf16[48,1152]{1,0:T(8,128)(2,1)}, u32[]{:S(2)}, u32[]{:S(2)}) collective-permute-start(bf16[48,1152]{1,0:T(8,128)(2,1)} %get-tuple-element.550), channel_id=1, source_target_pairs={{0,2},{1,3},{2,0},{3,1},{4,6},{5,7},{6,4},{7,5},{8,10},{9,11},{10,... | collective-permute-start | bytes 331784 | tf_op jit(solution)/shard_map/ppermute | solution.py:68
  134.1 50.1 %collective-permute-start.35 = (bf16[48,1152]{1,0:T(8,128)(2,1)}, bf16[48,1152]{1,0:T(8,128)(2,1)}, u32[]{:S(2)}, u32[]{:S(2)}) collective-permute-start(bf16[48,1152]{1,0:T(8,128)(2,1)} %get-tuple-element.549), channel_id=1, source_target_pairs={{0,3},{1,2},{2,1},{3,0},{4,7},{5,6},{6,5},{7,4},{8,11},{9,10},{10,... | collective-permute-start | bytes 331784 | tf_op jit(solution)/shard_map/ppermute | solution.py:68
  155.5 298.8 %all-gather.9.cloned.1.call-start = ((), (), s32[]{:S(2)}) async-start(), calls=%async_computation.6 | async-start | bytes 7962624 | tf_op jit(solution)/shard_map/all_gather | solution.py:700
  200.3 30.3 %collective-permute-start.40 = (bf16[192,1152]{1,0:T(8,128)(2,1)S(1)}, bf16[192,1152]{1,0:T(8,128)(2,1)S(1)}, u32[]{:S(2)}, u32[]{:S(2)}) collective-permute-start(bf16[192,1152]{1,0:T(8,128)(2,1)S(1)} %bitcast.656), channel_id=1, source_target_pairs={{4,0},{12,4},{20,12},{28,20},{24,28},{16,24},{8,16},{0,8},{5,1},{1... | collective-permute-start | bytes 1327112 | tf_op jit(solution)/shard_map/ppermute | solution.py:120
  209.7 296.2 %all-gather.11.cloned.1.call-start = ((), (), s32[]{:S(2)}) async-start(), calls=%async_computation.7 | async-start | bytes 3981312 | tf_op jit(solution)/shard_map/all_gather | solution.py:697
  235.4 36.2 %collective-permute-start.47 = (bf16[192,1152]{1,0:T(8,128)(2,1)S(1)}, bf16[192,1152]{1,0:T(8,128)(2,1)S(1)}, u32[]{:S(2)}, u32[]{:S(2)}) collective-permute-start(bf16[192,1152]{1,0:T(8,128)(2,1)S(1)} %collective-permute-done.40), channel_id=1, source_target_pairs={{4,0},{12,4},{20,12},{28,20},{24,28},{16,24},{8,16},{0,8},{5,1},{1... | collective-permute-start | bytes 1327112 | tf_op jit(solution)/shard_map/ppermute | solution.py:120
  235.4 36.2 %collective-permute-start.48 = (bf16[192,1152]{1,0:T(8,128)(2,1)}, bf16[192,1152]{1,0:T(8,128)(2,1)S(1)}, u32[]{:S(2)}, u32[]{:S(2)}) collective-permute-start(bf16[192,1152]{1,0:T(8,128)(2,1)} %collective-permute-done.41), channel_id=1, source_target_pairs={{0,4},{4,12},{12,20},{20,28},{28,24},{24,16},{16,8},{8,0},{1,5},{5... | collective-permute-start | bytes 1327112 | tf_op jit(solution)/shard_map/ppermute | solution.py:122
  271.7 32.1 %collective-permute-start.51 = (bf16[192,1152]{1,0:T(8,128)(2,1)S(1)}, bf16[192,1152]{1,0:T(8,128)(2,1)S(1)}, u32[]{:S(2)}, u32[]{:S(2)}) collective-permute-start(bf16[192,1152]{1,0:T(8,128)(2,1)S(1)} %collective-permute-done.47), channel_id=1, source_target_pairs={{4,0},{12,4},{20,12},{28,20},{24,28},{16,24},{8,16},{0,8},{5,1},{1... | collective-permute-start | bytes 1327112 | tf_op jit(solution)/shard_map/ppermute | solution.py:120
  271.7 32.1 %collective-permute-start.52 = (bf16[192,1152]{1,0:T(8,128)(2,1)S(1)}, bf16[192,1152]{1,0:T(8,128)(2,1)S(1)}, u32[]{:S(2)}, u32[]{:S(2)}) collective-permute-start(bf16[192,1152]{1,0:T(8,128)(2,1)S(1)} %collective-permute-done.48), channel_id=1, source_target_pairs={{0,4},{4,12},{12,20},{20,28},{28,24},{24,16},{16,8},{8,0},{1,5},{5... | collective-permute-start | bytes 1327112 | tf_op jit(solution)/shard_map/ppermute | solution.py:122
  274.1 29.7 %collective-permute-start.54 = (bf16[64,1536]{1,0:T(8,128)(2,1)S(1)}, bf16[64,1536]{1,0:T(8,128)(2,1)S(1)}, u32[]{:S(2)}, u32[]{:S(2)}) collective-permute-start(bf16[64,1536]{1,0:T(8,128)(2,1)S(1)} %collective-permute-done.50), channel_id=1, source_target_pairs={{4,0},{12,4},{20,12},{28,20},{24,28},{16,24},{8,16},{0,8},{5,1},{1... | collective-permute-start | bytes 589832 | tf_op jit(solution)/shard_map/ppermute | solution.py:122
  315.9 29.8 %collective-permute-start.58 = (bf16[192,1152]{1,0:T(8,128)(2,1)S(1)}, bf16[192,1152]{1,0:T(8,128)(2,1)S(1)}, u32[]{:S(2)}, u32[]{:S(2)}) collective-permute-start(bf16[192,1152]{1,0:T(8,128)(2,1)S(1)} %collective-permute-done.51), channel_id=1, source_target_pairs={{4,0},{12,4},{20,12},{28,20},{24,28},{16,24},{8,16},{0,8},{5,1},{1... | collective-permute-start | bytes 1327112 | tf_op jit(solution)/shard_map/ppermute | solution.py:120
  433.4 283.1 %reduce-scatter.5.cloned.1.call-start = ((), (), s32[]{:S(2)}) async-start(), calls=%async_computation.8 | async-start | bytes 3981312 | tf_op jit(solution)/shard_map/reduce_scatter | solution.py:786
  433.5 34.7 %collective-permute-start.75 = (bf16[256,1536]{1,0:T(8,128)(2,1)}, bf16[256,1536]{1,0:T(8,128)(2,1)}, u32[]{:S(2)}, u32[]{:S(2)}) collective-permute-start(bf16[256,1536]{1,0:T(8,128)(2,1)} %bitcast.649), channel_id=1, source_target_pairs={{0,2},{1,3},{2,0},{3,1},{4,6},{5,7},{6,4},{7,5},{8,10},{9,11},{10,... | collective-permute-start | bytes 2359304 | tf_op jit(solution)/shard_map/ppermute | solution.py:68
  530.1 220.3 %reduce-scatter.7.cloned.1.call-start = ((), (), s32[]{:S(2)}) async-start(), calls=%async_computation.9 | async-start | bytes 7962624 | tf_op jit(solution)/shard_map/reduce_scatter | solution.py:783
  587.9 348.7 %reduce-scatter.9.cloned.1.call-start = ((), (), s32[]{:S(2)}) async-start(), calls=%async_computation.10 | async-start | bytes 7962624 | tf_op jit(solution)/shard_map/reduce_scatter | solution.py:783
  747.4 263.8 %reduce-scatter.11.cloned.1.call-start = ((), (), s32[]{:S(2)}) async-start(), calls=%async_computation.11 | async-start | bytes 3981312 | tf_op jit(solution)/shard_map/reduce_scatter | solution.py:786
  747.5 31.1 %collective-permute-start.100 = (bf16[192,1152]{1,0:T(8,128)(2,1)S(1)}, bf16[192,1152]{1,0:T(8,128)(2,1)S(1)}, u32[]{:S(2)}, u32[]{:S(2)}) collective-permute-start(bf16[192,1152]{1,0:T(8,128)(2,1)S(1)} %get-tuple-element.313), channel_id=1, source_target_pairs={{0,4},{4,12},{12,20},{20,28},{28,24},{24,16},{16,8},{8,0},{1,5},{5... | collective-permute-start | bytes 1327112 | tf_op jit(solution)/shard_map/ppermute | solution.py:155
  747.6 31.1 %collective-permute-start.101 = (bf16[192,1152]{1,0:T(8,128)(2,1)S(1)}, bf16[192,1152]{1,0:T(8,128)(2,1)S(1)}, u32[]{:S(2)}, u32[]{:S(2)}) collective-permute-start(bf16[192,1152]{1,0:T(8,128)(2,1)S(1)} %get-tuple-element.314), channel_id=1, source_target_pairs={{4,0},{12,4},{20,12},{28,20},{24,28},{16,24},{8,16},{0,8},{5,1},{1... | collective-permute-start | bytes 1327112 | tf_op jit(solution)/shard_map/ppermute | solution.py:157
  749.0 29.6 %collective-permute-start.102 = (bf16[64,1536]{1,0:T(8,128)(2,1)S(1)}, bf16[64,1536]{1,0:T(8,128)(2,1)S(1)}, u32[]{:S(2)}, u32[]{:S(2)}) collective-permute-start(bf16[64,1536]{1,0:T(8,128)(2,1)S(1)} %copy-done.129), channel_id=1, source_target_pairs={{4,0},{12,4},{20,12},{28,20},{24,28},{16,24},{8,16},{0,8},{5,1},{1... | collective-permute-start | bytes 589832 | tf_op jit(solution)/shard_map/ppermute | solution.py:155
  789.8 33.8 %collective-permute-start.88 = (bf16[256,1536]{1,0:T(8,128)(2,1)S(1)}, bf16[256,1536]{1,0:T(8,128)(2,1)S(1)}, u32[]{:S(2)}, u32[]{:S(2)}) collective-permute-start(bf16[256,1536]{1,0:T(8,128)(2,1)S(1)} %add_convert_fusion.3), channel_id=1, source_target_pairs={{0,2},{1,3},{2,0},{3,1},{4,6},{5,7},{6,4},{7,5},{8,10},{9,11},{10,... | collective-permute-start | bytes 2359304 | tf_op jit(solution)/shard_map/ppermute | solution.py:68
  809.4 31.1 %collective-permute-start.108 = (bf16[256,1536]{1,0:T(8,128)(2,1)}, bf16[256,1536]{1,0:T(8,128)(2,1)}, u32[]{:S(2)}, u32[]{:S(2)}) collective-permute-start(bf16[256,1536]{1,0:T(8,128)(2,1)} %get-tuple-element.436), channel_id=1, source_target_pairs={{0,2},{1,3},{2,0},{3,1},{4,6},{5,7},{6,4},{7,5},{8,10},{9,11},{10,... | collective-permute-start | bytes 2359304 | tf_op jit(solution)/shard_map/ppermute | solution.py:68
  918.2 30.4 %collective-permute-start.119 = (bf16[192,1152]{1,0:T(8,128)(2,1)}, bf16[192,1152]{1,0:T(8,128)(2,1)}, u32[]{:S(2)}, u32[]{:S(2)}) collective-permute-start(bf16[192,1152]{1,0:T(8,128)(2,1)} %get-tuple-element.340), channel_id=1, source_target_pairs={{0,4},{4,12},{12,20},{20,28},{28,24},{24,16},{16,8},{8,0},{1,5},{5... | collective-permute-start | bytes 1327112 | tf_op jit(solution)/shard_map/ppermute | solution.py:155
  918.3 30.4 %collective-permute-start.120 = (bf16[192,1152]{1,0:T(8,128)(2,1)}, bf16[192,1152]{1,0:T(8,128)(2,1)}, u32[]{:S(2)}, u32[]{:S(2)}) collective-permute-start(bf16[192,1152]{1,0:T(8,128)(2,1)} %get-tuple-element.341), channel_id=1, source_target_pairs={{4,0},{12,4},{20,12},{28,20},{24,28},{16,24},{8,16},{0,8},{5,1},{1... | collective-permute-start | bytes 1327112 | tf_op jit(solution)/shard_map/ppermute | solution.py:157
  953.0 38.1 %collective-permute-start.126 = (bf16[192,1152]{1,0:T(8,128)(2,1)S(1)}, bf16[192,1152]{1,0:T(8,128)(2,1)S(1)}, u32[]{:S(2)}, u32[]{:S(2)}) collective-permute-start(bf16[192,1152]{1,0:T(8,128)(2,1)S(1)} %fusion.63), channel_id=1, source_target_pairs={{0,4},{4,12},{12,20},{20,28},{28,24},{24,16},{16,8},{8,0},{1,5},{5... | collective-permute-start | bytes 1327112 | tf_op jit(solution)/shard_map/ppermute | solution.py:155
  955.7 35.4 %collective-permute-start.128 = (bf16[192,1152]{1,0:T(8,128)(2,1)}, bf16[192,1152]{1,0:T(8,128)(2,1)S(1)}, u32[]{:S(2)}, u32[]{:S(2)}) collective-permute-start(bf16[192,1152]{1,0:T(8,128)(2,1)} %get-tuple-element.350), channel_id=1, source_target_pairs={{0,4},{4,12},{12,20},{20,28},{28,24},{24,16},{16,8},{8,0},{1,5},{5... | collective-permute-start | bytes 1327112 | tf_op jit(solution)/shard_map/ppermute | solution.py:155
  961.0 30.0 %collective-permute-start.129 = (bf16[192,1152]{1,0:T(8,128)(2,1)S(1)}, bf16[192,1152]{1,0:T(8,128)(2,1)S(1)}, u32[]{:S(2)}, u32[]{:S(2)}) collective-permute-start(bf16[192,1152]{1,0:T(8,128)(2,1)S(1)} %copy-done.102), channel_id=1, source_target_pairs={{4,0},{12,4},{20,12},{28,20},{24,28},{16,24},{8,16},{0,8},{5,1},{1... | collective-permute-start | bytes 1327112 | tf_op jit(solution)/shard_map/ppermute | solution.py:157
  961.1 29.9 %collective-permute-start.130 = (bf16[64,1536]{1,0:T(8,128)(2,1)S(1)}, bf16[64,1536]{1,0:T(8,128)(2,1)S(1)}, u32[]{:S(2)}, u32[]{:S(2)}) collective-permute-start(bf16[64,1536]{1,0:T(8,128)(2,1)S(1)} %copy-done.131), channel_id=1, source_target_pairs={{4,0},{12,4},{20,12},{28,20},{24,28},{16,24},{8,16},{0,8},{5,1},{1... | collective-permute-start | bytes 589832 | tf_op jit(solution)/shard_map/ppermute | solution.py:155
  1015.1 72.6 %collective-permute-start.154 = (f32[64,1536]{1,0:T(8,128)}, f32[64,1536]{1,0:T(8,128)}, u32[]{:S(2)}, u32[]{:S(2)}) collective-permute-start(f32[64,1536]{1,0:T(8,128)} %fusion.71), channel_id=1, source_target_pairs={{0,0},{4,1},{1,2},{5,3},{2,4},{6,5},{3,6},{7,7},{8,8},{12,9},{9,10... | collective-permute-start | bytes 1179656 | tf_op jit(solution)/shard_map/ppermute | solution.py:282
  (306 other events, 4009.5 us)
Sparse Core Ops, SparseCore 0:
  95.9 117.5 all-gather.4
  215.7 82.3 all-gather.6
  300.3 123.5 all-gather.8
  433.5 62.6 all-gather.10
  530.3 78.8 reduce-scatter.4
  612.7 128.7 reduce-scatter.6
  747.5 142.6 reduce-scatter.8
  893.8 99.7 reduce-scatter.10

commit v4 on v3

--- a/solution.py
+++ b/solution.py
@@ -75,11 +75,16 @@
     return jnp.concatenate([x, near, far, diagonal], axis=0)
 
 
-def tp_scatter(part):
-    far = (part[2].astype(f32) + swap(part[3], 1).astype(f32)).astype(bf16)
+def tp_scatter(term, *rows):
+    half = rows[0].shape[0] // 2
+    part = term(*[r[half:] for r in rows])
+    part = part.reshape(2, half // 2, -1)
+    far = (part[0].astype(f32) + swap(part[1], 1).astype(f32)).astype(bf16)
     across = swap(far, 2)
-    near = swap(part[1], 1)
-    return part[0].astype(f32) + near.astype(f32) + across.astype(f32)
+    close = term(*[r[:half] for r in rows])
+    close = close.reshape(2, half // 2, -1)
+    near = swap(close[1], 1)
+    return close[0].astype(f32) + near.astype(f32) + across.astype(f32)
 
 
 def wt_exchange(pieces):
@@ -742,7 +747,7 @@
     if following is not None:
         pump.add(following.first_job(), following.out_job())
         merged = pump.step(merged)
-    mixed = tp_scatter(dot(merged, wts.out, bf16).reshape(TP, -1, width))
+    mixed = tp_scatter(lambda rows: dot(rows, wts.out, bf16), merged)
     mixed, wts.wide = tie(mixed, wts.wide)
     mixed = pump.step(mixed)
     x1 = x + mixed
@@ -761,7 +766,7 @@
 def block_end(kept, wts):
     product = kept["product"]
     width = kept["x1"].shape[1]
-    return kept["x1"] + tp_scatter(dot(product, wts.down, bf16).reshape(TP, -1, width))
+    return kept["x1"] + tp_scatter(lambda rows: dot(rows, wts.down, bf16), product)
 
 
 def mlp_back(gx, g_down, wts, kept, results, rp, pump, above):
@@ -778,8 +783,7 @@
     d_wide, grad_wide, grad_down = tie(d_wide, grad_wide, grad_down)
     if above is not None:
         d_wide, above["wide"] = tie(d_wide, above["wide"])
-    part = dot_t(d_wide, wts.wide, bf16).reshape(TP, -1, width)
-    d_mlp_in = tp_scatter(pump.step(part))
+    d_mlp_in = tp_scatter(lambda rows: dot_t(rows, wts.wide, bf16), pump.step(d_wide))
     results["wide"] = lax.psum_scatter(grad_wide, "seq", scatter_dimension=0)
     if above is not None:
         d_mlp_in, grad_down = tie(d_mlp_in, grad_down)
@@ -810,7 +814,6 @@
     d_stream = lax.dynamic_update_slice(
         d_stream.reshape(streams, tokens, -1), tail.reshape(REACH, streams, -1).transpose(1, 0, 2), (0, tokens - REACH, 0)
     ).reshape(d_stream.shape)
-    part = (dot_t(d_branch, wts.gelu) + dot_t(d_stream, wts.stream)).astype(bf16).reshape(TP, -1, width)
 
     def full(v):
         lines = v.reshape(v.shape[0], -1, 1, HEAD_W)
@@ -833,12 +836,14 @@
         jnp.concatenate([grad_gelu, grad_stream, extra], axis=2), False, lambda total: results.update(raw=total)
     )
     if end is None:
-        part, results["wide"] = tie(part, results["wide"])
+        d_stream, results["wide"] = tie(d_stream, results["wide"])
     pump.add(
         both,
         ScatterJob(grad_out.reshape(n, -1, width), True, lambda total: results.update(out=from_heads(total))),
     )
-    d_normed = tp_scatter(pump.step(part))
+    d_normed = tp_scatter(
+        lambda branch, stream: (dot_t(branch, wts.gelu) + dot_t(stream, wts.stream)).astype(bf16), d_branch, pump.step(d_stream)
+    )
     if end is None:
         d_normed = pump.step(d_normed)
     dv, d_gain = rms_norm_back(kept["x"], wts.mix_gain, d_normed)

time: 1110 us -> 1130 us (1.018)
  waiting for transfers between devices: 429 us -> 409 us
  starting transfers between devices: 207 us -> 225 us
  matrix products: 181 us -> 194 us
    ppermute x77, waiting for transfers between devices: 265 us -> 233 us  [swap(): return lax.ppermute(x, 'wt', [(i, i ^ k) for i in range(TP)])]
    ppermute x21, starting transfers between devices: 48.6 us -> 61.2 us  [shift_seq(): lax.ppermute(x, 'seq', [(i, i + distance) for i in range(n) if 0 <= i + d...]
    dot_general x10 -> x16, matrix products: 72.2 us -> 82.4 us  [dot_t(): lax.dot_general(left, right, (((1,), (1,)), ((), ())), preferred_element_...]
    unnamed x350 -> x364, local copies, waits for them, and re-layouts: 16.9 us -> 26.8 us
    dot_general x12 -> x16, matrix products: 51.2 us -> 54 us  [dot(): lax.dot_general(left, right, (((1,), (0,)), ((), ())), preferred_element_...]
  transfers between devices with their start and end apart: 169 -> 169, of which waited for: 60 -> 58; matrix products, arithmetic and copies ran while one was open for 30% -> 31% of each run, Pallas kernels for 6% -> 6%
where the time goes in v4:
time: 1130 us; the launch traced here: 1120 us
  waiting for transfers between devices  409 us (36%)
  starting transfers between devices  225 us (20%)
  matrix products  194 us (17%)
  other arithmetic  114 us (10%)
  local copies, waits for them, and re-layouts  93.2 us (8%)
  Pallas kernels  64.8 us (6%)
  between operations  18.6 us (2%)
    ppermute x77, waiting for transfers between devices, swap(): return lax.ppermute(x, 'wt', [(i, i ^ k) for i in range(TP)])  233 us
    ppermute x32, waiting for transfers between devices, start(): flight = [lax.ppermute(self.a, 'seq', self.routes[0])]  111 us
    ppermute x77, starting transfers between devices, swap(): return lax.ppermute(x, 'wt', [(i, i ^ k) for i in range(TP)])  99.9 us
    dot_general x16, matrix products, dot_t(): lax.dot_general(left, right, (((1,), (1,)), ((), ())), preferred_element_...  82.4 us
    ppermute x21, starting transfers between devices, shift_seq(): lax.ppermute(x, 'seq', [(i, i + distance) for i in range(n) if 0 <= i + d...  61.2 us
    dot_general x10, matrix products, dot_tokens(): lax.dot_general(left, right, (((0,), (0,)), ((), ())), preferred_element_...  57.9 us
    dot_general x16, matrix products, dot(): lax.dot_general(left, right, (((1,), (0,)), ((), ())), preferred_element_...  54 us
    ppermute x24, waiting for transfers between devices, start(): flight.append(lax.ppermute(self.b, 'seq', self.routes[1]))  39.2 us
  transfers between devices with their start and end apart: 169, of which 58 were waited for; matrix products, arithmetic and copies ran while one was open for 31% of the time, Pallas kernels for 6%

profile of v4, /device:TPU:3, one launch (start us, length us, event | category | flops | bytes accessed | tf_op | source)
XLA Modules:
  0.0 1119.2 jit_solution(15697107255123323862)
XLA Ops:
  52.4 8.7 collective-permute-done.13
  67.3 12.0 %collective-permute-done.17 = bf16[64,1536]{1,0:T(8,128)(2,1)S(1)} collective-permute-done((bf16[64,1536]{1,0:T(8,128)(2,1)S(1)}, bf16[64,1536]{1,0:T(8,128)(2,1)S(1)}, u32[]{:S(2)}, u32[]{:S(2)}) %collective-permute-start.17) | collective-permute-done | bytes 196640 | tf_op jit(solution)/shard_map/ppermute | solution.py:125
  153.9 8.8 shard_map.238
  208.1 15.7 %collective-permute-done.39 = bf16[256,1536]{1,0:T(8,128)(2,1)} collective-permute-done((bf16[256,1536]{1,0:T(8,128)(2,1)}, bf16[256,1536]{1,0:T(8,128)(2,1)}, u32[]{:S(2)}, u32[]{:S(2)}) %collective-permute-start.39) | collective-permute-done | bytes 786464 | tf_op jit(solution)/shard_map/ppermute | solution.py:68
  273.4 18.3 %collective-permute-done.53 = bf16[64,1536]{1,0:T(8,128)(2,1)S(1)} collective-permute-done((bf16[64,1536]{1,0:T(8,128)(2,1)S(1)}, bf16[64,1536]{1,0:T(8,128)(2,1)S(1)}, u32[]{:S(2)}, u32[]{:S(2)}) %collective-permute-start.53) | collective-permute-done | bytes 196640 | tf_op jit(solution)/shard_map/ppermute | solution.py:125
  291.7 10.9 collective-permute-done.54
  324.2 15.6 %collective-permute-done.57 = bf16[256,1536]{1,0:T(8,128)(2,1)S(1)} collective-permute-done((bf16[256,1536]{1,0:T(8,128)(2,1)S(1)}, bf16[256,1536]{1,0:T(8,128)(2,1)S(1)}, u32[]{:S(2)}, u32[]{:S(2)}) %collective-permute-start.57) | collective-permute-done | bytes 786464 | tf_op jit(solution)/shard_map/ppermute | solution.py:68
  389.6 8.8 shard_map.240
  433.6 17.6 %collective-permute-done.70 = bf16[256,1536]{1,0:T(8,128)(2,1)} collective-permute-done((bf16[256,1536]{1,0:T(8,128)(2,1)}, bf16[256,1536]{1,0:T(8,128)(2,1)}, u32[]{:S(2)}, u32[]{:S(2)}) %collective-permute-start.70) | collective-permute-done | bytes 786464 | tf_op jit(solution)/shard_map/ppermute | solution.py:68
  458.5 9.5 collective-permute-done.75
  469.6 15.2 %collective-permute-done.78 = bf16[256,1536]{1,0:T(8,128)(2,1)S(1)} collective-permute-done((bf16[256,1536]{1,0:T(8,128)(2,1)S(1)}, bf16[256,1536]{1,0:T(8,128)(2,1)S(1)}, u32[]{:S(2)}, u32[]{:S(2)}) %collective-permute-start.78) | collective-permute-done | bytes 786464 | tf_op jit(solution)/shard_map/ppermute | solution.py:68
  505.7 11.1 multiply_convert_fusion.3
  520.0 9.8 convolution_convert_fusion.1
  538.2 7.6 convolution_convert_fusion.21
  548.2 16.9 %collective-permute-done.82 = bf16[256,1536]{1,0:T(8,128)(2,1)S(1)} collective-permute-done((bf16[256,1536]{1,0:T(8,128)(2,1)S(1)}, bf16[256,1536]{1,0:T(8,128)(2,1)S(1)}, u32[]{:S(2)}, u32[]{:S(2)}) %collective-permute-start.82) | collective-permute-done | bytes 786464 | tf_op jit(solution)/shard_map/ppermute | solution.py:68
  569.4 16.8 %collective-permute-done.84 = bf16[256,1536]{1,0:T(8,128)(2,1)} collective-permute-done((bf16[256,1536]{1,0:T(8,128)(2,1)}, bf16[256,1536]{1,0:T(8,128)(2,1)}, u32[]{:S(2)}, u32[]{:S(2)}) %collective-permute-start.84) | collective-permute-done | bytes 786464 | tf_op jit(solution)/shard_map/ppermute | solution.py:68
  627.4 14.7 %shard_map.244 = (bf16[1024,512]{1,0:T(8,128)(2,1)S(1)}, f32[24,512]{1,0:T(8,128)S(1)}, f32[24,512]{1,0:T(8,128)S(1)}, f32[4,128,256]{2,1,0:T(8,128)S(1)}, f32[4,512]{1,0:T(4,128)S(1)}, /*index=5*/f32[1,512]{1,0:T(1,128)S(1)}) custom-call(f32[1024,512]{1,0:T(8,128)S(1)} %get-tuple-element.295.dh_ref, f32[1024,512]{1,0:T(8,128)S(1)} %copy-done.1, ...), custom_call_target="tpu_custom_call" | custom-call | flops 629145600 | bytes 11534336 | tf_op jit(solution)/shard_map/pallas_call | solution.py:567
  674.0 16.7 %collective-permute-done.96 = bf16[256,1536]{1,0:T(8,128)(2,1)S(1)} collective-permute-done((bf16[256,1536]{1,0:T(8,128)(2,1)S(1)}, bf16[256,1536]{1,0:T(8,128)(2,1)S(1)}, u32[]{:S(2)}, u32[]{:S(2)}) %collective-permute-start.96) | collective-permute-done | bytes 786464 | tf_op jit(solution)/shard_map/ppermute | solution.py:68
  695.4 16.2 %collective-permute-done.98 = bf16[256,1536]{1,0:T(8,128)(2,1)S(1)} collective-permute-done((bf16[256,1536]{1,0:T(8,128)(2,1)S(1)}, bf16[256,1536]{1,0:T(8,128)(2,1)S(1)}, u32[]{:S(2)}, u32[]{:S(2)}) %collective-permute-start.98) | collective-permute-done | bytes 786464 | tf_op jit(solution)/shard_map/ppermute | solution.py:68
  719.6 8.4 convolution_convert_fusion.2
  728.0 9.4 multiply_convert_fusion.1
  740.9 10.0 convolution_convert_fusion
  764.2 25.1 %collective-permute-done.102 = bf16[64,1536]{1,0:T(8,128)(2,1)} collective-permute-done((bf16[64,1536]{1,0:T(8,128)(2,1)}, bf16[64,1536]{1,0:T(8,128)(2,1)}, u32[]{:S(2)}, u32[]{:S(2)}) %collective-permute-start.102) | collective-permute-done | bytes 196640 | tf_op jit(solution)/shard_map/ppermute | solution.py:160
  789.3 7.6 convolution_convert_fusion.15
  811.3 12.7 %collective-permute-done.106 = bf16[256,1536]{1,0:T(8,128)(2,1)S(1)} collective-permute-done((bf16[256,1536]{1,0:T(8,128)(2,1)S(1)}, bf16[256,1536]{1,0:T(8,128)(2,1)S(1)}, u32[]{:S(2)}, u32[]{:S(2)}) %collective-permute-start.106) | collective-permute-done | bytes 786464 | tf_op jit(solution)/shard_map/ppermute | solution.py:68
  828.1 12.8 %collective-permute-done.88 = bf16[256,1536]{1,0:T(8,128)(2,1)S(1)} collective-permute-done((bf16[256,1536]{1,0:T(8,128)(2,1)S(1)}, bf16[256,1536]{1,0:T(8,128)(2,1)S(1)}, u32[]{:S(2)}, u32[]{:S(2)}) %collective-permute-start.88) | collective-permute-done | bytes 786464 | tf_op jit(solution)/shard_map/ppermute | solution.py:68
  844.9 12.8 %collective-permute-done.108 = bf16[256,1536]{1,0:T(8,128)(2,1)} collective-permute-done((bf16[256,1536]{1,0:T(8,128)(2,1)}, bf16[256,1536]{1,0:T(8,128)(2,1)}, u32[]{:S(2)}, u32[]{:S(2)}) %collective-permute-start.108) | collective-permute-done | bytes 786464 | tf_op jit(solution)/shard_map/ppermute | solution.py:68
  878.9 12.5 %collective-permute-done.110 = bf16[192,1152]{1,0:T(8,128)(2,1)S(1)} collective-permute-done((bf16[192,1152]{1,0:T(8,128)(2,1)}, bf16[192,1152]{1,0:T(8,128)(2,1)S(1)}, u32[]{:S(2)}, u32[]{:S(2)}) %collective-permute-start.110) | collective-permute-done | bytes 442400 | tf_op jit(solution)/shard_map/ppermute | solution.py:160
  891.4 10.3 collective-permute-done.111
  936.2 14.7 %shard_map.246 = (bf16[1024,512]{1,0:T(8,128)(2,1)S(1)}, f32[24,512]{1,0:T(8,128)S(1)}, f32[24,512]{1,0:T(8,128)S(1)}, f32[4,128,256]{2,1,0:T(8,128)S(1)}, f32[4,512]{1,0:T(4,128)S(1)}, /*index=5*/f32[1,512]{1,0:T(1,128)S(1)}) custom-call(f32[1024,512]{1,0:T(8,128)S(1)} %get-tuple-element.322.dh_ref, f32[1024,512]{1,0:T(8,128)S(1)} %get-tuple-element.236.a_ref, ...), custom_call_target="tpu_custom_call" | custom-call | flops 629145600 | bytes 11534336 | tf_op jit(solution)/shard_map/pallas_call | solution.py:567
  993.9 13.8 %collective-permute-done.125 = bf16[256,1536]{1,0:T(8,128)(2,1)S(1)} collective-permute-done((bf16[256,1536]{1,0:T(8,128)(2,1)S(1)}, bf16[256,1536]{1,0:T(8,128)(2,1)S(1)}, u32[]{:S(2)}, u32[]{:S(2)}) %collective-permute-start.125) | collective-permute-done | bytes 786464 | tf_op jit(solution)/shard_map/ppermute | solution.py:68
  1049.4 13.4 %collective-permute-done.143 = bf16[64,1536]{1,0:T(8,128)(2,1)S(1)} collective-permute-done((bf16[64,1536]{1,0:T(8,128)(2,1)S(1)}, bf16[64,1536]{1,0:T(8,128)(2,1)S(1)}, u32[]{:S(2)}, u32[]{:S(2)}) %collective-permute-start.143) | collective-permute-done | bytes 196640 | tf_op jit(solution)/shard_map/ppermute | solution.py:160
  (1059 shorter events, 686.1 us)
Async XLA Ops:
  7.2 219.6 %all-gather.5.cloned.1.call-start = ((), (), s32[]{:S(2)}) async-start(), calls=%async_computation.4 | async-start | bytes 7962624 | tf_op jit(solution)/shard_map/all_gather | solution.py:705
  46.9 39.2 %collective-permute-start.19 = (bf16[256,1536]{1,0:T(8,128)(2,1)S(1)}, bf16[256,1536]{1,0:T(8,128)(2,1)S(1)}, u32[]{:S(2)}, u32[]{:S(2)}) collective-permute-start(bf16[256,1536]{1,0:T(8,128)(2,1)S(1)} %bitcast.584), channel_id=1, source_target_pairs={{0,1},{1,0},{2,3},{3,2},{4,5},{5,4},{6,7},{7,6},{8,9},{9,8},{10,11... | collective-permute-start | bytes 2359304 | tf_op jit(solution)/shard_map/ppermute | solution.py:68
  51.2 34.9 %collective-permute-start.21 = (bf16[256,1536]{1,0:T(8,128)(2,1)}, bf16[256,1536]{1,0:T(8,128)(2,1)S(1)}, u32[]{:S(2)}, u32[]{:S(2)}) collective-permute-start(bf16[256,1536]{1,0:T(8,128)(2,1)} %collective-permute-done.20), channel_id=1, source_target_pairs={{0,1},{1,0},{2,3},{3,2},{4,5},{5,4},{6,7},{7,6},{8,9},{9,8},{10,11... | collective-permute-start | bytes 2359304 | tf_op jit(solution)/shard_map/ppermute | solution.py:68
  93.7 213.7 %all-gather.7.cloned.1.call-start = ((), (), s32[]{:S(2)}) async-start(), calls=%async_computation.5 | async-start | bytes 3981312 | tf_op jit(solution)/shard_map/all_gather | solution.py:702
  126.4 51.3 %collective-permute-start.33 = (bf16[48,1152]{1,0:T(8,128)(2,1)}, bf16[48,1152]{1,0:T(8,128)(2,1)}, u32[]{:S(2)}, u32[]{:S(2)}) collective-permute-start(bf16[48,1152]{1,0:T(8,128)(2,1)} %get-tuple-element.535), channel_id=1, source_target_pairs={{0,1},{1,0},{2,3},{3,2},{4,5},{5,4},{6,7},{7,6},{8,9},{9,8},{10,11... | collective-permute-start | bytes 331784 | tf_op jit(solution)/shard_map/ppermute | solution.py:68
  127.2 50.8 %collective-permute-start.34 = (bf16[48,1152]{1,0:T(8,128)(2,1)}, bf16[48,1152]{1,0:T(8,128)(2,1)}, u32[]{:S(2)}, u32[]{:S(2)}) collective-permute-start(bf16[48,1152]{1,0:T(8,128)(2,1)} %get-tuple-element.534), channel_id=1, source_target_pairs={{0,2},{1,3},{2,0},{3,1},{4,6},{5,7},{6,4},{7,5},{8,10},{9,11},{10,... | collective-permute-start | bytes 331784 | tf_op jit(solution)/shard_map/ppermute | solution.py:68
  128.4 53.2 %collective-permute-start.35 = (bf16[48,1152]{1,0:T(8,128)(2,1)}, bf16[48,1152]{1,0:T(8,128)(2,1)}, u32[]{:S(2)}, u32[]{:S(2)}) collective-permute-start(bf16[48,1152]{1,0:T(8,128)(2,1)} %get-tuple-element.533), channel_id=1, source_target_pairs={{0,3},{1,2},{2,1},{3,0},{4,7},{5,6},{6,5},{7,4},{8,11},{9,10},{10,... | collective-permute-start | bytes 331784 | tf_op jit(solution)/shard_map/ppermute | solution.py:68
  142.0 312.3 %all-gather.9.cloned.1.call-start = ((), (), s32[]{:S(2)}) async-start(), calls=%async_computation.6 | async-start | bytes 7962624 | tf_op jit(solution)/shard_map/all_gather | solution.py:705
  207.4 298.3 %all-gather.11.cloned.1.call-start = ((), (), s32[]{:S(2)}) async-start(), calls=%async_computation.7 | async-start | bytes 3981312 | tf_op jit(solution)/shard_map/all_gather | solution.py:702
  233.2 28.6 %collective-permute-start.47 = (bf16[192,1152]{1,0:T(8,128)(2,1)}, bf16[192,1152]{1,0:T(8,128)(2,1)S(1)}, u32[]{:S(2)}, u32[]{:S(2)}) collective-permute-start(bf16[192,1152]{1,0:T(8,128)(2,1)} %collective-permute-done.40), channel_id=1, source_target_pairs={{4,0},{12,4},{20,12},{28,20},{24,28},{16,24},{8,16},{0,8},{5,1},{1... | collective-permute-start | bytes 1327112 | tf_op jit(solution)/shard_map/ppermute | solution.py:125
  233.4 28.4 %collective-permute-start.48 = (bf16[192,1152]{1,0:T(8,128)(2,1)}, bf16[192,1152]{1,0:T(8,128)(2,1)S(1)}, u32[]{:S(2)}, u32[]{:S(2)}) collective-permute-start(bf16[192,1152]{1,0:T(8,128)(2,1)} %collective-permute-done.41), channel_id=1, source_target_pairs={{0,4},{4,12},{12,20},{20,28},{28,24},{24,16},{16,8},{8,0},{1,5},{5... | collective-permute-start | bytes 1327112 | tf_op jit(solution)/shard_map/ppermute | solution.py:127
  261.8 40.8 %collective-permute-start.51 = (bf16[192,1152]{1,0:T(8,128)(2,1)S(1)}, bf16[192,1152]{1,0:T(8,128)(2,1)S(1)}, u32[]{:S(2)}, u32[]{:S(2)}) collective-permute-start(bf16[192,1152]{1,0:T(8,128)(2,1)S(1)} %collective-permute-done.47), channel_id=1, source_target_pairs={{4,0},{12,4},{20,12},{28,20},{24,28},{16,24},{8,16},{0,8},{5,1},{1... | collective-permute-start | bytes 1327112 | tf_op jit(solution)/shard_map/ppermute | solution.py:125
  262.3 40.3 %collective-permute-start.52 = (bf16[192,1152]{1,0:T(8,128)(2,1)S(1)}, bf16[192,1152]{1,0:T(8,128)(2,1)S(1)}, u32[]{:S(2)}, u32[]{:S(2)}) collective-permute-start(bf16[192,1152]{1,0:T(8,128)(2,1)S(1)} %collective-permute-done.48), channel_id=1, source_target_pairs={{0,4},{4,12},{12,20},{20,28},{28,24},{24,16},{16,8},{8,0},{1,5},{5... | collective-permute-start | bytes 1327112 | tf_op jit(solution)/shard_map/ppermute | solution.py:127
  263.6 28.1 %collective-permute-start.53 = (bf16[64,1536]{1,0:T(8,128)(2,1)S(1)}, bf16[64,1536]{1,0:T(8,128)(2,1)S(1)}, u32[]{:S(2)}, u32[]{:S(2)}) collective-permute-start(bf16[64,1536]{1,0:T(8,128)(2,1)S(1)} %collective-permute-done.49), channel_id=1, source_target_pairs={{0,4},{4,12},{12,20},{20,28},{28,24},{24,16},{16,8},{8,0},{1,5},{5... | collective-permute-start | bytes 589832 | tf_op jit(solution)/shard_map/ppermute | solution.py:125
  265.0 37.6 %collective-permute-start.54 = (bf16[64,1536]{1,0:T(8,128)(2,1)S(1)}, bf16[64,1536]{1,0:T(8,128)(2,1)S(1)}, u32[]{:S(2)}, u32[]{:S(2)}) collective-permute-start(bf16[64,1536]{1,0:T(8,128)(2,1)S(1)} %collective-permute-done.50), channel_id=1, source_target_pairs={{4,0},{12,4},{20,12},{28,20},{24,28},{16,24},{8,16},{0,8},{5,1},{1... | collective-permute-start | bytes 589832 | tf_op jit(solution)/shard_map/ppermute | solution.py:127
  431.9 285.6 %reduce-scatter.5.cloned.1.call-start = ((), (), s32[]{:S(2)}) async-start(), calls=%async_computation.8 | async-start | bytes 3981312 | tf_op jit(solution)/shard_map/reduce_scatter | solution.py:790
  432.0 36.0 %collective-permute-start.75 = (bf16[256,1536]{1,0:T(8,128)(2,1)}, bf16[256,1536]{1,0:T(8,128)(2,1)}, u32[]{:S(2)}, u32[]{:S(2)}) collective-permute-start(bf16[256,1536]{1,0:T(8,128)(2,1)} %bitcast.598), channel_id=1, source_target_pairs={{0,2},{1,3},{2,0},{3,1},{4,6},{5,7},{6,4},{7,5},{8,10},{9,11},{10,... | collective-permute-start | bytes 2359304 | tf_op jit(solution)/shard_map/ppermute | solution.py:68
  456.7 28.2 %collective-permute-start.78 = (bf16[256,1536]{1,0:T(8,128)(2,1)S(1)}, bf16[256,1536]{1,0:T(8,128)(2,1)S(1)}, u32[]{:S(2)}, u32[]{:S(2)}) collective-permute-start(bf16[256,1536]{1,0:T(8,128)(2,1)S(1)} %multiply_convert_fusion.4), channel_id=1, source_target_pairs={{0,2},{1,3},{2,0},{3,1},{4,6},{5,7},{6,4},{7,5},{8,10},{9,11},{10,... | collective-permute-start | bytes 2359304 | tf_op jit(solution)/shard_map/ppermute | solution.py:68
  457.1 28.7 %collective-permute-start.74 = (bf16[256,1536]{1,0:T(8,128)(2,1)S(1)}, bf16[256,1536]{1,0:T(8,128)(2,1)S(1)}, u32[]{:S(2)}, u32[]{:S(2)}) collective-permute-start(bf16[256,1536]{1,0:T(8,128)(2,1)S(1)} %bitcast.599), channel_id=1, source_target_pairs={{0,1},{1,0},{2,3},{3,2},{4,5},{5,4},{6,7},{7,6},{8,9},{9,8},{10,11... | collective-permute-start | bytes 2359304 | tf_op jit(solution)/shard_map/ppermute | solution.py:68
  529.9 234.3 %reduce-scatter.7.cloned.1.call-start = ((), (), s32[]{:S(2)}) async-start(), calls=%async_computation.9 | async-start | bytes 7962624 | tf_op jit(solution)/shard_map/reduce_scatter | solution.py:787
  588.5 378.3 %reduce-scatter.9.cloned.1.call-start = ((), (), s32[]{:S(2)}) async-start(), calls=%async_computation.10 | async-start | bytes 7962624 | tf_op jit(solution)/shard_map/reduce_scatter | solution.py:787
  750.9 282.4 %reduce-scatter.11.cloned.1.call-start = ((), (), s32[]{:S(2)}) async-start(), calls=%async_computation.11 | async-start | bytes 3981312 | tf_op jit(solution)/shard_map/reduce_scatter | solution.py:790
  753.0 36.3 %collective-permute-start.100 = (bf16[192,1152]{1,0:T(8,128)(2,1)}, bf16[192,1152]{1,0:T(8,128)(2,1)}, u32[]{:S(2)}, u32[]{:S(2)}) collective-permute-start(bf16[192,1152]{1,0:T(8,128)(2,1)} %get-tuple-element.313), channel_id=1, source_target_pairs={{0,4},{4,12},{12,20},{20,28},{28,24},{24,16},{16,8},{8,0},{1,5},{5... | collective-permute-start | bytes 1327112 | tf_op jit(solution)/shard_map/ppermute | solution.py:160
  753.0 36.3 %collective-permute-start.101 = (bf16[192,1152]{1,0:T(8,128)(2,1)S(1)}, bf16[192,1152]{1,0:T(8,128)(2,1)}, u32[]{:S(2)}, u32[]{:S(2)}) collective-permute-start(bf16[192,1152]{1,0:T(8,128)(2,1)S(1)} %get-tuple-element.314), channel_id=1, source_target_pairs={{4,0},{12,4},{20,12},{28,20},{24,28},{16,24},{8,16},{0,8},{5,1},{1... | collective-permute-start | bytes 1327112 | tf_op jit(solution)/shard_map/ppermute | solution.py:162
  754.5 34.8 %collective-permute-start.102 = (bf16[64,1536]{1,0:T(8,128)(2,1)}, bf16[64,1536]{1,0:T(8,128)(2,1)}, u32[]{:S(2)}, u32[]{:S(2)}) collective-permute-start(bf16[64,1536]{1,0:T(8,128)(2,1)} %get-tuple-element.315), channel_id=1, source_target_pairs={{4,0},{12,4},{20,12},{28,20},{24,28},{16,24},{8,16},{0,8},{5,1},{1... | collective-permute-start | bytes 589832 | tf_op jit(solution)/shard_map/ppermute | solution.py:160
  754.5 34.8 %collective-permute-start.103 = (bf16[64,1536]{1,0:T(8,128)(2,1)S(1)}, bf16[64,1536]{1,0:T(8,128)(2,1)}, u32[]{:S(2)}, u32[]{:S(2)}) collective-permute-start(bf16[64,1536]{1,0:T(8,128)(2,1)S(1)} %copy-done.133), channel_id=1, source_target_pairs={{0,4},{4,12},{12,20},{20,28},{28,24},{24,16},{16,8},{8,0},{1,5},{5... | collective-permute-start | bytes 589832 | tf_op jit(solution)/shard_map/ppermute | solution.py:162
  762.8 46.1 %collective-permute-start.87 = (bf16[256,1536]{1,0:T(8,128)(2,1)}, bf16[256,1536]{1,0:T(8,128)(2,1)}, u32[]{:S(2)}, u32[]{:S(2)}) collective-permute-start(bf16[256,1536]{1,0:T(8,128)(2,1)} %slice.673), channel_id=1, source_target_pairs={{0,1},{1,0},{2,3},{3,2},{4,5},{5,4},{6,7},{7,6},{8,9},{9,8},{10,11... | collective-permute-start | bytes 2359304 | tf_op jit(solution)/shard_map/ppermute | solution.py:68
  810.3 30.5 %collective-permute-start.88 = (bf16[256,1536]{1,0:T(8,128)(2,1)S(1)}, bf16[256,1536]{1,0:T(8,128)(2,1)S(1)}, u32[]{:S(2)}, u32[]{:S(2)}) collective-permute-start(bf16[256,1536]{1,0:T(8,128)(2,1)S(1)} %add_convert_fusion.4), channel_id=1, source_target_pairs={{0,2},{1,3},{2,0},{3,1},{4,6},{5,7},{6,4},{7,5},{8,10},{9,11},{10,... | collective-permute-start | bytes 2359304 | tf_op jit(solution)/shard_map/ppermute | solution.py:68
  827.2 30.5 %collective-permute-start.108 = (bf16[256,1536]{1,0:T(8,128)(2,1)}, bf16[256,1536]{1,0:T(8,128)(2,1)}, u32[]{:S(2)}, u32[]{:S(2)}) collective-permute-start(bf16[256,1536]{1,0:T(8,128)(2,1)} %get-tuple-element.436), channel_id=1, source_target_pairs={{0,2},{1,3},{2,0},{3,1},{4,6},{5,7},{6,4},{7,5},{8,10},{9,11},{10,... | collective-permute-start | bytes 2359304 | tf_op jit(solution)/shard_map/ppermute | solution.py:68
  868.8 32.9 %collective-permute-start.111 = (bf16[192,1152]{1,0:T(8,128)(2,1)}, bf16[192,1152]{1,0:T(8,128)(2,1)S(1)}, u32[]{:S(2)}, u32[]{:S(2)}) collective-permute-start(bf16[192,1152]{1,0:T(8,128)(2,1)} %get-tuple-element.458), channel_id=1, source_target_pairs={{4,0},{12,4},{20,12},{28,20},{24,28},{16,24},{8,16},{0,8},{5,1},{1... | collective-permute-start | bytes 1327112 | tf_op jit(solution)/shard_map/ppermute | solution.py:162
  1037.1 72.8 %collective-permute-start.154 = (f32[64,1536]{1,0:T(8,128)}, f32[64,1536]{1,0:T(8,128)}, u32[]{:S(2)}, u32[]{:S(2)}) collective-permute-start(f32[64,1536]{1,0:T(8,128)} %fusion.83), channel_id=1, source_target_pairs={{0,0},{4,1},{1,2},{5,3},{2,4},{6,5},{3,6},{7,7},{8,8},{12,9},{9,10... | collective-permute-start | bytes 1179656 | tf_op jit(solution)/shard_map/ppermute | solution.py:287
  1082.6 27.3 %collective-permute-start.153 = (f32[64,1536]{1,0:T(8,128)}, f32[64,1536]{1,0:T(8,128)}, u32[]{:S(2)}, u32[]{:S(2)}) collective-permute-start(f32[64,1536]{1,0:T(8,128)} %fusion.85), channel_id=1, source_target_pairs={{0,0},{4,1},{1,2},{5,3},{2,4},{6,5},{3,6},{7,7},{8,8},{12,9},{9,10... | collective-permute-start | bytes 1179656 | tf_op jit(solution)/shard_map/ppermute | solution.py:287
  (313 other events, 3930.7 us)
Sparse Core Ops, SparseCore 0:
  93.8 123.4 all-gather.4
  219.5 87.8 all-gather.6
  309.5 119.1 all-gather.8
  432.0 65.0 all-gather.10
  530.0 77.4 reduce-scatter.4
  611.0 129.4 reduce-scatter.6
  751.1 152.6 reduce-scatter.8
  907.4 86.9 reduce-scatter.10

commit v5 on v3

--- a/solution.py
+++ b/solution.py
@@ -800,6 +800,7 @@
         ends = end(ends)
     ends = pump.hold(ends)
     back = carry_in(kept["whole"], ends, -1)
+    pump.add(ScatterJob(grad_out.reshape(n, -1, width), True, lambda total: results.update(out=from_heads(total))))
     back = pump.step(back)
     d_stream, tail, head, d_gates, d_taps, d_decay = mix_back(
         streams, dh, kept["a"], kept["h"], kept["start"], back, kept["conv"], kept["stream"], kept["halo"], keep,
@@ -836,7 +837,6 @@
         part, results["wide"] = tie(part, results["wide"])
     pump.add(
         both,
-        ScatterJob(grad_out.reshape(n, -1, width), True, lambda total: results.update(out=from_heads(total))),
     )
     d_normed = tp_scatter(pump.step(part))
     if end is None:
@@ -936,10 +936,10 @@
         jobs.append(both)
     pump.complete(jobs[:-1])
     held = [found.pop("raw") for found in results[1:]]
-    wide = [found["wide"] for found in results[1:]]
-    held, wide = pump.step(pump.step((held, wide)))
-    for layer in range(1, layers):
-        results[layer]["wide"] = wide[layer - 1]
+    held, wide = pump.step((held, [found["wide"] for found in results]))
+    for found, total in zip(results, wide):
+        found["wide"] = total
+    held = pump.step(held)
     pump.finish()
     for layer in reversed(range(layers)):
         raw = held[layer - 1] if layer else results[0].pop("raw")

time: 1110 us -> 1130 us (1.018)
    ppermute x77, waiting for transfers between devices: 265 us -> 252 us  [swap(): return lax.ppermute(x, 'wt', [(i, i ^ k) for i in range(TP)])]
    ppermute x24, waiting for transfers between devices: 36.3 us -> 48.3 us  [start(): flight.append(lax.ppermute(self.b, 'seq', self.routes[1]))]
  transfers between devices with their start and end apart: 169 -> 169, of which waited for: 60 -> 70; matrix products, arithmetic and copies ran while one was open for 30% -> 30% of each run, Pallas kernels for 6% -> 6%
where the time goes in v5:
time: 1130 us; the launch traced here: 1120 us
  waiting for transfers between devices  440 us (39%)
  starting transfers between devices  212 us (19%)
  matrix products  183 us (16%)
  other arithmetic  110 us (10%)
  local copies, waits for them, and re-layouts  89.1 us (8%)
  Pallas kernels  65.8 us (6%)
  between operations  18.4 us (2%)
    ppermute x77, waiting for transfers between devices, swap(): return lax.ppermute(x, 'wt', [(i, i ^ k) for i in range(TP)])  252 us
    ppermute x32, waiting for transfers between devices, start(): flight = [lax.ppermute(self.a, 'seq', self.routes[0])]  108 us
    ppermute x77, starting transfers between devices, swap(): return lax.ppermute(x, 'wt', [(i, i ^ k) for i in range(TP)])  103 us
    dot_general x10, matrix products, dot_t(): lax.dot_general(left, right, (((1,), (1,)), ((), ())), preferred_element_...  72.4 us
    dot_general x10, matrix products, dot_tokens(): lax.dot_general(left, right, (((0,), (0,)), ((), ())), preferred_element_...  57.7 us
    dot_general x12, matrix products, dot(): lax.dot_general(left, right, (((1,), (0,)), ((), ())), preferred_element_...  53.3 us
    ppermute x21, starting transfers between devices, shift_seq(): lax.ppermute(x, 'seq', [(i, i + distance) for i in range(n) if 0 <= i + d...  52.3 us
    ppermute x24, waiting for transfers between devices, start(): flight.append(lax.ppermute(self.b, 'seq', self.routes[1]))  48.3 us
  transfers between devices with their start and end apart: 169, of which 70 were waited for; matrix products, arithmetic and copies ran while one was open for 30% of the time, Pallas kernels for 6%

profile of v5, /device:TPU:3, one launch (start us, length us, event | category | flops | bytes accessed | tf_op | source)
XLA Modules:
  0.0 1118.6 jit_solution(9299459133285930770)
XLA Ops:
  50.1 8.8 collective-permute-done.20
  69.4 12.0 %collective-permute-done.17 = bf16[64,1536]{1,0:T(8,128)(2,1)S(1)} collective-permute-done((bf16[64,1536]{1,0:T(8,128)(2,1)S(1)}, bf16[64,1536]{1,0:T(8,128)(2,1)S(1)}, u32[]{:S(2)}, u32[]{:S(2)}) %collective-permute-start.17) | collective-permute-done | bytes 196640 | tf_op jit(solution)/shard_map/ppermute | solution.py:120
  161.3 8.8 shard_map.238
  209.8 17.4 %collective-permute-done.39 = bf16[256,1536]{1,0:T(8,128)(2,1)} collective-permute-done((bf16[256,1536]{1,0:T(8,128)(2,1)}, bf16[256,1536]{1,0:T(8,128)(2,1)}, u32[]{:S(2)}, u32[]{:S(2)}) %collective-permute-start.39) | collective-permute-done | bytes 786464 | tf_op jit(solution)/shard_map/ppermute | solution.py:68
  240.0 12.4 %collective-permute-done.45 = bf16[256,1536]{1,0:T(8,128)(2,1)S(1)} collective-permute-done((bf16[256,1536]{1,0:T(8,128)(2,1)S(1)}, bf16[256,1536]{1,0:T(8,128)(2,1)S(1)}, u32[]{:S(2)}, u32[]{:S(2)}) %collective-permute-start.45) | collective-permute-done | bytes 786464 | tf_op jit(solution)/shard_map/ppermute | solution.py:68
  256.9 14.2 %collective-permute-done.50 = bf16[64,1536]{1,0:T(8,128)(2,1)S(1)} collective-permute-done((bf16[64,1536]{1,0:T(8,128)(2,1)S(1)}, bf16[64,1536]{1,0:T(8,128)(2,1)S(1)}, u32[]{:S(2)}, u32[]{:S(2)}) %collective-permute-start.50) | collective-permute-done | bytes 196640 | tf_op jit(solution)/shard_map/ppermute | solution.py:122
  281.9 15.7 %collective-permute-done.53 = bf16[64,1536]{1,0:T(8,128)(2,1)} collective-permute-done((bf16[64,1536]{1,0:T(8,128)(2,1)S(1)}, bf16[64,1536]{1,0:T(8,128)(2,1)}, u32[]{:S(2)}, u32[]{:S(2)}) %collective-permute-start.53) | collective-permute-done | bytes 196640 | tf_op jit(solution)/shard_map/ppermute | solution.py:120
  320.7 15.3 %collective-permute-done.57 = bf16[256,1536]{1,0:T(8,128)(2,1)S(1)} collective-permute-done((bf16[256,1536]{1,0:T(8,128)(2,1)S(1)}, bf16[256,1536]{1,0:T(8,128)(2,1)S(1)}, u32[]{:S(2)}, u32[]{:S(2)}) %collective-permute-start.57) | collective-permute-done | bytes 786464 | tf_op jit(solution)/shard_map/ppermute | solution.py:68
  336.4 9.6 collective-permute-done.58
  355.9 14.4 %collective-permute-done.61 = bf16[256,1536]{1,0:T(8,128)(2,1)} collective-permute-done((bf16[256,1536]{1,0:T(8,128)(2,1)}, bf16[256,1536]{1,0:T(8,128)(2,1)}, u32[]{:S(2)}, u32[]{:S(2)}) %collective-permute-start.61) | collective-permute-done | bytes 786464 | tf_op jit(solution)/shard_map/ppermute | solution.py:68
  387.9 8.9 shard_map.240
  430.7 17.4 %collective-permute-done.70 = bf16[256,1536]{1,0:T(8,128)(2,1)} collective-permute-done((bf16[256,1536]{1,0:T(8,128)(2,1)}, bf16[256,1536]{1,0:T(8,128)(2,1)}, u32[]{:S(2)}, u32[]{:S(2)}) %collective-permute-start.70) | collective-permute-done | bytes 786464 | tf_op jit(solution)/shard_map/ppermute | solution.py:68
  466.9 14.8 %collective-permute-done.78 = bf16[256,1536]{1,0:T(8,128)(2,1)S(1)} collective-permute-done((bf16[256,1536]{1,0:T(8,128)(2,1)S(1)}, bf16[256,1536]{1,0:T(8,128)(2,1)S(1)}, u32[]{:S(2)}, u32[]{:S(2)}) %collective-permute-start.78) | collective-permute-done | bytes 786464 | tf_op jit(solution)/shard_map/ppermute | solution.py:68
  502.8 11.1 multiply_convert_fusion.3
  517.1 9.8 convolution_convert_fusion.1
  527.1 11.4 %convolution_convert_fusion.5 = bf16[1024,1536]{1,0:T(8,128)(2,1)S(1)} fusion(bf16[1024,2304]{1,0:T(8,128)(2,1)} %pad_maximum_fusion, bf16[1536,2304]{1,0:T(8,128)(2,1)} %all-gather.9.cloned.1.call-done), kind=kOutput, calls=%fused_computation.34 | convolution fusion | flops 7249330176 | bytes 14942208 | tf_op jit(solution)/shard_map/dot_general | solution.py:27
  542.4 17.7 %collective-permute-done.82 = bf16[256,1536]{1,0:T(8,128)(2,1)S(1)} collective-permute-done((bf16[256,1536]{1,0:T(8,128)(2,1)S(1)}, bf16[256,1536]{1,0:T(8,128)(2,1)S(1)}, u32[]{:S(2)}, u32[]{:S(2)}) %collective-permute-start.82) | collective-permute-done | bytes 786464 | tf_op jit(solution)/shard_map/ppermute | solution.py:68
  565.4 15.7 %collective-permute-done.84 = bf16[256,1536]{1,0:T(8,128)(2,1)} collective-permute-done((bf16[256,1536]{1,0:T(8,128)(2,1)}, bf16[256,1536]{1,0:T(8,128)(2,1)}, u32[]{:S(2)}, u32[]{:S(2)}) %collective-permute-start.84) | collective-permute-done | bytes 786464 | tf_op jit(solution)/shard_map/ppermute | solution.py:68
  623.8 15.4 %shard_map.244 = (bf16[1024,512]{1,0:T(8,128)(2,1)S(1)}, f32[24,512]{1,0:T(8,128)S(1)}, f32[24,512]{1,0:T(8,128)}, f32[4,128,256]{2,1,0:T(8,128)S(1)}, f32[4,512]{1,0:T(4,128)S(1)}, /*index=5*/f32[1,512]{1,0:T(1,128)S(1)}) custom-call(f32[1024,512]{1,0:T(8,128)S(1)} %get-tuple-element.297.dh_ref, f32[1024,512]{1,0:T(8,128)S(1)} %get-tuple-element.277.a_ref, ...), custom_call_target="tpu_custom_call" | custom-call | flops 629145600 | bytes 11534336 | tf_op jit(solution)/shard_map/pallas_call | solution.py:562
  670.3 17.7 %collective-permute-done.98 = bf16[256,1536]{1,0:T(8,128)(2,1)S(1)} collective-permute-done((bf16[256,1536]{1,0:T(8,128)(2,1)S(1)}, bf16[256,1536]{1,0:T(8,128)(2,1)S(1)}, u32[]{:S(2)}, u32[]{:S(2)}) %collective-permute-start.98) | collective-permute-done | bytes 786464 | tf_op jit(solution)/shard_map/ppermute | solution.py:68
  693.0 15.4 %collective-permute-done.100 = bf16[256,1536]{1,0:T(8,128)(2,1)S(1)} collective-permute-done((bf16[256,1536]{1,0:T(8,128)(2,1)S(1)}, bf16[256,1536]{1,0:T(8,128)(2,1)S(1)}, u32[]{:S(2)}, u32[]{:S(2)}) %collective-permute-start.100) | collective-permute-done | bytes 786464 | tf_op jit(solution)/shard_map/ppermute | solution.py:68
  716.3 8.5 convolution_convert_fusion.2
  734.9 10.2 convolution_convert_fusion
  749.5 11.1 convolution_convert_fusion.4
  789.9 9.5 collective-permute-done.108
  807.2 14.3 %collective-permute-done.110 = bf16[256,1536]{1,0:T(8,128)(2,1)} collective-permute-done((bf16[256,1536]{1,0:T(8,128)(2,1)}, bf16[256,1536]{1,0:T(8,128)(2,1)}, u32[]{:S(2)}, u32[]{:S(2)}) %collective-permute-start.110) | collective-permute-done | bytes 786464 | tf_op jit(solution)/shard_map/ppermute | solution.py:68
  842.2 11.1 collective-permute-done.112
  885.6 14.7 %shard_map.246 = (bf16[1024,512]{1,0:T(8,128)(2,1)S(1)}, f32[24,512]{1,0:T(8,128)S(1)}, f32[24,512]{1,0:T(8,128)S(1)}, f32[4,128,256]{2,1,0:T(8,128)S(1)}, f32[4,512]{1,0:T(4,128)S(1)}, /*index=5*/f32[1,512]{1,0:T(1,128)S(1)}) custom-call(f32[1024,512]{1,0:T(8,128)S(1)} %get-tuple-element.327.dh_ref, f32[1024,512]{1,0:T(8,128)S(1)} %copy-done.1, ...), custom_call_target="tpu_custom_call" | custom-call | flops 629145600 | bytes 11534336 | tf_op jit(solution)/shard_map/pallas_call | solution.py:562
  921.2 15.3 %collective-permute-done.121 = bf16[64,1536]{1,0:T(8,128)(2,1)} collective-permute-done((bf16[64,1536]{1,0:T(8,128)(2,1)}, bf16[64,1536]{1,0:T(8,128)(2,1)}, u32[]{:S(2)}, u32[]{:S(2)}) %collective-permute-start.121) | collective-permute-done | bytes 196640 | tf_op jit(solution)/shard_map/ppermute | solution.py:155
  937.6 9.0 collective-permute-done.124
  972.5 13.6 %collective-permute-done.128 = bf16[256,1536]{1,0:T(8,128)(2,1)S(1)} collective-permute-done((bf16[256,1536]{1,0:T(8,128)(2,1)S(1)}, bf16[256,1536]{1,0:T(8,128)(2,1)S(1)}, u32[]{:S(2)}, u32[]{:S(2)}) %collective-permute-start.128) | collective-permute-done | bytes 786464 | tf_op jit(solution)/shard_map/ppermute | solution.py:68
  989.5 12.0 %collective-permute-done.132 = bf16[192,1152]{1,0:T(8,128)(2,1)S(1)} collective-permute-done((bf16[192,1152]{1,0:T(8,128)(2,1)S(1)}, bf16[192,1152]{1,0:T(8,128)(2,1)S(1)}, u32[]{:S(2)}, u32[]{:S(2)}) %collective-permute-start.132) | collective-permute-done | bytes 442400 | tf_op jit(solution)/shard_map/ppermute | solution.py:155
  (1023 shorter events, 687.2 us)
Async XLA Ops:
  7.2 223.1 %all-gather.5.cloned.1.call-start = ((), (), s32[]{:S(2)}) async-start(), calls=%async_computation.4 | async-start | bytes 7962624 | tf_op jit(solution)/shard_map/all_gather | solution.py:700
  48.4 39.8 %collective-permute-start.19 = (bf16[256,1536]{1,0:T(8,128)(2,1)S(1)}, bf16[256,1536]{1,0:T(8,128)(2,1)S(1)}, u32[]{:S(2)}, u32[]{:S(2)}) collective-permute-start(bf16[256,1536]{1,0:T(8,128)(2,1)S(1)} %bitcast.626), channel_id=1, source_target_pairs={{0,1},{1,0},{2,3},{3,2},{4,5},{5,4},{6,7},{7,6},{8,9},{9,8},{10,11... | collective-permute-start | bytes 2359304 | tf_op jit(solution)/shard_map/ppermute | solution.py:68
  58.9 29.3 %collective-permute-start.21 = (bf16[256,1536]{1,0:T(8,128)(2,1)S(1)}, bf16[256,1536]{1,0:T(8,128)(2,1)S(1)}, u32[]{:S(2)}, u32[]{:S(2)}) collective-permute-start(bf16[256,1536]{1,0:T(8,128)(2,1)S(1)} %collective-permute-done.20), channel_id=1, source_target_pairs={{0,1},{1,0},{2,3},{3,2},{4,5},{5,4},{6,7},{7,6},{8,9},{9,8},{10,11... | collective-permute-start | bytes 2359304 | tf_op jit(solution)/shard_map/ppermute | solution.py:68
  95.7 211.0 %all-gather.7.cloned.1.call-start = ((), (), s32[]{:S(2)}) async-start(), calls=%async_computation.5 | async-start | bytes 3981312 | tf_op jit(solution)/shard_map/all_gather | solution.py:697
  133.1 49.6 %collective-permute-start.33 = (bf16[48,1152]{1,0:T(8,128)(2,1)}, bf16[48,1152]{1,0:T(8,128)(2,1)}, u32[]{:S(2)}, u32[]{:S(2)}) collective-permute-start(bf16[48,1152]{1,0:T(8,128)(2,1)} %get-tuple-element.555), channel_id=1, source_target_pairs={{0,1},{1,0},{2,3},{3,2},{4,5},{5,4},{6,7},{7,6},{8,9},{9,8},{10,11... | collective-permute-start | bytes 331784 | tf_op jit(solution)/shard_map/ppermute | solution.py:68
  133.8 50.2 %collective-permute-start.34 = (bf16[48,1152]{1,0:T(8,128)(2,1)}, bf16[48,1152]{1,0:T(8,128)(2,1)}, u32[]{:S(2)}, u32[]{:S(2)}) collective-permute-start(bf16[48,1152]{1,0:T(8,128)(2,1)} %get-tuple-element.554), channel_id=1, source_target_pairs={{0,2},{1,3},{2,0},{3,1},{4,6},{5,7},{6,4},{7,5},{8,10},{9,11},{10,... | collective-permute-start | bytes 331784 | tf_op jit(solution)/shard_map/ppermute | solution.py:68
  134.0 50.0 %collective-permute-start.35 = (bf16[48,1152]{1,0:T(8,128)(2,1)}, bf16[48,1152]{1,0:T(8,128)(2,1)}, u32[]{:S(2)}, u32[]{:S(2)}) collective-permute-start(bf16[48,1152]{1,0:T(8,128)(2,1)} %get-tuple-element.553), channel_id=1, source_target_pairs={{0,3},{1,2},{2,1},{3,0},{4,7},{5,6},{6,5},{7,4},{8,11},{9,10},{10,... | collective-permute-start | bytes 331784 | tf_op jit(solution)/shard_map/ppermute | solution.py:68
  155.5 295.6 %all-gather.9.cloned.1.call-start = ((), (), s32[]{:S(2)}) async-start(), calls=%async_computation.6 | async-start | bytes 7962624 | tf_op jit(solution)/shard_map/all_gather | solution.py:700
  200.0 30.4 %collective-permute-start.40 = (bf16[192,1152]{1,0:T(8,128)(2,1)S(1)}, bf16[192,1152]{1,0:T(8,128)(2,1)S(1)}, u32[]{:S(2)}, u32[]{:S(2)}) collective-permute-start(bf16[192,1152]{1,0:T(8,128)(2,1)S(1)} %bitcast.656), channel_id=1, source_target_pairs={{4,0},{12,4},{20,12},{28,20},{24,28},{16,24},{8,16},{0,8},{5,1},{1... | collective-permute-start | bytes 1327112 | tf_op jit(solution)/shard_map/ppermute | solution.py:120
  209.7 293.1 %all-gather.11.cloned.1.call-start = ((), (), s32[]{:S(2)}) async-start(), calls=%async_computation.7 | async-start | bytes 3981312 | tf_op jit(solution)/shard_map/all_gather | solution.py:697
  235.4 35.8 %collective-permute-start.47 = (bf16[192,1152]{1,0:T(8,128)(2,1)S(1)}, bf16[192,1152]{1,0:T(8,128)(2,1)S(1)}, u32[]{:S(2)}, u32[]{:S(2)}) collective-permute-start(bf16[192,1152]{1,0:T(8,128)(2,1)S(1)} %collective-permute-done.40), channel_id=1, source_target_pairs={{4,0},{12,4},{20,12},{28,20},{24,28},{16,24},{8,16},{0,8},{5,1},{1... | collective-permute-start | bytes 1327112 | tf_op jit(solution)/shard_map/ppermute | solution.py:120
  235.4 35.8 %collective-permute-start.48 = (bf16[192,1152]{1,0:T(8,128)(2,1)}, bf16[192,1152]{1,0:T(8,128)(2,1)S(1)}, u32[]{:S(2)}, u32[]{:S(2)}) collective-permute-start(bf16[192,1152]{1,0:T(8,128)(2,1)} %collective-permute-done.41), channel_id=1, source_target_pairs={{0,4},{4,12},{12,20},{20,28},{28,24},{24,16},{16,8},{8,0},{1,5},{5... | collective-permute-start | bytes 1327112 | tf_op jit(solution)/shard_map/ppermute | solution.py:122
  271.2 32.8 %collective-permute-start.51 = (bf16[192,1152]{1,0:T(8,128)(2,1)S(1)}, bf16[192,1152]{1,0:T(8,128)(2,1)S(1)}, u32[]{:S(2)}, u32[]{:S(2)}) collective-permute-start(bf16[192,1152]{1,0:T(8,128)(2,1)S(1)} %collective-permute-done.47), channel_id=1, source_target_pairs={{4,0},{12,4},{20,12},{28,20},{24,28},{16,24},{8,16},{0,8},{5,1},{1... | collective-permute-start | bytes 1327112 | tf_op jit(solution)/shard_map/ppermute | solution.py:120
  271.3 32.8 %collective-permute-start.52 = (bf16[192,1152]{1,0:T(8,128)(2,1)S(1)}, bf16[192,1152]{1,0:T(8,128)(2,1)S(1)}, u32[]{:S(2)}, u32[]{:S(2)}) collective-permute-start(bf16[192,1152]{1,0:T(8,128)(2,1)S(1)} %collective-permute-done.48), channel_id=1, source_target_pairs={{0,4},{4,12},{12,20},{20,28},{28,24},{24,16},{16,8},{8,0},{1,5},{5... | collective-permute-start | bytes 1327112 | tf_op jit(solution)/shard_map/ppermute | solution.py:122
  273.3 30.7 %collective-permute-start.54 = (bf16[64,1536]{1,0:T(8,128)(2,1)S(1)}, bf16[64,1536]{1,0:T(8,128)(2,1)S(1)}, u32[]{:S(2)}, u32[]{:S(2)}) collective-permute-start(bf16[64,1536]{1,0:T(8,128)(2,1)S(1)} %collective-permute-done.50), channel_id=1, source_target_pairs={{4,0},{12,4},{20,12},{28,20},{24,28},{16,24},{8,16},{0,8},{5,1},{1... | collective-permute-start | bytes 589832 | tf_op jit(solution)/shard_map/ppermute | solution.py:122
  316.1 29.8 %collective-permute-start.58 = (bf16[192,1152]{1,0:T(8,128)(2,1)S(1)}, bf16[192,1152]{1,0:T(8,128)(2,1)S(1)}, u32[]{:S(2)}, u32[]{:S(2)}) collective-permute-start(bf16[192,1152]{1,0:T(8,128)(2,1)S(1)} %collective-permute-done.51), channel_id=1, source_target_pairs={{4,0},{12,4},{20,12},{28,20},{24,28},{16,24},{8,16},{0,8},{5,1},{1... | collective-permute-start | bytes 1327112 | tf_op jit(solution)/shard_map/ppermute | solution.py:120
  430.2 284.1 %reduce-scatter.5.cloned.1.call-start = ((), (), s32[]{:S(2)}) async-start(), calls=%async_computation.8 | async-start | bytes 3981312 | tf_op jit(solution)/shard_map/reduce_scatter | solution.py:786
  430.2 34.7 %collective-permute-start.75 = (bf16[256,1536]{1,0:T(8,128)(2,1)}, bf16[256,1536]{1,0:T(8,128)(2,1)}, u32[]{:S(2)}, u32[]{:S(2)}) collective-permute-start(bf16[256,1536]{1,0:T(8,128)(2,1)} %bitcast.649), channel_id=1, source_target_pairs={{0,2},{1,3},{2,0},{3,1},{4,6},{5,7},{6,4},{7,5},{8,10},{9,11},{10,... | collective-permute-start | bytes 2359304 | tf_op jit(solution)/shard_map/ppermute | solution.py:68
  453.6 28.2 %collective-permute-start.78 = (bf16[256,1536]{1,0:T(8,128)(2,1)S(1)}, bf16[256,1536]{1,0:T(8,128)(2,1)S(1)}, u32[]{:S(2)}, u32[]{:S(2)}) collective-permute-start(bf16[256,1536]{1,0:T(8,128)(2,1)S(1)} %multiply_convert_fusion.4), channel_id=1, source_target_pairs={{0,2},{1,3},{2,0},{3,1},{4,6},{5,7},{6,4},{7,5},{8,10},{9,11},{10,... | collective-permute-start | bytes 2359304 | tf_op jit(solution)/shard_map/ppermute | solution.py:68
  454.8 28.1 %collective-permute-start.74 = (bf16[256,1536]{1,0:T(8,128)(2,1)S(1)}, bf16[256,1536]{1,0:T(8,128)(2,1)S(1)}, u32[]{:S(2)}, u32[]{:S(2)}) collective-permute-start(bf16[256,1536]{1,0:T(8,128)(2,1)S(1)} %bitcast.650), channel_id=1, source_target_pairs={{0,1},{1,0},{2,3},{3,2},{4,5},{5,4},{6,7},{7,6},{8,9},{9,8},{10,11... | collective-permute-start | bytes 2359304 | tf_op jit(solution)/shard_map/ppermute | solution.py:68
  527.0 222.5 %reduce-scatter.7.cloned.1.call-start = ((), (), s32[]{:S(2)}) async-start(), calls=%async_computation.9 | async-start | bytes 7962624 | tf_op jit(solution)/shard_map/reduce_scatter | solution.py:783
  584.5 364.5 %reduce-scatter.9.cloned.1.call-start = ((), (), s32[]{:S(2)}) async-start(), calls=%async_computation.10 | async-start | bytes 7962624 | tf_op jit(solution)/shard_map/reduce_scatter | solution.py:783
  745.1 280.9 %reduce-scatter.11.cloned.1.call-start = ((), (), s32[]{:S(2)}) async-start(), calls=%async_computation.11 | async-start | bytes 3981312 | tf_op jit(solution)/shard_map/reduce_scatter | solution.py:786
  804.5 155.5 %collective-permute-start.86 = (bf16[256,1536]{1,0:T(8,128)(2,1)}, bf16[256,1536]{1,0:T(8,128)(2,1)}, u32[]{:S(2)}, u32[]{:S(2)}) collective-permute-start(bf16[256,1536]{1,0:T(8,128)(2,1)} %get-tuple-element.472), channel_id=1, source_target_pairs={{0,1},{1,0},{2,3},{3,2},{4,5},{5,4},{6,7},{7,6},{8,9},{9,8},{10,11... | collective-permute-start | bytes 2359304 | tf_op jit(solution)/shard_map/ppermute | solution.py:68
  825.9 27.6 %collective-permute-start.114 = (bf16[192,1152]{1,0:T(8,128)(2,1)}, bf16[192,1152]{1,0:T(8,128)(2,1)S(1)}, u32[]{:S(2)}, u32[]{:S(2)}) collective-permute-start(bf16[192,1152]{1,0:T(8,128)(2,1)} %get-tuple-element.463), channel_id=1, source_target_pairs={{0,4},{4,12},{12,20},{20,28},{28,24},{24,16},{16,8},{8,0},{1,5},{5... | collective-permute-start | bytes 1327112 | tf_op jit(solution)/shard_map/ppermute | solution.py:155
  904.3 51.5 %collective-permute-start.122 = (bf16[192,1152]{1,0:T(8,128)(2,1)}, bf16[192,1152]{1,0:T(8,128)(2,1)}, u32[]{:S(2)}, u32[]{:S(2)}) collective-permute-start(bf16[192,1152]{1,0:T(8,128)(2,1)} %get-tuple-element.346), channel_id=1, source_target_pairs={{0,4},{4,12},{12,20},{20,28},{28,24},{24,16},{16,8},{8,0},{1,5},{5... | collective-permute-start | bytes 1327112 | tf_op jit(solution)/shard_map/ppermute | solution.py:155
  904.4 51.5 %collective-permute-start.123 = (bf16[192,1152]{1,0:T(8,128)(2,1)}, bf16[192,1152]{1,0:T(8,128)(2,1)}, u32[]{:S(2)}, u32[]{:S(2)}) collective-permute-start(bf16[192,1152]{1,0:T(8,128)(2,1)} %get-tuple-element.347), channel_id=1, source_target_pairs={{4,0},{12,4},{20,12},{28,20},{24,28},{16,24},{8,16},{0,8},{5,1},{1... | collective-permute-start | bytes 1327112 | tf_op jit(solution)/shard_map/ppermute | solution.py:157
  905.8 30.7 %collective-permute-start.121 = (bf16[64,1536]{1,0:T(8,128)(2,1)}, bf16[64,1536]{1,0:T(8,128)(2,1)}, u32[]{:S(2)}, u32[]{:S(2)}) collective-permute-start(bf16[64,1536]{1,0:T(8,128)(2,1)} %fusion.78), channel_id=1, source_target_pairs={{4,0},{12,4},{20,12},{28,20},{24,28},{16,24},{8,16},{0,8},{5,1},{1... | collective-permute-start | bytes 589832 | tf_op jit(solution)/shard_map/ppermute | solution.py:155
  908.2 38.4 %collective-permute-start.124 = (bf16[64,1536]{1,0:T(8,128)(2,1)}, bf16[64,1536]{1,0:T(8,128)(2,1)}, u32[]{:S(2)}, u32[]{:S(2)}) collective-permute-start(bf16[64,1536]{1,0:T(8,128)(2,1)} %get-tuple-element.348), channel_id=1, source_target_pairs={{4,0},{12,4},{20,12},{28,20},{24,28},{16,24},{8,16},{0,8},{5,1},{1... | collective-permute-start | bytes 589832 | tf_op jit(solution)/shard_map/ppermute | solution.py:155
  971.3 30.2 %collective-permute-start.132 = (bf16[192,1152]{1,0:T(8,128)(2,1)S(1)}, bf16[192,1152]{1,0:T(8,128)(2,1)S(1)}, u32[]{:S(2)}, u32[]{:S(2)}) collective-permute-start(bf16[192,1152]{1,0:T(8,128)(2,1)S(1)} %copy-done.102), channel_id=1, source_target_pairs={{0,4},{4,12},{12,20},{20,28},{28,24},{24,16},{16,8},{8,0},{1,5},{5... | collective-permute-start | bytes 1327112 | tf_op jit(solution)/shard_map/ppermute | solution.py:155
  986.4 93.8 %collective-permute-start.154 = (f32[64,1536]{1,0:T(8,128)}, f32[64,1536]{1,0:T(8,128)}, u32[]{:S(2)}, u32[]{:S(2)}) collective-permute-start(f32[64,1536]{1,0:T(8,128)} %fusion.71), channel_id=1, source_target_pairs={{0,0},{4,1},{1,2},{5,3},{2,4},{6,5},{3,6},{7,7},{8,8},{12,9},{9,10... | collective-permute-start | bytes 1179656 | tf_op jit(solution)/shard_map/ppermute | solution.py:282
  1005.7 28.4 %collective-permute-start.141 = (bf16[192,1152]{1,0:T(8,128)(2,1)}, bf16[192,1152]{1,0:T(8,128)(2,1)}, u32[]{:S(2)}, u32[]{:S(2)}) collective-permute-start(bf16[192,1152]{1,0:T(8,128)(2,1)} %get-tuple-element.457), channel_id=1, source_target_pairs={{0,4},{4,12},{12,20},{20,28},{28,24},{24,16},{16,8},{8,0},{1,5},{5... | collective-permute-start | bytes 1327112 | tf_op jit(solution)/shard_map/ppermute | solution.py:155
  (304 other events, 3910.7 us)
Sparse Core Ops, SparseCore 0:
  95.9 117.9 all-gather.4
  216.0 82.6 all-gather.6
  300.9 122.9 all-gather.8
  430.3 63.5 all-gather.10
  527.1 79.4 reduce-scatter.4
  610.2 134.0 reduce-scatter.6
  748.4 144.9 reduce-scatter.8
  897.0 107.6 reduce-scatter.10

commit v6 on v3

--- a/solution.py
+++ b/solution.py
@@ -797,7 +797,7 @@
     grad_out = dot_tokens(kept["merged"], g_branch)
     dh, d_branch, ends = states_back(streams, d_merged, kept["branch"], kept["a"], kept["h"])
     if end is not None:
-        ends = end(ends)
+        ends = end[0](ends)
     ends = pump.hold(ends)
     back = carry_in(kept["whole"], ends, -1)
     back = pump.step(back)
@@ -805,6 +805,8 @@
         streams, dh, kept["a"], kept["h"], kept["start"], back, kept["conv"], kept["stream"], kept["halo"], keep,
         wts.taps, wts.decay, wts.slope, wts.gates,
     )
+    if end is not None:
+        d_stream = end[1](d_stream)
     tail = (tail + shift_seq(head, -1)).astype(bf16)
     tokens = d_stream.shape[0] // streams
     d_stream = lax.dynamic_update_slice(
@@ -923,6 +925,10 @@
         outcome.append(block_end(kept[-1], weights[-1]))
         return ends
 
+    def settle(d_stream):
+        d_stream, outcome[0] = tie(d_stream, outcome[0])
+        return d_stream
+
     for layer in reversed(range(layers)):
         if layer != layers - 1:
             g_down = tp_gather(gx.astype(bf16))
@@ -931,7 +937,7 @@
             gx, g_down, weights[layer], kept[layer], results[layer], rp, pump, results[layer + 1] if layer < layers - 1 else None
         )
         gx, d_mix, both = mixer_back(
-            d_x1, keep, streams, weights[layer], kept[layer], d_mlp, d_mix, sizes, results[layer], pump, last if layer == layers - 1 else None
+            d_x1, keep, streams, weights[layer], kept[layer], d_mlp, d_mix, sizes, results[layer], pump, (last, settle) if layer == layers - 1 else None
         )
         jobs.append(both)
     pump.complete(jobs[:-1])

time: 1110 us -> 1150 us (1.036)
  waiting for transfers between devices: 429 us -> 472 us
    reduce_scatter x2, waiting for transfers between devices: 0.01 us -> 40.5 us  [mlp_back(): lax.psum_scatter(grad_down.reshape(n, -1, width), 'seq', scatter_dimensio...]
    ppermute x77, waiting for transfers between devices: 265 us -> 253 us  [swap(): return lax.ppermute(x, 'wt', [(i, i ^ k) for i in range(TP)])]
    ppermute x32, waiting for transfers between devices: 104 us -> 115 us  [start(): flight = [lax.ppermute(self.a, 'seq', self.routes[0])]]
  transfers between devices with their start and end apart: 169 -> 169, of which waited for: 60 -> 58; matrix products, arithmetic and copies ran while one was open for 30% -> 30% of each run, Pallas kernels for 6% -> 6%
where the time goes in v6:
time: 1150 us; the launch traced here: 1140 us
  waiting for transfers between devices  472 us (41%)
  starting transfers between devices  199 us (17%)
  matrix products  181 us (16%)
  other arithmetic  117 us (10%)
  local copies, waits for them, and re-layouts  90.2 us (8%)
  Pallas kernels  65.6 us (6%)
  between operations  18.1 us (2%)
    ppermute x77, waiting for transfers between devices, swap(): return lax.ppermute(x, 'wt', [(i, i ^ k) for i in range(TP)])  253 us
    ppermute x32, waiting for transfers between devices, start(): flight = [lax.ppermute(self.a, 'seq', self.routes[0])]  115 us
    ppermute x77, starting transfers between devices, swap(): return lax.ppermute(x, 'wt', [(i, i ^ k) for i in range(TP)])  96.4 us
    dot_general x10, matrix products, dot_t(): lax.dot_general(left, right, (((1,), (1,)), ((), ())), preferred_element_...  74.8 us
    dot_general x10, matrix products, dot_tokens(): lax.dot_general(left, right, (((0,), (0,)), ((), ())), preferred_element_...  54.3 us
    dot_general x12, matrix products, dot(): lax.dot_general(left, right, (((1,), (0,)), ((), ())), preferred_element_...  52 us
    ppermute x21, starting transfers between devices, shift_seq(): lax.ppermute(x, 'seq', [(i, i + distance) for i in range(n) if 0 <= i + d...  47.8 us
    reduce_scatter x2, waiting for transfers between devices, mlp_back(): lax.psum_scatter(grad_down.reshape(n, -1, width), 'seq', scatter_dimensio...  40.5 us
  transfers between devices with their start and end apart: 169, of which 58 were waited for; matrix products, arithmetic and copies ran while one was open for 30% of the time, Pallas kernels for 6%

profile of v6, /device:TPU:3, one launch (start us, length us, event | category | flops | bytes accessed | tf_op | source)
XLA Modules:
  0.0 1142.7 jit_solution(13662611425312844244)
XLA Ops:
  46.3 8.9 collective-permute-done.20
  65.1 11.4 %collective-permute-done.17 = bf16[64,1536]{1,0:T(8,128)(2,1)S(1)} collective-permute-done((bf16[64,1536]{1,0:T(8,128)(2,1)S(1)}, bf16[64,1536]{1,0:T(8,128)(2,1)S(1)}, u32[]{:S(2)}, u32[]{:S(2)}) %collective-permute-start.17) | collective-permute-done | bytes 196640 | tf_op jit(solution)/shard_map/ppermute | solution.py:120
  157.7 8.8 shard_map.238
  206.7 18.5 %collective-permute-done.39 = bf16[256,1536]{1,0:T(8,128)(2,1)} collective-permute-done((bf16[256,1536]{1,0:T(8,128)(2,1)}, bf16[256,1536]{1,0:T(8,128)(2,1)}, u32[]{:S(2)}, u32[]{:S(2)}) %collective-permute-start.39) | collective-permute-done | bytes 786464 | tf_op jit(solution)/shard_map/ppermute | solution.py:68
  237.5 12.9 %collective-permute-done.45 = bf16[256,1536]{1,0:T(8,128)(2,1)S(1)} collective-permute-done((bf16[256,1536]{1,0:T(8,128)(2,1)S(1)}, bf16[256,1536]{1,0:T(8,128)(2,1)S(1)}, u32[]{:S(2)}, u32[]{:S(2)}) %collective-permute-start.45) | collective-permute-done | bytes 786464 | tf_op jit(solution)/shard_map/ppermute | solution.py:68
  254.3 16.0 %collective-permute-done.50 = bf16[64,1536]{1,0:T(8,128)(2,1)S(1)} collective-permute-done((bf16[64,1536]{1,0:T(8,128)(2,1)S(1)}, bf16[64,1536]{1,0:T(8,128)(2,1)S(1)}, u32[]{:S(2)}, u32[]{:S(2)}) %collective-permute-start.50) | collective-permute-done | bytes 196640 | tf_op jit(solution)/shard_map/ppermute | solution.py:122
  281.2 13.1 %collective-permute-done.53 = bf16[64,1536]{1,0:T(8,128)(2,1)} collective-permute-done((bf16[64,1536]{1,0:T(8,128)(2,1)S(1)}, bf16[64,1536]{1,0:T(8,128)(2,1)}, u32[]{:S(2)}, u32[]{:S(2)}) %collective-permute-start.53) | collective-permute-done | bytes 196640 | tf_op jit(solution)/shard_map/ppermute | solution.py:120
  318.3 15.7 %collective-permute-done.57 = bf16[256,1536]{1,0:T(8,128)(2,1)S(1)} collective-permute-done((bf16[256,1536]{1,0:T(8,128)(2,1)S(1)}, bf16[256,1536]{1,0:T(8,128)(2,1)S(1)}, u32[]{:S(2)}, u32[]{:S(2)}) %collective-permute-start.57) | collective-permute-done | bytes 786464 | tf_op jit(solution)/shard_map/ppermute | solution.py:68
  334.3 11.5 %collective-permute-done.58 = bf16[192,1152]{1,0:T(8,128)(2,1)S(1)} collective-permute-done((bf16[192,1152]{1,0:T(8,128)(2,1)S(1)}, bf16[192,1152]{1,0:T(8,128)(2,1)S(1)}, u32[]{:S(2)}, u32[]{:S(2)}) %collective-permute-start.58) | collective-permute-done | bytes 442400 | tf_op jit(solution)/shard_map/ppermute | solution.py:120
  354.2 13.7 %collective-permute-done.61 = bf16[256,1536]{1,0:T(8,128)(2,1)} collective-permute-done((bf16[256,1536]{1,0:T(8,128)(2,1)}, bf16[256,1536]{1,0:T(8,128)(2,1)}, u32[]{:S(2)}, u32[]{:S(2)}) %collective-permute-start.61) | collective-permute-done | bytes 786464 | tf_op jit(solution)/shard_map/ppermute | solution.py:68
  386.5 8.8 shard_map.240
  428.5 17.4 %collective-permute-done.70 = bf16[256,1536]{1,0:T(8,128)(2,1)} collective-permute-done((bf16[256,1536]{1,0:T(8,128)(2,1)}, bf16[256,1536]{1,0:T(8,128)(2,1)}, u32[]{:S(2)}, u32[]{:S(2)}) %collective-permute-start.70) | collective-permute-done | bytes 786464 | tf_op jit(solution)/shard_map/ppermute | solution.py:68
  464.8 14.8 %collective-permute-done.78 = bf16[256,1536]{1,0:T(8,128)(2,1)S(1)} collective-permute-done((bf16[256,1536]{1,0:T(8,128)(2,1)S(1)}, bf16[256,1536]{1,0:T(8,128)(2,1)S(1)}, u32[]{:S(2)}, u32[]{:S(2)}) %collective-permute-start.78) | collective-permute-done | bytes 786464 | tf_op jit(solution)/shard_map/ppermute | solution.py:68
  500.5 11.1 multiply_convert_fusion.3
  514.8 9.8 convolution_convert_fusion.1
  524.7 11.6 %convolution_convert_fusion.5 = bf16[1024,1536]{1,0:T(8,128)(2,1)S(1)} fusion(bf16[1024,2304]{1,0:T(8,128)(2,1)} %pad_maximum_fusion, bf16[1536,2304]{1,0:T(8,128)(2,1)} %all-gather.9.cloned.1.call-done), kind=kOutput, calls=%fused_computation.34 | convolution fusion | flops 7249330176 | bytes 14942208 | tf_op jit(solution)/shard_map/dot_general | solution.py:27
  540.3 17.6 %collective-permute-done.82 = bf16[256,1536]{1,0:T(8,128)(2,1)S(1)} collective-permute-done((bf16[256,1536]{1,0:T(8,128)(2,1)S(1)}, bf16[256,1536]{1,0:T(8,128)(2,1)S(1)}, u32[]{:S(2)}, u32[]{:S(2)}) %collective-permute-start.82) | collective-permute-done | bytes 786464 | tf_op jit(solution)/shard_map/ppermute | solution.py:68
  563.4 15.6 %collective-permute-done.84 = bf16[256,1536]{1,0:T(8,128)(2,1)} collective-permute-done((bf16[256,1536]{1,0:T(8,128)(2,1)}, bf16[256,1536]{1,0:T(8,128)(2,1)}, u32[]{:S(2)}, u32[]{:S(2)}) %collective-permute-start.84) | collective-permute-done | bytes 786464 | tf_op jit(solution)/shard_map/ppermute | solution.py:68
  631.0 15.4 %shard_map.244 = (bf16[1024,512]{1,0:T(8,128)(2,1)S(1)}, f32[24,512]{1,0:T(8,128)S(1)}, f32[24,512]{1,0:T(8,128)}, f32[4,128,256]{2,1,0:T(8,128)S(1)}, f32[4,512]{1,0:T(4,128)S(1)}, /*index=5*/f32[1,512]{1,0:T(1,128)S(1)}) custom-call(f32[1024,512]{1,0:T(8,128)S(1)} %get-tuple-element.294.dh_ref, f32[1024,512]{1,0:T(8,128)S(1)} %get-tuple-element.278.a_ref, ...), custom_call_target="tpu_custom_call" | custom-call | flops 629145600 | bytes 11534336 | tf_op jit(solution)/shard_map/pallas_call | solution.py:562
  658.3 15.4 %collective-permute-done.92 = bf16[256,1536]{1,0:T(8,128)(2,1)S(1)} collective-permute-done((bf16[256,1536]{1,0:T(8,128)(2,1)S(1)}, bf16[256,1536]{1,0:T(8,128)(2,1)S(1)}, u32[]{:S(2)}, u32[]{:S(2)}) %collective-permute-start.92) | collective-permute-done | bytes 786464 | tf_op jit(solution)/shard_map/ppermute | solution.py:68
  695.5 17.7 %collective-permute-done.96 = bf16[256,1536]{1,0:T(8,128)(2,1)S(1)} collective-permute-done((bf16[256,1536]{1,0:T(8,128)(2,1)S(1)}, bf16[256,1536]{1,0:T(8,128)(2,1)S(1)}, u32[]{:S(2)}, u32[]{:S(2)}) %collective-permute-start.96) | collective-permute-done | bytes 786464 | tf_op jit(solution)/shard_map/ppermute | solution.py:68
  717.2 15.5 %collective-permute-done.98 = bf16[256,1536]{1,0:T(8,128)(2,1)} collective-permute-done((bf16[256,1536]{1,0:T(8,128)(2,1)S(1)}, bf16[256,1536]{1,0:T(8,128)(2,1)}, u32[]{:S(2)}, u32[]{:S(2)}) %collective-permute-start.98) | collective-permute-done | bytes 786464 | tf_op jit(solution)/shard_map/ppermute | solution.py:68
  754.4 10.3 convolution_convert_fusion
  768.2 11.3 convolution_convert_fusion.4
  779.5 19.7 %collective-permute-done.102 = bf16[64,1536]{1,0:T(8,128)(2,1)} collective-permute-done((bf16[64,1536]{1,0:T(8,128)(2,1)}, bf16[64,1536]{1,0:T(8,128)(2,1)}, u32[]{:S(2)}, u32[]{:S(2)}) %collective-permute-start.102) | collective-permute-done | bytes 196640 | tf_op jit(solution)/shard_map/ppermute | solution.py:155
  807.3 17.7 %collective-permute-done.106 = bf16[256,1536]{1,0:T(8,128)(2,1)S(1)} collective-permute-done((bf16[256,1536]{1,0:T(8,128)(2,1)S(1)}, bf16[256,1536]{1,0:T(8,128)(2,1)S(1)}, u32[]{:S(2)}, u32[]{:S(2)}) %collective-permute-start.106) | collective-permute-done | bytes 786464 | tf_op jit(solution)/shard_map/ppermute | solution.py:68
  830.5 15.3 %collective-permute-done.108 = bf16[256,1536]{1,0:T(8,128)(2,1)} collective-permute-done((bf16[256,1536]{1,0:T(8,128)(2,1)}, bf16[256,1536]{1,0:T(8,128)(2,1)}, u32[]{:S(2)}, u32[]{:S(2)}) %collective-permute-start.108) | collective-permute-done | bytes 786464 | tf_op jit(solution)/shard_map/ppermute | solution.py:68
  907.4 14.7 %shard_map.246 = (bf16[1024,512]{1,0:T(8,128)(2,1)S(1)}, f32[24,512]{1,0:T(8,128)S(1)}, f32[24,512]{1,0:T(8,128)S(1)}, f32[4,128,256]{2,1,0:T(8,128)S(1)}, f32[4,512]{1,0:T(4,128)S(1)}, /*index=5*/f32[1,512]{1,0:T(1,128)S(1)}) custom-call(f32[1024,512]{1,0:T(8,128)S(1)} %get-tuple-element.326.dh_ref, f32[1024,512]{1,0:T(8,128)S(1)} %copy-done.1, ...), custom_call_target="tpu_custom_call" | custom-call | flops 629145600 | bytes 11534336 | tf_op jit(solution)/shard_map/pallas_call | solution.py:562
  947.1 10.0 collective-permute-done.121
  974.9 40.5 %reduce-scatter.11.cloned.1.call-done = bf16[1,144,1536]{2,1,0:T(8,128)(2,1)} async-done(((bf16[8,144,1536]{2,1,0:T(8,128)(2,1)}), bf16[1,144,1536]{2,1,0:T(8,128)(2,1)}) %reduce-scatter.11.cloned.1.call-update) | async-done | bytes 442384 | tf_op jit(solution)/shard_map/reduce_scatter | solution.py:786
  1022.8 11.2 collective-permute-done.130
  1070.7 13.6 %collective-permute-done.143 = bf16[64,1536]{1,0:T(8,128)(2,1)S(1)} collective-permute-done((bf16[64,1536]{1,0:T(8,128)(2,1)S(1)}, bf16[64,1536]{1,0:T(8,128)(2,1)S(1)}, u32[]{:S(2)}, u32[]{:S(2)}) %collective-permute-start.143) | collective-permute-done | bytes 196640 | tf_op jit(solution)/shard_map/ppermute | solution.py:155
  (1004 shorter events, 658.9 us)
Async XLA Ops:
  7.2 221.2 %all-gather.5.cloned.1.call-start = ((), (), s32[]{:S(2)}) async-start(), calls=%async_computation.4 | async-start | bytes 7962624 | tf_op jit(solution)/shard_map/all_gather | solution.py:700
  44.3 39.0 %collective-permute-start.19 = (bf16[256,1536]{1,0:T(8,128)(2,1)S(1)}, bf16[256,1536]{1,0:T(8,128)(2,1)S(1)}, u32[]{:S(2)}, u32[]{:S(2)}) collective-permute-start(bf16[256,1536]{1,0:T(8,128)(2,1)S(1)} %bitcast.626), channel_id=1, source_target_pairs={{0,1},{1,0},{2,3},{3,2},{4,5},{5,4},{6,7},{7,6},{8,9},{9,8},{10,11... | collective-permute-start | bytes 2359304 | tf_op jit(solution)/shard_map/ppermute | solution.py:68
  91.2 213.1 %all-gather.7.cloned.1.call-start = ((), (), s32[]{:S(2)}) async-start(), calls=%async_computation.5 | async-start | bytes 3981312 | tf_op jit(solution)/shard_map/all_gather | solution.py:697
  129.0 51.1 %collective-permute-start.33 = (bf16[48,1152]{1,0:T(8,128)(2,1)}, bf16[48,1152]{1,0:T(8,128)(2,1)}, u32[]{:S(2)}, u32[]{:S(2)}) collective-permute-start(bf16[48,1152]{1,0:T(8,128)(2,1)} %get-tuple-element.555), channel_id=1, source_target_pairs={{0,1},{1,0},{2,3},{3,2},{4,5},{5,4},{6,7},{7,6},{8,9},{9,8},{10,11... | collective-permute-start | bytes 331784 | tf_op jit(solution)/shard_map/ppermute | solution.py:68
  129.8 51.7 %collective-permute-start.34 = (bf16[48,1152]{1,0:T(8,128)(2,1)}, bf16[48,1152]{1,0:T(8,128)(2,1)}, u32[]{:S(2)}, u32[]{:S(2)}) collective-permute-start(bf16[48,1152]{1,0:T(8,128)(2,1)} %get-tuple-element.554), channel_id=1, source_target_pairs={{0,2},{1,3},{2,0},{3,1},{4,6},{5,7},{6,4},{7,5},{8,10},{9,11},{10,... | collective-permute-start | bytes 331784 | tf_op jit(solution)/shard_map/ppermute | solution.py:68
  130.3 51.1 %collective-permute-start.35 = (bf16[48,1152]{1,0:T(8,128)(2,1)}, bf16[48,1152]{1,0:T(8,128)(2,1)}, u32[]{:S(2)}, u32[]{:S(2)}) collective-permute-start(bf16[48,1152]{1,0:T(8,128)(2,1)} %get-tuple-element.553), channel_id=1, source_target_pairs={{0,3},{1,2},{2,1},{3,0},{4,7},{5,6},{6,5},{7,4},{8,11},{9,10},{10,... | collective-permute-start | bytes 331784 | tf_op jit(solution)/shard_map/ppermute | solution.py:68
  151.8 297.1 %all-gather.9.cloned.1.call-start = ((), (), s32[]{:S(2)}) async-start(), calls=%async_computation.6 | async-start | bytes 7962624 | tf_op jit(solution)/shard_map/all_gather | solution.py:700
  206.6 293.8 %all-gather.11.cloned.1.call-start = ((), (), s32[]{:S(2)}) async-start(), calls=%async_computation.7 | async-start | bytes 3981312 | tf_op jit(solution)/shard_map/all_gather | solution.py:697
  232.4 37.9 %collective-permute-start.47 = (bf16[192,1152]{1,0:T(8,128)(2,1)S(1)}, bf16[192,1152]{1,0:T(8,128)(2,1)S(1)}, u32[]{:S(2)}, u32[]{:S(2)}) collective-permute-start(bf16[192,1152]{1,0:T(8,128)(2,1)S(1)} %collective-permute-done.40), channel_id=1, source_target_pairs={{4,0},{12,4},{20,12},{28,20},{24,28},{16,24},{8,16},{0,8},{5,1},{1... | collective-permute-start | bytes 1327112 | tf_op jit(solution)/shard_map/ppermute | solution.py:120
  232.4 37.8 %collective-permute-start.48 = (bf16[192,1152]{1,0:T(8,128)(2,1)}, bf16[192,1152]{1,0:T(8,128)(2,1)S(1)}, u32[]{:S(2)}, u32[]{:S(2)}) collective-permute-start(bf16[192,1152]{1,0:T(8,128)(2,1)} %collective-permute-done.41), channel_id=1, source_target_pairs={{0,4},{4,12},{12,20},{20,28},{28,24},{24,16},{16,8},{8,0},{1,5},{5... | collective-permute-start | bytes 1327112 | tf_op jit(solution)/shard_map/ppermute | solution.py:122
  270.3 31.3 %collective-permute-start.51 = (bf16[192,1152]{1,0:T(8,128)(2,1)S(1)}, bf16[192,1152]{1,0:T(8,128)(2,1)S(1)}, u32[]{:S(2)}, u32[]{:S(2)}) collective-permute-start(bf16[192,1152]{1,0:T(8,128)(2,1)S(1)} %collective-permute-done.47), channel_id=1, source_target_pairs={{4,0},{12,4},{20,12},{28,20},{24,28},{16,24},{8,16},{0,8},{5,1},{1... | collective-permute-start | bytes 1327112 | tf_op jit(solution)/shard_map/ppermute | solution.py:120
  270.3 31.3 %collective-permute-start.52 = (bf16[192,1152]{1,0:T(8,128)(2,1)S(1)}, bf16[192,1152]{1,0:T(8,128)(2,1)S(1)}, u32[]{:S(2)}, u32[]{:S(2)}) collective-permute-start(bf16[192,1152]{1,0:T(8,128)(2,1)S(1)} %collective-permute-done.48), channel_id=1, source_target_pairs={{0,4},{4,12},{12,20},{20,28},{28,24},{24,16},{16,8},{8,0},{1,5},{5... | collective-permute-start | bytes 1327112 | tf_op jit(solution)/shard_map/ppermute | solution.py:122
  314.1 31.7 %collective-permute-start.58 = (bf16[192,1152]{1,0:T(8,128)(2,1)S(1)}, bf16[192,1152]{1,0:T(8,128)(2,1)S(1)}, u32[]{:S(2)}, u32[]{:S(2)}) collective-permute-start(bf16[192,1152]{1,0:T(8,128)(2,1)S(1)} %collective-permute-done.51), channel_id=1, source_target_pairs={{4,0},{12,4},{20,12},{28,20},{24,28},{16,24},{8,16},{0,8},{5,1},{1... | collective-permute-start | bytes 1327112 | tf_op jit(solution)/shard_map/ppermute | solution.py:120
  428.1 306.6 %reduce-scatter.5.cloned.1.call-start = ((), (), s32[]{:S(2)}) async-start(), calls=%async_computation.8 | async-start | bytes 3981312 | tf_op jit(solution)/shard_map/reduce_scatter | solution.py:786
  428.2 34.6 %collective-permute-start.75 = (bf16[256,1536]{1,0:T(8,128)(2,1)}, bf16[256,1536]{1,0:T(8,128)(2,1)}, u32[]{:S(2)}, u32[]{:S(2)}) collective-permute-start(bf16[256,1536]{1,0:T(8,128)(2,1)} %bitcast.647), channel_id=1, source_target_pairs={{0,2},{1,3},{2,0},{3,1},{4,6},{5,7},{6,4},{7,5},{8,10},{9,11},{10,... | collective-permute-start | bytes 2359304 | tf_op jit(solution)/shard_map/ppermute | solution.py:68
  524.7 243.5 %reduce-scatter.7.cloned.1.call-start = ((), (), s32[]{:S(2)}) async-start(), calls=%async_computation.9 | async-start | bytes 7962624 | tf_op jit(solution)/shard_map/reduce_scatter | solution.py:783
  582.4 362.1 %reduce-scatter.9.cloned.1.call-start = ((), (), s32[]{:S(2)}) async-start(), calls=%async_computation.10 | async-start | bytes 7962624 | tf_op jit(solution)/shard_map/reduce_scatter | solution.py:783
  618.1 35.5 %collective-permute-start.91 = (bf16[256,1536]{1,0:T(8,128)(2,1)}, bf16[256,1536]{1,0:T(8,128)(2,1)}, u32[]{:S(2)}, u32[]{:S(2)}) collective-permute-start(bf16[256,1536]{1,0:T(8,128)(2,1)} %get-tuple-element.473), channel_id=1, source_target_pairs={{0,1},{1,0},{2,3},{3,2},{4,5},{5,4},{6,7},{7,6},{8,9},{9,8},{10,11... | collective-permute-start | bytes 2359304 | tf_op jit(solution)/shard_map/ppermute | solution.py:68
  622.4 35.8 %collective-permute-start.90 = (bf16[256,1536]{1,0:T(8,128)(2,1)}, bf16[256,1536]{1,0:T(8,128)(2,1)}, u32[]{:S(2)}, u32[]{:S(2)}) collective-permute-start(bf16[256,1536]{1,0:T(8,128)(2,1)} %get-tuple-element.472), channel_id=1, source_target_pairs={{0,1},{1,0},{2,3},{3,2},{4,5},{5,4},{6,7},{7,6},{8,9},{9,8},{10,11... | collective-permute-start | bytes 2359304 | tf_op jit(solution)/shard_map/ppermute | solution.py:68
  764.8 250.7 %reduce-scatter.11.cloned.1.call-start = ((), (), s32[]{:S(2)}) async-start(), calls=%async_computation.11 | async-start | bytes 3981312 | tf_op jit(solution)/shard_map/reduce_scatter | solution.py:786
  764.8 34.4 %collective-permute-start.100 = (bf16[192,1152]{1,0:T(8,128)(2,1)}, bf16[192,1152]{1,0:T(8,128)(2,1)S(1)}, u32[]{:S(2)}, u32[]{:S(2)}) collective-permute-start(bf16[192,1152]{1,0:T(8,128)(2,1)} %get-tuple-element.317), channel_id=1, source_target_pairs={{0,4},{4,12},{12,20},{20,28},{28,24},{24,16},{16,8},{8,0},{1,5},{5... | collective-permute-start | bytes 1327112 | tf_op jit(solution)/shard_map/ppermute | solution.py:155
  765.7 33.4 %collective-permute-start.101 = (bf16[192,1152]{1,0:T(8,128)(2,1)S(1)}, bf16[192,1152]{1,0:T(8,128)(2,1)S(1)}, u32[]{:S(2)}, u32[]{:S(2)}) collective-permute-start(bf16[192,1152]{1,0:T(8,128)(2,1)S(1)} %copy-done.98), channel_id=1, source_target_pairs={{4,0},{12,4},{20,12},{28,20},{24,28},{16,24},{8,16},{0,8},{5,1},{1... | collective-permute-start | bytes 1327112 | tf_op jit(solution)/shard_map/ppermute | solution.py:157
  766.3 32.8 %collective-permute-start.102 = (bf16[64,1536]{1,0:T(8,128)(2,1)}, bf16[64,1536]{1,0:T(8,128)(2,1)}, u32[]{:S(2)}, u32[]{:S(2)}) collective-permute-start(bf16[64,1536]{1,0:T(8,128)(2,1)} %get-tuple-element.319), channel_id=1, source_target_pairs={{4,0},{12,4},{20,12},{28,20},{24,28},{16,24},{8,16},{0,8},{5,1},{1... | collective-permute-start | bytes 589832 | tf_op jit(solution)/shard_map/ppermute | solution.py:155
  924.6 37.3 %collective-permute-start.119 = (bf16[192,1152]{1,0:T(8,128)(2,1)}, bf16[192,1152]{1,0:T(8,128)(2,1)}, u32[]{:S(2)}, u32[]{:S(2)}) collective-permute-start(bf16[192,1152]{1,0:T(8,128)(2,1)} %get-tuple-element.344), channel_id=1, source_target_pairs={{0,4},{4,12},{12,20},{20,28},{28,24},{24,16},{16,8},{8,0},{1,5},{5... | collective-permute-start | bytes 1327112 | tf_op jit(solution)/shard_map/ppermute | solution.py:155
  924.6 37.2 %collective-permute-start.120 = (bf16[192,1152]{1,0:T(8,128)(2,1)}, bf16[192,1152]{1,0:T(8,128)(2,1)}, u32[]{:S(2)}, u32[]{:S(2)}) collective-permute-start(bf16[192,1152]{1,0:T(8,128)(2,1)} %get-tuple-element.345), channel_id=1, source_target_pairs={{4,0},{12,4},{20,12},{28,20},{24,28},{16,24},{8,16},{0,8},{5,1},{1... | collective-permute-start | bytes 1327112 | tf_op jit(solution)/shard_map/ppermute | solution.py:157
  926.1 31.1 %collective-permute-start.121 = (bf16[64,1536]{1,0:T(8,128)(2,1)}, bf16[64,1536]{1,0:T(8,128)(2,1)}, u32[]{:S(2)}, u32[]{:S(2)}) collective-permute-start(bf16[64,1536]{1,0:T(8,128)(2,1)} %get-tuple-element.346), channel_id=1, source_target_pairs={{4,0},{12,4},{20,12},{28,20},{24,28},{16,24},{8,16},{0,8},{5,1},{1... | collective-permute-start | bytes 589832 | tf_op jit(solution)/shard_map/ppermute | solution.py:155
  963.6 55.5 %collective-permute-start.127 = (bf16[64,1536]{1,0:T(8,128)(2,1)}, bf16[64,1536]{1,0:T(8,128)(2,1)}, u32[]{:S(2)}, u32[]{:S(2)}) collective-permute-start(bf16[64,1536]{1,0:T(8,128)(2,1)} %fusion.78), channel_id=1, source_target_pairs={{4,0},{12,4},{20,12},{28,20},{24,28},{16,24},{8,16},{0,8},{5,1},{1... | collective-permute-start | bytes 589832 | tf_op jit(solution)/shard_map/ppermute | solution.py:155
  968.9 65.2 %collective-permute-start.126 = (bf16[192,1152]{1,0:T(8,128)(2,1)}, bf16[192,1152]{1,0:T(8,128)(2,1)}, u32[]{:S(2)}, u32[]{:S(2)}) collective-permute-start(bf16[192,1152]{1,0:T(8,128)(2,1)} %fusion.63), channel_id=1, source_target_pairs={{0,4},{4,12},{12,20},{20,28},{28,24},{24,16},{16,8},{8,0},{1,5},{5... | collective-permute-start | bytes 1327112 | tf_op jit(solution)/shard_map/ppermute | solution.py:155
  968.9 50.6 %collective-permute-start.123 = (bf16[256,1536]{1,0:T(8,128)(2,1)S(1)}, bf16[256,1536]{1,0:T(8,128)(2,1)}, u32[]{:S(2)}, u32[]{:S(2)}) collective-permute-start(bf16[256,1536]{1,0:T(8,128)(2,1)S(1)} %get-tuple-element.466), channel_id=1, source_target_pairs={{0,1},{1,0},{2,3},{3,2},{4,5},{5,4},{6,7},{7,6},{8,9},{9,8},{10,11... | collective-permute-start | bytes 2359304 | tf_op jit(solution)/shard_map/ppermute | solution.py:68
  970.6 63.5 %collective-permute-start.128 = (bf16[192,1152]{1,0:T(8,128)(2,1)}, bf16[192,1152]{1,0:T(8,128)(2,1)}, u32[]{:S(2)}, u32[]{:S(2)}) collective-permute-start(bf16[192,1152]{1,0:T(8,128)(2,1)} %get-tuple-element.354), channel_id=1, source_target_pairs={{0,4},{4,12},{12,20},{20,28},{28,24},{24,16},{16,8},{8,0},{1,5},{5... | collective-permute-start | bytes 1327112 | tf_op jit(solution)/shard_map/ppermute | solution.py:155
  973.1 47.8 %collective-permute-start.125 = (bf16[256,1536]{1,0:T(8,128)(2,1)}, bf16[256,1536]{1,0:T(8,128)(2,1)}, u32[]{:S(2)}, u32[]{:S(2)}) collective-permute-start(bf16[256,1536]{1,0:T(8,128)(2,1)} %fusion.22), channel_id=1, source_target_pairs={{0,2},{1,3},{2,0},{3,1},{4,6},{5,7},{6,4},{7,5},{8,10},{9,11},{10,... | collective-permute-start | bytes 2359304 | tf_op jit(solution)/shard_map/ppermute | solution.py:68
  1058.7 74.8 %collective-permute-start.154 = (f32[64,1536]{1,0:T(8,128)}, f32[64,1536]{1,0:T(8,128)}, u32[]{:S(2)}, u32[]{:S(2)}) collective-permute-start(f32[64,1536]{1,0:T(8,128)} %fusion.71), channel_id=1, source_target_pairs={{0,0},{4,1},{1,2},{5,3},{2,4},{6,5},{3,6},{7,7},{8,8},{12,9},{9,10... | collective-permute-start | bytes 1179656 | tf_op jit(solution)/shard_map/ppermute | solution.py:282
  (295 other events, 3875.1 us)
Sparse Core Ops, SparseCore 0:
  91.3 119.0 all-gather.4
  212.6 84.0 all-gather.6
  298.9 122.8 all-gather.8
  428.3 62.1 all-gather.10
  524.8 79.0 reduce-scatter.4
  607.4 128.7 reduce-scatter.6
  764.9 147.9 reduce-scatter.8
  916.5 98.8 reduce-scatter.10
